TPU v7x, 32 devices: a whole 2x2x4 slice. The times are simulated.
32 devices in a mesh: lat: 8 (over z, core), row: 4 (over y, x).
Axes of the slice: x: 2, y: 2, z: 4, core: 2. Of those that a mesh axis runs over, the one named last changes fastest.
Arguments:
- inputs: bfloat16 [256, 3584], P('row', 'lat'), may hold values from -6 to 6
- encoder: bfloat16 [5376, 3584], P(('lat', 'row')), may hold values from -0.09375 to 0.09375
- latent_bias: float32 [5376], P(('lat', 'row')), may hold values from -3 to 3
- decoder: bfloat16 [5376, 3584], P(('lat', 'row')), may hold values from -0.49099025 to 0.49099025
- center_bias: float32 [3584], P('lat'), may hold values from -3 to 3
Outputs:
- encoder_grad: bfloat16 [5376, 3584], P(('lat', 'row'))
- decoder_grad: bfloat16 [5376, 3584], P(('lat', 'row'))
- bias_grad: float32 [5376], P(('lat', 'row'))
- center_grad: float32 [3584], P(('lat', 'row'))
All inputs are finite; a program needn't handle non-finite values.
Results may differ from a plain program's by a relative error of at most 0.005.
Values may be sent and summed in bfloat16 or wider, within the bound.
No kernel may reach another device: no remote copies, remote signals or barrier semaphores. Data moves between devices by JAX's collectives and lax.ppermute only.
A program may use at most 64 MiB of HBM per device.

v0:
```python
import jax
import jax.numpy as jnp
from jax import lax
from jax.sharding import PartitionSpec as P

sparsity_weight = 1.0


def on_device(inputs, encoder, latent_bias, decoder, center_bias):
    centered_part = (inputs.astype(jnp.float32) - center_bias).astype(jnp.bfloat16)
    rows_local, cols_local = centered_part.shape
    by_rows = lax.all_gather(centered_part, "row", axis=0, tiled=True)
    centered = lax.all_gather(by_rows, "lat", axis=1, tiled=True)
    preact = (
        lax.dot_general(
            centered, encoder, (((1,), (1,)), ((), ())), preferred_element_type=jnp.float32
        )
        + latent_bias
    )
    latents = (jax.nn.softplus(4.0 * preact) / 4.0).astype(jnp.bfloat16)
    partial_sum = jnp.dot(latents, decoder, preferred_element_type=jnp.float32)
    feature_part = lax.psum_scatter(
        partial_sum.astype(jnp.bfloat16), "lat", scatter_dimension=1, tiled=True
    )
    recon_part = lax.psum_scatter(feature_part, "row", scatter_dimension=0, tiled=True).astype(
        jnp.float32
    )
    error = recon_part + center_bias - inputs.astype(jnp.float32)
    error_half = error.astype(jnp.bfloat16)
    error_rows = lax.all_gather(error_half, "row", axis=0, tiled=True)
    width_full = decoder.shape[1]
    row_norm = jnp.sqrt(jnp.sum(jnp.square(decoder.astype(jnp.float32)), axis=1) + 1e-06)
    piece = lax.all_gather(error_rows, "lat", axis=1, tiled=True)
    grad_sum = lax.dot_general(
        piece, decoder, (((1,), (1,)), ((), ())), preferred_element_type=jnp.float32
    )
    block = lax.dot_general(
        latents, piece, (((0,), (0,)), ((), ())), preferred_element_type=jnp.float32
    )
    grad_sum, decoder_term = (grad_sum, block)
    grad_latent = grad_sum + sparsity_weight * row_norm
    grad_pre = (grad_latent * jax.nn.sigmoid(4.0 * preact)).astype(jnp.bfloat16)
    encoder_grad = lax.dot_general(
        grad_pre, centered, (((0,), (0,)), ((), ())), preferred_element_type=jnp.float32
    ).astype(jnp.bfloat16)
    latent_total = jnp.sum(latents.astype(jnp.float32), axis=0)
    decoder_grad = (
        decoder_term
        + sparsity_weight * latent_total[:, None] * decoder.astype(jnp.float32) / row_norm[:, None]
    ).astype(jnp.bfloat16)
    bias_grad = jnp.sum(grad_pre.astype(jnp.float32), axis=0)
    encoder_term = -jnp.dot(bias_grad, encoder.astype(jnp.float32), precision=lax.Precision.HIGHEST)
    column_sum = jnp.sum(error, axis=0)
    placed = lax.dynamic_update_slice_in_dim(
        jnp.zeros((width_full,), jnp.float32), column_sum, lax.axis_index("lat") * cols_local, 0
    )
    center_grad = lax.psum_scatter(
        encoder_term + placed, ("lat", "row"), scatter_dimension=0, tiled=True
    )
    return (encoder_grad, decoder_grad, bias_grad, center_grad)


def solution(mesh):
    in_specs = (
        P("row", "lat"),
        P(("lat", "row"), None),
        P(("lat", "row")),
        P(("lat", "row"), None),
        P("lat"),
    )
    out_specs = (
        P(("lat", "row"), None),
        P(("lat", "row"), None),
        P(("lat", "row")),
        P(("lat", "row")),
    )
    return jax.shard_map(
        on_device, mesh=mesh, in_specs=in_specs, out_specs=out_specs, check_vma=False
    )
```

profile of v0, /device:TPU:0, one launch (start us, length us, event | category | flops | bytes accessed | tf_op | source)
XLA Modules:
  0.0 205.3 jit_solution(4003787050387092567)
XLA Ops:
  7.2 0.9 fusion.8
  8.2 10.4 %all_gather.12 = bf16[256,448]{1,0:T(8,128)(2,1)S(1)} all-gather(bf16[64,448]{1,0:T(8,128)(2,1)S(1)} %fusion.8), channel_id=1, replica_groups=mesh['lat'=8,'row'=4] {'row'}, dimensions={0}, use_global_device_ids=true | all-gather | bytes 286720 | tf_op jit(solution)/shard_map/all_gather | solution.py:12
  18.6 0.8 copy.11
  19.5 0.0 reduce-scatter.5.cloned.1.call-start
  19.5 27.3 %all-gather.3.cloned.1.call-done = bf16[256,3584]{0,1:T(8,128)(2,1)} async-done(((bf16[256,448]{0,1:T(8,128)(2,1)}), bf16[256,3584]{0,1:T(8,128)(2,1)}) %all-gather.3.cloned.1.call-update) | async-done | bytes 1835024 | tf_op jit(solution)/shard_map/all_gather | solution.py:13
  46.9 2.2 %convert_reduce_fusion.1 = (f32[168]{0:T(256)S(1)}, bf16[256,168]{0,1:T(8,128)(2,1)S(1)}, f32[256,168]{0,1:T(8,128)S(1)}) fusion(f32[168]{0:T(256)} %param.7, bf16[256,3584]{0,1:T(8,128)(2,1)} %all-gather.3.cloned.1.call-done, bf16[168,3584]{1,0:T(8,128)(2,1)S(1)} %copy-done), kind=kOutput, calls=%fused_computation.18 | convolution fusion | flops 308797280 | bytes 3298624 | tf_op jit(solution)/shard_map/dot_general | solution.py:15
  49.0 2.1 %convolution_convert_fusion = bf16[256,3584]{0,1:T(8,128)(2,1)} fusion(bf16[256,168]{0,1:T(8,128)(2,1)S(1)} %get-tuple-element.5, bf16[168,3584]{1,0:T(8,128)(2,1)S(1)} %copy-done.1), kind=kOutput, calls=%fused_computation | convolution fusion | flops 309198848 | bytes 3125248 | tf_op jit(solution)/shard_map/dot_general | solution.py:21
  51.2 0.0 reduce-scatter.7.cloned.1.call-start
  51.2 34.7 %reduce-scatter.5.cloned.1.call-done = bf16[256,448]{0,1:T(8,128)(2,1)} async-done(((bf16[256,3584]{0,1:T(8,128)(2,1)}), bf16[256,448]{0,1:T(8,128)(2,1)}) %reduce-scatter.5.cloned.1.call-update) | async-done | bytes 229392 | tf_op jit(solution)/shard_map/reduce_scatter | solution.py:22
  86.0 1.8 copy.14
  87.8 0.0 all-gather.5.cloned.1.call-start
  87.8 23.9 %reduce-scatter.7.cloned.1.call-done = bf16[64,448]{1,0:T(8,128)(2,1)} async-done(((bf16[256,448]{1,0:T(8,128)(2,1)}), bf16[64,448]{1,0:T(8,128)(2,1)}) %reduce-scatter.7.cloned.1.call-update) | async-done | bytes 57360 | tf_op jit(solution)/shard_map/reduce_scatter | solution.py:25
  111.7 0.9 fusion.9
  112.6 9.3 %all_gather.14 = bf16[256,448]{1,0:T(8,128)(2,1)S(1)} all-gather(bf16[64,448]{1,0:T(8,128)(2,1)S(1)} %get-tuple-element.7), channel_id=1, replica_groups=mesh['lat'=8,'row'=4] {'row'}, dimensions={0}, use_global_device_ids=true | all-gather | bytes 286720 | tf_op jit(solution)/shard_map/all_gather | solution.py:30
  121.9 0.8 copy.13
  122.7 0.3 fusion.1
  123.1 26.7 %all-gather.5.cloned.1.call-done = bf16[256,3584]{0,1:T(8,128)(2,1)} async-done(((bf16[256,448]{0,1:T(8,128)(2,1)}), bf16[256,3584]{0,1:T(8,128)(2,1)}) %all-gather.5.cloned.1.call-update) | async-done | bytes 1835024 | tf_op jit(solution)/shard_map/all_gather | solution.py:33
  149.8 2.1 %convert_reduce_fusion = (f32[168]{0:T(256)S(1)}, bf16[256,168]{0,1:T(8,128)(2,1)S(1)}) fusion(f32[256,168]{0,1:T(8,128)S(1)} %get-tuple-element.8, f32[168]{0:T(256)S(1)} %add_sqrt_fusion, bf16[256,3584]{0,1:T(8,128)(2,1)} %all-gather.5.cloned.1.call-done, bf16[168,3584]{1,0:T(8,128)(2,1)S(1)} %copy-done.1), kind=kOutput, calls=%fused_computation.17 | convolution fusion | flops 308625248 | bytes 3298624 | tf_op jit(solution)/shard_map/dot_general | solution.py:34
  151.9 0.6 convolution_reduce_fusion
  152.5 0.2 add_dynamic-update-slice_fusion
  152.7 40.3 %all-reduce = f32[3584]{0:T(1024)S(1)} all-reduce(f32[3584]{0:T(1024)S(1)} %add_dynamic-update-slice_fusion), channel_id=4, replica_groups=mesh['lat'=8,'row'=4] {'lat','row'}, use_global_device_ids=true, to_apply=%region_6.7.clone | all-reduce | flops 3584 | bytes 28672
  193.0 0.6 dynamic-slice.1
  193.6 3.4 %fusion = bf16[168,3584]{1,0:T(8,128)(2,1)} fusion(bf16[256,168]{0,1:T(8,128)(2,1)S(1)} %get-tuple-element.5, bf16[256,3584]{0,1:T(8,128)(2,1)} %all-gather.5.cloned.1.call-done, bf16[168,3584]{1,0:T(8,128)(2,1)S(1)} %copy-done.1, f32[168]{0:T(256)S(1)} %add_sqrt_fusion, f32[168]{0:T(256)S(1)} %get-tuple-element.4), kind=kOutput, calls=%fused_computation.2 | convolution fusion | flops 311291904 | bytes 4330816 | tf_op jit(solution)/shard_map/dot_general | solution.py:37
  197.0 1.8 convolution_convert_fusion.1
  (19 shorter events, 0.1 us)
Async XLA Ops:
  7.2 39.7 %copy-start = (bf16[168,3584]{1,0:T(8,128)(2,1)S(1)}, bf16[168,3584]{1,0:T(8,128)(2,1)}, u32[]{:S(2)}) copy-start(bf16[168,3584]{1,0:T(8,128)(2,1)} %param.6) | copy-start | bytes 3612676
  7.2 39.7 %all-gather.3.cloned.1.call-start = ((), (), s32[]{:S(2)}) async-start(), calls=%async_computation.2 | async-start | bytes 2064384 | tf_op jit(solution)/shard_map/all_gather | solution.py:13
  19.5 29.6 %copy-start.1 = (bf16[168,3584]{1,0:T(8,128)(2,1)S(1)}, bf16[168,3584]{1,0:T(8,128)(2,1)}, u32[]{:S(2)}) copy-start(bf16[168,3584]{1,0:T(8,128)(2,1)} %param.8) | copy-start | bytes 3612676
  19.5 66.5 %reduce-scatter.5.cloned.1.call-start = ((), (), s32[]{:S(2)}) async-start(), calls=%async_computation.3 | async-start | bytes 2064384 | tf_op jit(solution)/shard_map/reduce_scatter | solution.py:22
  51.1 60.6 %copy-start.3 = (bf16[64,448]{1,0:T(8,128)(2,1)S(1)}, bf16[64,448]{1,0:T(8,128)(2,1)}, u32[]{:S(2)}) copy-start(bf16[64,448]{1,0:T(8,128)(2,1)} %param.5) | copy-start | bytes 172036
  51.1 60.6 %copy-start.4 = (f32[448]{0:T(512)S(1)}, f32[448]{0:T(512)}, u32[]{:S(2)}) copy-start(f32[448]{0:T(512)} %param.9) | copy-start | bytes 5380
  51.2 60.5 %reduce-scatter.7.cloned.1.call-start = ((), (), s32[]{:S(2)}) async-start(), calls=%async_computation.5 | async-start | bytes 327680 | tf_op jit(solution)/shard_map/reduce_scatter | solution.py:25
  87.8 62.0 %all-gather.5.cloned.1.call-start = ((), (), s32[]{:S(2)}) async-start(), calls=%async_computation.4 | async-start | bytes 2064384 | tf_op jit(solution)/shard_map/all_gather | solution.py:33
  151.9 45.1 %copy-start.5 = (f32[168]{0:T(256)}, f32[168]{0:T(256)S(1)}, u32[]{:S(2)}) copy-start(f32[168]{0:T(256)S(1)} %get-tuple-element.9) | copy-start | bytes 2020
  193.6 3.4 %copy-start.2 = (bf16[256,3584]{0,1:T(8,128)(2,1)S(1)}, bf16[256,3584]{0,1:T(8,128)(2,1)}, u32[]{:S(2)}) copy-start(bf16[256,3584]{0,1:T(8,128)(2,1)} %all-gather.3.cloned.1.call-done) | copy-start | bytes 5505028
Sparse Core Ops, SparseCore 0:
  19.6 27.2 all-gather.2
  51.3 34.6 reduce-scatter.4
  89.3 22.3 reduce-scatter.6
  122.9 26.8 all-gather.4
where the time goes:
time: 206 us; the launch traced here: 205 us
  waiting for transfers between devices  113 us (55%)
  blocking collectives  60 us (29%)
  between operations  13.8 us (7%)
  matrix products  12.2 us (6%)
  local copies, waits for them, and re-layouts  4.05 us (2%)
  other arithmetic  2.36 us (1%)
    unnamed x1, blocking collectives  40.3 us
    reduce_scatter x1, waiting for transfers between devices, on_device(): lax.psum_scatter(partial_sum.astype(jnp.bfloat16), 'lat', scatter_dimensi...  34.7 us
    all_gather x1, waiting for transfers between devices, on_device(): centered = lax.all_gather(by_rows, 'lat', axis=1, tiled=True)  27.3 us
    all_gather x1, waiting for transfers between devices, on_device(): piece = lax.all_gather(error_rows, 'lat', axis=1, tiled=True)  26.7 us
    reduce_scatter x1, waiting for transfers between devices, on_device(): lax.psum_scatter(feature_part, 'row', scatter_dimension=0, tiled=True)  23.9 us
    all_gather x1, blocking collectives, on_device(): by_rows = lax.all_gather(centered_part, 'row', axis=0, tiled=True)  10.4 us
    all_gather x1, blocking collectives, on_device(): error_rows = lax.all_gather(error_half, 'row', axis=0, tiled=True)  9.29 us
  transfers between devices with their start and end apart: 4, of which 4 were waited for; matrix products, arithmetic and copies ran while one was open for 0% of the time, Pallas kernels for 0%

commit v1 on v0

v1 whole, which is shorter than its diff:
```python
import jax
import jax.numpy as jnp
from jax import lax
from jax.sharding import PartitionSpec as P

sparsity_weight = 1.0
AXES = ("lat", "row")
CHUNKS = 2
f32 = jnp.float32
bf16 = jnp.bfloat16


def bits_below(n):
    return [1 << k for k in range(n.bit_length() - 1)]


class Grid:
    def __init__(self, mesh):
        self.lats, self.rows = mesh.shape["lat"], mesh.shape["row"]
        self.size = self.lats * self.rows
        self.core = self.rows
        self.row_bits = bits_below(self.rows)
        self.chip_bits = [2 * self.rows * b for b in bits_below(self.lats // 2)]
        self.chips = self.lats // 2

    def stream_of(self, i):
        parity = (i // self.core) % 2
        for b in self.row_bits + self.chip_bits:
            parity = parity ^ ((i // b) % 2)
        return parity

    def orders(self, bits):
        return list(zip(bits, bits[::-1]))

    def swap_core(self, v):
        return lax.ppermute(v, AXES, [(i, i ^ self.core) for i in range(self.size)])

    def step(self, v, pair):
        target = [i ^ self.core ^ pair[self.stream_of(i)] for i in range(self.size)]
        return lax.ppermute(v, AXES, list(enumerate(target)))


def on_device(grid, inputs, encoder, latent_bias, decoder, center_bias):
    me = lax.axis_index("lat") * grid.rows + lax.axis_index("row")
    core = (me // grid.core) % 2
    stream = grid.stream_of(me)
    chip = me // (2 * grid.core)
    nl, width = encoder.shape
    half, block = inputs.shape[0] // 2, 2 * inputs.shape[1]
    part = half // CHUNKS

    encoder_all = jnp.concatenate([encoder, grid.swap_core(encoder)], axis=0)
    decoder_all = jnp.concatenate([decoder, grid.swap_core(decoder)], axis=0)
    bias_all = jnp.concatenate([latent_bias, grid.swap_core(latent_bias)], axis=0)
    decoder_wide = decoder_all.astype(f32)
    norm_all = jnp.sqrt(jnp.sum(jnp.square(decoder_wide), axis=1) + 1e-06)

    shifted = inputs.astype(f32) - center_bias
    mine = jnp.where(stream == 0, shifted[:half], shifted[half:])
    other = jnp.where(stream == 0, shifted[half:], shifted[:half])
    theirs = grid.swap_core(other)
    shifted = jnp.where(
        core == 0,
        jnp.concatenate([mine, theirs], axis=1),
        jnp.concatenate([theirs, mine], axis=1),
    )

    def gather_columns(v):
        held = [v]
        for b in grid.chip_bits[::-1]:
            held = [held, [grid.step(u, (b, b)) for u in held]]
            held = held[0] + held[1]
        masks = [0]
        for b in bits_below(grid.chips)[::-1]:
            masks = masks + [m ^ b for m in masks]
        held = [u for _, u in sorted(zip(masks, held), key=lambda t: t[0])]
        for b in bits_below(grid.chips):
            flip = (chip // b) % 2 == 1
            held = [jnp.where(flip, held[k ^ b], held[k]) for k in range(len(held))]
        return jnp.concatenate(held, axis=1)

    def gather_rows(v):
        for pair in grid.orders(grid.row_bits):
            v = jnp.concatenate([v, grid.step(v, pair)], axis=0)
        return v

    def scatter_rows(v):
        for pair in grid.orders(grid.row_bits)[::-1]:
            n = v.shape[0] // 2
            v = v[:n] + grid.step(v[n:].astype(bf16), pair).astype(f32)
        return v

    def sum_chips(v):
        for pair in grid.orders(grid.chip_bits):
            v = v + grid.step(v.astype(bf16), pair).astype(f32)
        return v

    centered, latents, errors, grad_pres = [], [], [], []
    column_sum = 0.0
    blocks = gather_columns(shifted.astype(bf16))
    for k in range(CHUNKS):
        rows = slice(k * part, (k + 1) * part)
        cent = gather_rows(blocks[rows])
        preact = (
            lax.dot_general(cent, encoder_all, (((1,), (1,)), ((), ())), preferred_element_type=f32)
            + bias_all
        )
        lats = (jax.nn.softplus(4.0 * preact) / 4.0).astype(bf16)
        recon = jnp.dot(lats, decoder_all, preferred_element_type=f32)
        own = scatter_rows(recon)
        zeros = jnp.zeros((part, block), f32)
        placed = jnp.concatenate(
            [jnp.where(chip == p, shifted[rows], zeros) for p in range(grid.chips)], axis=1
        )
        error = sum_chips(own - placed)
        column_sum = column_sum + jnp.sum(error, axis=0)
        err = gather_rows(error.astype(bf16))
        grad_latent = (
            lax.dot_general(err, decoder_all, (((1,), (1,)), ((), ())), preferred_element_type=f32)
            + sparsity_weight * norm_all
        )
        grad_pre = (grad_latent * jax.nn.sigmoid(4.0 * preact)).astype(bf16)
        centered += [cent, grid.swap_core(cent)]
        latents += [lats[:, :nl], grid.swap_core(lats[:, nl:])]
        errors += [err, grid.swap_core(err)]
        grad_pres += [grad_pre]

    bias_part = sum(jnp.sum(g.astype(f32), axis=0) for g in grad_pres)
    terms = column_sum * (1.0 / grid.chips) - jnp.dot(
        bias_part, encoder_all.astype(f32), precision=lax.Precision.HIGHEST
    )
    left = (terms + grid.swap_core(terms)).reshape(1, width)

    def halve(left, b):
        n = left.shape[1] // 2
        upper = (me // b) % 2 == 1
        kept = jnp.where(upper, left[:, n:], left[:, :n])
        sent = jnp.where(upper, left[:, :n], left[:, n:])
        return kept + grid.step(sent, (b, b))

    for b in grid.chip_bits[::-1]:
        left = halve(left, b)
    left = left.reshape(2, width // grid.chips // 2)
    for b in grid.row_bits[::-1]:
        left = halve(left, b)
    center_grad = jnp.where(core == 0, left[0], left[1])

    pres = []
    for g in grad_pres:
        pres += [g[:, :nl], grid.swap_core(g[:, nl:])]
    centered, latents = jnp.concatenate(centered), jnp.concatenate(latents)
    errors, pres = jnp.concatenate(errors), jnp.concatenate(pres)
    latent_total = jnp.sum(latents.astype(f32), axis=0)
    bias_grad = jnp.sum(pres.astype(f32), axis=0)
    scale = sparsity_weight * latent_total / norm_all[:nl]
    decoder_grad = (
        lax.dot_general(latents, errors, (((0,), (0,)), ((), ())), preferred_element_type=f32)
        + scale[:, None] * decoder.astype(f32)
    ).astype(bf16)
    encoder_grad = lax.dot_general(
        pres, centered, (((0,), (0,)), ((), ())), preferred_element_type=f32
    ).astype(bf16)
    return (encoder_grad, decoder_grad, bias_grad, center_grad)


def solution(mesh):
    grid = Grid(mesh)
    in_specs = (P("row", "lat"), P(AXES, None), P(AXES), P(AXES, None), P("lat"))
    out_specs = (P(AXES, None), P(AXES, None), P(AXES), P(AXES))

    def device_function(*args):
        return on_device(grid, *args)

    return jax.shard_map(
        device_function, mesh=mesh, in_specs=in_specs, out_specs=out_specs, check_vma=False
    )
```

time: 206 us -> 110 us (0.53)
  waiting for transfers between devices: 113 us -> 40.3 us
  blocking collectives: 60 us -> 0 us
  starting transfers between devices: 0.16 us -> 40.8 us
  between operations: 13.8 us -> 1.05 us
  local copies, waits for them, and re-layouts: 4.05 us -> 12.7 us
  other arithmetic: 2.36 us -> 5.18 us
    reduce_scatter x2 -> x0, waiting for transfers between devices: 58.6 us -> none  [the longest x1 34.7 us: on_device(): lax.psum_scatter(partial_sum.astype(jnp.bfloat16), 'lat', scatter_dimensi...]
    all_gather x2 -> x0, waiting for transfers between devices: 54 us -> none  [the longest x1 27.3 us: on_device(): centered = lax.all_gather(by_rows, 'lat', axis=1, tiled=True)]
    ppermute x0 -> x36, starting transfers between devices: none -> 40.8 us  [the longest x23 37 us: step(): return lax.ppermute(v, AXES, list(enumerate(target)))]
    ppermute x0 -> x36, waiting for transfers between devices: none -> 40.3 us  [the longest x23 37.7 us: step(): return lax.ppermute(v, AXES, list(enumerate(target)))]
    unnamed x1 -> x0, blocking collectives: 40.3 us -> none
    all_gather x2 -> x0, blocking collectives: 19.7 us -> none  [the longest x1 10.4 us: on_device(): by_rows = lax.all_gather(centered_part, 'row', axis=0, tiled=True)]
    unnamed x14 -> x23, local copies, waits for them, and re-layouts: 2.39 us -> 8.6 us
    concatenate x0 -> x4, local copies, waits for them, and re-layouts: none -> 3.57 us  [the longest x1 1.36 us: on_device(): decoder_all = jnp.concatenate([decoder, grid.swap_core(decoder)], axis=0)]
  transfers between devices with their start and end apart: 4 -> 36, of which waited for: 4 -> 20; matrix products, arithmetic and copies ran while one was open for 0% -> 16% of each run, Pallas kernels for 0% -> 0%
where the time goes in v1:
time: 110 us
  starting transfers between devices  40.8 us (37%)
  waiting for transfers between devices  40.3 us (37%)
  local copies, waits for them, and re-layouts  12.7 us (12%)
  matrix products  10.2 us (9%)
  other arithmetic  5.18 us (5%)
    ppermute x23, waiting for transfers between devices, step(): return lax.ppermute(v, AXES, list(enumerate(target)))  37.7 us
    ppermute x23, starting transfers between devices, step(): return lax.ppermute(v, AXES, list(enumerate(target)))  37 us
    unnamed x23, local copies, waits for them, and re-layouts  8.6 us
    ppermute x13, starting transfers between devices, swap_core(): return lax.ppermute(v, AXES, [(i, i ^ self.core) for i in range(self.size)])  3.79 us
    dot_general x1, matrix products, on_device(): lax.dot_general(latents, errors, (((0,), (0,)), ((), ())), preferred_elem...  3.04 us
    ppermute x13, waiting for transfers between devices, swap_core(): return lax.ppermute(v, AXES, [(i, i ^ self.core) for i in range(self.size)])  2.57 us
  transfers between devices with their start and end apart: 36, of which 20 were waited for; matrix products, arithmetic and copies ran while one was open for 16% of the time, Pallas kernels for 0%

profile of v1, /device:TPU:0, one launch (start us, length us, event | category | flops | bytes accessed | tf_op | source)
XLA Modules:
  0.0 110.2 jit_solution(17617960017012015389)
XLA Ops:
  2.7 2.4 %constant_dynamic-update-slice_fusion.1 = bf16[336,3584]{1,0:T(8,128)(2,1)} fusion(bf16[168,3584]{1,0:T(8,128)(2,1)} %param.6), kind=kLoop, calls=%fused_computation.77 | loop fusion | bytes 2408448
  5.2 3.8 %collective-permute-start.1 = (bf16[32,896]{1,0:T(8,128)(2,1)S(1)}, bf16[32,896]{1,0:T(8,128)(2,1)S(1)}, u32[]{:S(2)}, u32[]{:S(2)}) collective-permute-start(bf16[32,896]{1,0:T(8,128)(2,1)S(1)} %get-tuple-element.12), channel_id=1, source_target_pairs={{0,20},{1,21},{2,22},{3,23},{4,16},{5,17},{6,18},{7,19},{8,28},{9,... | collective-permute-start | bytes 172040 | tf_op jit(solution)/shard_map/ppermute | solution.py:40
  14.3 1.7 %collective-permute-done.2 = bf16[32,896]{1,0:T(8,128)(2,1)S(1)} collective-permute-done((bf16[32,896]{1,0:T(8,128)(2,1)S(1)}, bf16[32,896]{1,0:T(8,128)(2,1)S(1)}, u32[]{:S(2)}, u32[]{:S(2)}) %collective-permute-start.2) | collective-permute-done | bytes 57376 | tf_op jit(solution)/shard_map/ppermute | solution.py:40
  16.0 1.7 %collective-permute-start.16 = (bf16[16,3584]{1,0:T(8,128)(2,1)S(1)}, bf16[16,3584]{1,0:T(8,128)(2,1)S(1)}, u32[]{:S(2)}, u32[]{:S(2)}) collective-permute-start(bf16[16,3584]{1,0:T(8,128)(2,1)S(1)} %get-tuple-element.14), channel_id=1, source_target_pairs={{0,5},{1,7},{2,4},{3,6},{4,2},{5,0},{6,3},{7,1},{8,14},{9,12},{10,... | collective-permute-start | bytes 344072 | tf_op jit(solution)/shard_map/ppermute | solution.py:40
  17.9 2.4 %collective-permute-done.16 = bf16[16,3584]{1,0:T(8,128)(2,1)S(1)} collective-permute-done((bf16[16,3584]{1,0:T(8,128)(2,1)S(1)}, bf16[16,3584]{1,0:T(8,128)(2,1)S(1)}, u32[]{:S(2)}, u32[]{:S(2)}) %collective-permute-start.16) | collective-permute-done | bytes 114720 | tf_op jit(solution)/shard_map/ppermute | solution.py:40
  20.3 2.0 %collective-permute-start.17 = (bf16[32,3584]{1,0:T(8,128)(2,1)S(1)}, bf16[32,3584]{1,0:T(8,128)(2,1)S(1)}, u32[]{:S(2)}, u32[]{:S(2)}) collective-permute-start(bf16[32,3584]{1,0:T(8,128)(2,1)S(1)} %pad_maximum_fusion.7), channel_id=1, source_target_pairs={{0,6},{1,4},{2,7},{3,5},{4,1},{5,3},{6,0},{7,2},{8,13},{9,15},{10,... | collective-permute-start | bytes 688136 | tf_op jit(solution)/shard_map/ppermute | solution.py:40
  23.3 5.2 %collective-permute-done.5 = bf16[32,3584]{1,0:T(8,128)(2,1)S(1)} collective-permute-done((bf16[32,3584]{1,0:T(8,128)(2,1)S(1)}, bf16[32,3584]{1,0:T(8,128)(2,1)S(1)}, u32[]{:S(2)}, u32[]{:S(2)}) %collective-permute-start.5) | collective-permute-done | bytes 229408 | tf_op jit(solution)/shard_map/ppermute | solution.py:40
  39.3 1.8 %collective-permute-start.18 = (bf16[32,3584]{1,0:T(8,128)(2,1)S(1)}, bf16[32,3584]{1,0:T(8,128)(2,1)S(1)}, u32[]{:S(2)}, u32[]{:S(2)}) collective-permute-start(bf16[32,3584]{1,0:T(8,128)(2,1)S(1)} %slice.227), channel_id=1, source_target_pairs={{0,6},{1,4},{2,7},{3,5},{4,1},{5,3},{6,0},{7,2},{8,13},{9,15},{10,... | collective-permute-start | bytes 688136 | tf_op jit(solution)/shard_map/ppermute | solution.py:40
  41.3 6.0 %collective-permute-done.9 = bf16[32,3584]{1,0:T(8,128)(2,1)S(1)} collective-permute-done((bf16[32,3584]{1,0:T(8,128)(2,1)S(1)}, bf16[32,3584]{1,0:T(8,128)(2,1)S(1)}, u32[]{:S(2)}, u32[]{:S(2)}) %collective-permute-start.9) | collective-permute-done | bytes 229408 | tf_op jit(solution)/shard_map/ppermute | solution.py:40
  47.4 1.8 %collective-permute-start.10 = (bf16[16,3584]{1,0:T(8,128)(2,1)S(1)}, bf16[16,3584]{1,0:T(8,128)(2,1)S(1)}, u32[]{:S(2)}, u32[]{:S(2)}) collective-permute-start(bf16[16,3584]{1,0:T(8,128)(2,1)S(1)} %slice.230), channel_id=1, source_target_pairs={{0,5},{1,7},{2,4},{3,6},{4,2},{5,0},{6,3},{7,1},{8,14},{9,12},{10,... | collective-permute-start | bytes 344072 | tf_op jit(solution)/shard_map/ppermute | solution.py:40
  49.3 2.3 %collective-permute-done.10 = bf16[16,3584]{1,0:T(8,128)(2,1)S(1)} collective-permute-done((bf16[16,3584]{1,0:T(8,128)(2,1)S(1)}, bf16[16,3584]{1,0:T(8,128)(2,1)S(1)}, u32[]{:S(2)}, u32[]{:S(2)}) %collective-permute-start.10) | collective-permute-done | bytes 114720 | tf_op jit(solution)/shard_map/ppermute | solution.py:40
  51.7 2.0 %collective-permute-start.11 = (bf16[16,3584]{1,0:T(8,128)(2,1)S(1)}, bf16[16,3584]{1,0:T(8,128)(2,1)S(1)}, u32[]{:S(2)}, u32[]{:S(2)}) collective-permute-start(bf16[16,3584]{1,0:T(8,128)(2,1)S(1)} %get-tuple-element.8), channel_id=1, source_target_pairs={{0,12},{1,21},{2,22},{3,15},{4,16},{5,9},{6,10},{7,19},{8,28},{9,5... | collective-permute-start | bytes 344072 | tf_op jit(solution)/shard_map/ppermute | solution.py:40
  54.8 2.1 %collective-permute-done.11 = bf16[16,3584]{1,0:T(8,128)(2,1)S(1)} collective-permute-done((bf16[16,3584]{1,0:T(8,128)(2,1)S(1)}, bf16[16,3584]{1,0:T(8,128)(2,1)S(1)}, u32[]{:S(2)}, u32[]{:S(2)}) %collective-permute-start.11) | collective-permute-done | bytes 114720 | tf_op jit(solution)/shard_map/ppermute | solution.py:40
  57.0 3.6 %collective-permute-start.12 = (bf16[16,3584]{1,0:T(8,128)(2,1)S(1)}, bf16[16,3584]{1,0:T(8,128)(2,1)S(1)}, u32[]{:S(2)}, u32[]{:S(2)}) collective-permute-start(bf16[16,3584]{1,0:T(8,128)(2,1)S(1)} %fusion.9), channel_id=1, source_target_pairs={{0,20},{1,13},{2,14},{3,23},{4,8},{5,17},{6,18},{7,11},{8,4},{9,29... | collective-permute-start | bytes 344072 | tf_op jit(solution)/shard_map/ppermute | solution.py:40
  60.6 2.1 %collective-permute-start.21 = (bf16[16,3584]{1,0:T(8,128)(2,1)S(1)}, bf16[16,3584]{1,0:T(8,128)(2,1)S(1)}, u32[]{:S(2)}, u32[]{:S(2)}) collective-permute-start(bf16[16,3584]{1,0:T(8,128)(2,1)S(1)} %fusion.10), channel_id=1, source_target_pairs={{0,20},{1,13},{2,14},{3,23},{4,8},{5,17},{6,18},{7,11},{8,4},{9,29... | collective-permute-start | bytes 344072 | tf_op jit(solution)/shard_map/ppermute | solution.py:40
  62.7 2.2 %collective-permute-done.12 = bf16[16,3584]{1,0:T(8,128)(2,1)S(1)} collective-permute-done((bf16[16,3584]{1,0:T(8,128)(2,1)S(1)}, bf16[16,3584]{1,0:T(8,128)(2,1)S(1)}, u32[]{:S(2)}, u32[]{:S(2)}) %collective-permute-start.12) | collective-permute-done | bytes 114720 | tf_op jit(solution)/shard_map/ppermute | solution.py:40
  67.4 2.4 %collective-permute-done.13 = bf16[16,3584]{1,0:T(8,128)(2,1)S(1)} collective-permute-done((bf16[16,3584]{1,0:T(8,128)(2,1)S(1)}, bf16[16,3584]{1,0:T(8,128)(2,1)S(1)}, u32[]{:S(2)}, u32[]{:S(2)}) %collective-permute-start.13) | collective-permute-done | bytes 114720 | tf_op jit(solution)/shard_map/ppermute | solution.py:40
  71.8 3.5 %collective-permute-done.14 = bf16[32,3584]{1,0:T(8,128)(2,1)S(1)} collective-permute-done((bf16[32,3584]{1,0:T(8,128)(2,1)S(1)}, bf16[32,3584]{1,0:T(8,128)(2,1)S(1)}, u32[]{:S(2)}, u32[]{:S(2)}) %collective-permute-start.14) | collective-permute-done | bytes 229408 | tf_op jit(solution)/shard_map/ppermute | solution.py:40
  80.4 2.6 %collective-permute-done.22 = bf16[16,3584]{1,0:T(8,128)(2,1)S(1)} collective-permute-done((bf16[16,3584]{1,0:T(8,128)(2,1)S(1)}, bf16[16,3584]{1,0:T(8,128)(2,1)S(1)}, u32[]{:S(2)}, u32[]{:S(2)}) %collective-permute-start.22) | collective-permute-done | bytes 114720 | tf_op jit(solution)/shard_map/ppermute | solution.py:40
  85.0 3.5 %collective-permute-done.23 = bf16[32,3584]{1,0:T(8,128)(2,1)S(1)} collective-permute-done((bf16[32,3584]{1,0:T(8,128)(2,1)S(1)}, bf16[32,3584]{1,0:T(8,128)(2,1)S(1)}, u32[]{:S(2)}, u32[]{:S(2)}) %collective-permute-start.23) | collective-permute-done | bytes 229408 | tf_op jit(solution)/shard_map/ppermute | solution.py:40
  91.7 2.7 %collective-permute-start.32 = (f32[1,1792]{1,0:T(1,128)S(1)}, f32[1,1792]{1,0:T(1,128)S(1)}, u32[]{:S(2)}, u32[]{:S(2)}) collective-permute-start(f32[1,1792]{1,0:T(1,128)S(1)} %broadcast_select_fusion.8), channel_id=1, source_target_pairs={{0,20},{1,21},{2,22},{3,23},{4,16},{5,17},{6,18},{7,19},{8,28},{9,... | collective-permute-start | bytes 21512 | tf_op jit(solution)/shard_map/ppermute | solution.py:40
  95.8 1.9 %collective-permute-start.33 = (f32[1,896]{1,0:T(1,128)S(1)}, f32[1,896]{1,0:T(1,128)S(1)}, u32[]{:S(2)}, u32[]{:S(2)}) collective-permute-start(f32[1,896]{1,0:T(1,128)S(1)} %broadcast_select_fusion.10), channel_id=1, source_target_pairs={{0,12},{1,13},{2,14},{3,15},{4,8},{5,9},{6,10},{7,11},{8,4},{9,5},... | collective-permute-start | bytes 10760 | tf_op jit(solution)/shard_map/ppermute | solution.py:40
  99.3 1.7 %collective-permute-start.34 = (f32[2,224]{1,0:T(2,128)S(1)}, f32[2,224]{1,0:T(2,128)S(1)}, u32[]{:S(2)}, u32[]{:S(2)}) collective-permute-start(f32[2,224]{1,0:T(2,128)S(1)} %broadcast_select_fusion.12), channel_id=1, source_target_pairs={{0,6},{1,7},{2,4},{3,5},{4,2},{5,3},{6,0},{7,1},{8,14},{9,15},{10,... | collective-permute-start | bytes 5384 | tf_op jit(solution)/shard_map/ppermute | solution.py:40
  107.1 3.0 %fusion = bf16[168,3584]{1,0:T(8,128)(2,1)} fusion(bf16[256,3584]{1,0:T(8,128)(2,1)} %constant_dynamic-update-slice_fusion.12, bf16[168,3584]{1,0:T(8,128)(2,1)S(1)} %copy-done.1, f32[168]{0:T(256)S(1)} %slice_divide_fusion, bf16[64,168]{1,0:T(8,128)(2,1)S(1)} %collective-permute-done.28, bf16[64,168]{1,0:T(8,128)(2,1)S(1)} %get-tuple-element.33, ...), kind=kOutput, calls=%fused_computation.1 | convolution fusion | flops 311033856 | bytes 4330144 | tf_op jit(solution)/shard_map/dot_general | solution.py:157
  (138 shorter events, 44.7 us)
Async XLA Ops:
  0.6 12.7 %collective-permute-start.7 = (f32[168]{0:T(256)}, f32[168]{0:T(256)S(1)}, u32[]{:S(2)}, u32[]{:S(2)}) collective-permute-start(f32[168]{0:T(256)} %param.7), channel_id=1, source_target_pairs={{0,4},{1,5},{2,6},{3,7},{4,0},{5,1},{6,2},{7,3},{8,12},{9,13},{10,... | collective-permute-start | bytes 2024 | tf_op jit(solution)/shard_map/ppermute | solution.py:36
  2.2 30.1 %collective-permute-start.6 = (bf16[168,3584]{1,0:T(8,128)(2,1)}, bf16[168,3584]{1,0:T(8,128)(2,1)}, u32[]{:S(2)}, u32[]{:S(2)}) collective-permute-start(bf16[168,3584]{1,0:T(8,128)(2,1)} %param.6), channel_id=1, source_target_pairs={{0,4},{1,5},{2,6},{3,7},{4,0},{5,1},{6,2},{7,3},{8,12},{9,13},{10,... | collective-permute-start | bytes 3612680 | tf_op jit(solution)/shard_map/ppermute | solution.py:36
  2.6 32.1 %collective-permute-start.8 = (bf16[168,3584]{1,0:T(8,128)(2,1)}, bf16[168,3584]{1,0:T(8,128)(2,1)}, u32[]{:S(2)}, u32[]{:S(2)}) collective-permute-start(bf16[168,3584]{1,0:T(8,128)(2,1)} %param.8), channel_id=1, source_target_pairs={{0,4},{1,5},{2,6},{3,7},{4,0},{5,1},{6,2},{7,3},{8,12},{9,13},{10,... | collective-permute-start | bytes 3612680 | tf_op jit(solution)/shard_map/ppermute | solution.py:36
  5.2 6.8 %collective-permute-start.1 = (bf16[32,896]{1,0:T(8,128)(2,1)S(1)}, bf16[32,896]{1,0:T(8,128)(2,1)S(1)}, u32[]{:S(2)}, u32[]{:S(2)}) collective-permute-start(bf16[32,896]{1,0:T(8,128)(2,1)S(1)} %get-tuple-element.12), channel_id=1, source_target_pairs={{0,20},{1,21},{2,22},{3,23},{4,16},{5,17},{6,18},{7,19},{8,28},{9,... | collective-permute-start | bytes 172040 | tf_op jit(solution)/shard_map/ppermute | solution.py:40
  16.0 4.3 %collective-permute-start.16 = (bf16[16,3584]{1,0:T(8,128)(2,1)S(1)}, bf16[16,3584]{1,0:T(8,128)(2,1)S(1)}, u32[]{:S(2)}, u32[]{:S(2)}) collective-permute-start(bf16[16,3584]{1,0:T(8,128)(2,1)S(1)} %get-tuple-element.14), channel_id=1, source_target_pairs={{0,5},{1,7},{2,4},{3,6},{4,2},{5,0},{6,3},{7,1},{8,14},{9,12},{10,... | collective-permute-start | bytes 344072 | tf_op jit(solution)/shard_map/ppermute | solution.py:40
  17.7 4.6 %collective-permute-start.4 = (bf16[16,3584]{1,0:T(8,128)(2,1)S(1)}, bf16[16,3584]{1,0:T(8,128)(2,1)S(1)}, u32[]{:S(2)}, u32[]{:S(2)}) collective-permute-start(bf16[16,3584]{1,0:T(8,128)(2,1)S(1)} %get-tuple-element.16), channel_id=1, source_target_pairs={{0,5},{1,7},{2,4},{3,6},{4,2},{5,0},{6,3},{7,1},{8,14},{9,12},{10,... | collective-permute-start | bytes 344072 | tf_op jit(solution)/shard_map/ppermute | solution.py:40
  20.3 8.4 %collective-permute-start.17 = (bf16[32,3584]{1,0:T(8,128)(2,1)S(1)}, bf16[32,3584]{1,0:T(8,128)(2,1)S(1)}, u32[]{:S(2)}, u32[]{:S(2)}) collective-permute-start(bf16[32,3584]{1,0:T(8,128)(2,1)S(1)} %pad_maximum_fusion.7), channel_id=1, source_target_pairs={{0,6},{1,4},{2,7},{3,5},{4,1},{5,3},{6,0},{7,2},{8,13},{9,15},{10,... | collective-permute-start | bytes 688136 | tf_op jit(solution)/shard_map/ppermute | solution.py:40
  22.3 6.1 %collective-permute-start.5 = (bf16[32,3584]{1,0:T(8,128)(2,1)S(1)}, bf16[32,3584]{1,0:T(8,128)(2,1)S(1)}, u32[]{:S(2)}, u32[]{:S(2)}) collective-permute-start(bf16[32,3584]{1,0:T(8,128)(2,1)S(1)} %pad_maximum_fusion.5), channel_id=1, source_target_pairs={{0,6},{1,4},{2,7},{3,5},{4,1},{5,3},{6,0},{7,2},{8,13},{9,15},{10,... | collective-permute-start | bytes 688136 | tf_op jit(solution)/shard_map/ppermute | solution.py:40
  39.3 9.8 %collective-permute-start.18 = (bf16[32,3584]{1,0:T(8,128)(2,1)S(1)}, bf16[32,3584]{1,0:T(8,128)(2,1)S(1)}, u32[]{:S(2)}, u32[]{:S(2)}) collective-permute-start(bf16[32,3584]{1,0:T(8,128)(2,1)S(1)} %slice.227), channel_id=1, source_target_pairs={{0,6},{1,4},{2,7},{3,5},{4,1},{5,3},{6,0},{7,2},{8,13},{9,15},{10,... | collective-permute-start | bytes 688136 | tf_op jit(solution)/shard_map/ppermute | solution.py:40
  41.2 6.2 %collective-permute-start.9 = (bf16[32,3584]{1,0:T(8,128)(2,1)S(1)}, bf16[32,3584]{1,0:T(8,128)(2,1)S(1)}, u32[]{:S(2)}, u32[]{:S(2)}) collective-permute-start(bf16[32,3584]{1,0:T(8,128)(2,1)S(1)} %slice.228), channel_id=1, source_target_pairs={{0,6},{1,4},{2,7},{3,5},{4,1},{5,3},{6,0},{7,2},{8,13},{9,15},{10,... | collective-permute-start | bytes 688136 | tf_op jit(solution)/shard_map/ppermute | solution.py:40
  47.4 4.3 %collective-permute-start.10 = (bf16[16,3584]{1,0:T(8,128)(2,1)S(1)}, bf16[16,3584]{1,0:T(8,128)(2,1)S(1)}, u32[]{:S(2)}, u32[]{:S(2)}) collective-permute-start(bf16[16,3584]{1,0:T(8,128)(2,1)S(1)} %slice.230), channel_id=1, source_target_pairs={{0,5},{1,7},{2,4},{3,6},{4,2},{5,0},{6,3},{7,1},{8,14},{9,12},{10,... | collective-permute-start | bytes 344072 | tf_op jit(solution)/shard_map/ppermute | solution.py:40
  49.2 4.5 %collective-permute-start.19 = (bf16[16,3584]{1,0:T(8,128)(2,1)S(1)}, bf16[16,3584]{1,0:T(8,128)(2,1)S(1)}, u32[]{:S(2)}, u32[]{:S(2)}) collective-permute-start(bf16[16,3584]{1,0:T(8,128)(2,1)S(1)} %slice.229), channel_id=1, source_target_pairs={{0,5},{1,7},{2,4},{3,6},{4,2},{5,0},{6,3},{7,1},{8,14},{9,12},{10,... | collective-permute-start | bytes 344072 | tf_op jit(solution)/shard_map/ppermute | solution.py:40
  51.7 5.3 %collective-permute-start.11 = (bf16[16,3584]{1,0:T(8,128)(2,1)S(1)}, bf16[16,3584]{1,0:T(8,128)(2,1)S(1)}, u32[]{:S(2)}, u32[]{:S(2)}) collective-permute-start(bf16[16,3584]{1,0:T(8,128)(2,1)S(1)} %get-tuple-element.8), channel_id=1, source_target_pairs={{0,12},{1,21},{2,22},{3,15},{4,16},{5,9},{6,10},{7,19},{8,28},{9,5... | collective-permute-start | bytes 344072 | tf_op jit(solution)/shard_map/ppermute | solution.py:40
  53.8 6.8 %collective-permute-start.20 = (bf16[16,3584]{1,0:T(8,128)(2,1)S(1)}, bf16[16,3584]{1,0:T(8,128)(2,1)S(1)}, u32[]{:S(2)}, u32[]{:S(2)}) collective-permute-start(bf16[16,3584]{1,0:T(8,128)(2,1)S(1)} %get-tuple-element.10), channel_id=1, source_target_pairs={{0,12},{1,21},{2,22},{3,15},{4,16},{5,9},{6,10},{7,19},{8,28},{9,5... | collective-permute-start | bytes 344072 | tf_op jit(solution)/shard_map/ppermute | solution.py:40
  57.0 7.9 %collective-permute-start.12 = (bf16[16,3584]{1,0:T(8,128)(2,1)S(1)}, bf16[16,3584]{1,0:T(8,128)(2,1)S(1)}, u32[]{:S(2)}, u32[]{:S(2)}) collective-permute-start(bf16[16,3584]{1,0:T(8,128)(2,1)S(1)} %fusion.9), channel_id=1, source_target_pairs={{0,20},{1,13},{2,14},{3,23},{4,8},{5,17},{6,18},{7,11},{8,4},{9,29... | collective-permute-start | bytes 344072 | tf_op jit(solution)/shard_map/ppermute | solution.py:40
  60.6 6.7 %collective-permute-start.21 = (bf16[16,3584]{1,0:T(8,128)(2,1)S(1)}, bf16[16,3584]{1,0:T(8,128)(2,1)S(1)}, u32[]{:S(2)}, u32[]{:S(2)}) collective-permute-start(bf16[16,3584]{1,0:T(8,128)(2,1)S(1)} %fusion.10), channel_id=1, source_target_pairs={{0,20},{1,13},{2,14},{3,23},{4,8},{5,17},{6,18},{7,11},{8,4},{9,29... | collective-permute-start | bytes 344072 | tf_op jit(solution)/shard_map/ppermute | solution.py:40
  65.6 4.2 %collective-permute-start.13 = (bf16[16,3584]{1,0:T(8,128)(2,1)S(1)}, bf16[16,3584]{1,0:T(8,128)(2,1)S(1)}, u32[]{:S(2)}, u32[]{:S(2)}) collective-permute-start(bf16[16,3584]{1,0:T(8,128)(2,1)S(1)} %get-tuple-element.7), channel_id=1, source_target_pairs={{0,5},{1,7},{2,4},{3,6},{4,2},{5,0},{6,3},{7,1},{8,14},{9,12},{10,... | collective-permute-start | bytes 344072 | tf_op jit(solution)/shard_map/ppermute | solution.py:40
  69.8 5.5 %collective-permute-start.14 = (bf16[32,3584]{1,0:T(8,128)(2,1)S(1)}, bf16[32,3584]{1,0:T(8,128)(2,1)S(1)}, u32[]{:S(2)}, u32[]{:S(2)}) collective-permute-start(bf16[32,3584]{1,0:T(8,128)(2,1)S(1)} %pad_maximum_fusion.6), channel_id=1, source_target_pairs={{0,6},{1,4},{2,7},{3,5},{4,1},{5,3},{6,0},{7,2},{8,13},{9,15},{10,... | collective-permute-start | bytes 688136 | tf_op jit(solution)/shard_map/ppermute | solution.py:40
  78.7 4.2 %collective-permute-start.22 = (bf16[16,3584]{1,0:T(8,128)(2,1)S(1)}, bf16[16,3584]{1,0:T(8,128)(2,1)S(1)}, u32[]{:S(2)}, u32[]{:S(2)}) collective-permute-start(bf16[16,3584]{1,0:T(8,128)(2,1)S(1)} %get-tuple-element.5), channel_id=1, source_target_pairs={{0,5},{1,7},{2,4},{3,6},{4,2},{5,0},{6,3},{7,1},{8,14},{9,12},{10,... | collective-permute-start | bytes 344072 | tf_op jit(solution)/shard_map/ppermute | solution.py:40
  80.1 20.9 %collective-permute-start.15 = (bf16[64,168]{1,0:T(8,128)(2,1)S(1)}, bf16[64,168]{1,0:T(8,128)(2,1)S(1)}, u32[]{:S(2)}, u32[]{:S(2)}) collective-permute-start(bf16[64,168]{1,0:T(8,128)(2,1)S(1)} %get-tuple-element.36), channel_id=1, source_target_pairs={{0,4},{1,5},{2,6},{3,7},{4,0},{5,1},{6,2},{7,3},{8,12},{9,13},{10,... | collective-permute-start | bytes 64520 | tf_op jit(solution)/shard_map/ppermute | solution.py:36
  83.0 5.5 %collective-permute-start.23 = (bf16[32,3584]{1,0:T(8,128)(2,1)S(1)}, bf16[32,3584]{1,0:T(8,128)(2,1)S(1)}, u32[]{:S(2)}, u32[]{:S(2)}) collective-permute-start(bf16[32,3584]{1,0:T(8,128)(2,1)S(1)} %pad_maximum_fusion.8), channel_id=1, source_target_pairs={{0,6},{1,4},{2,7},{3,5},{4,1},{5,3},{6,0},{7,2},{8,13},{9,15},{10,... | collective-permute-start | bytes 688136 | tf_op jit(solution)/shard_map/ppermute | solution.py:40
  90.8 10.2 %collective-permute-start.24 = (bf16[64,168]{1,0:T(8,128)(2,1)S(1)}, bf16[64,168]{1,0:T(8,128)(2,1)S(1)}, u32[]{:S(2)}, u32[]{:S(2)}) collective-permute-start(bf16[64,168]{1,0:T(8,128)(2,1)S(1)} %get-tuple-element.38), channel_id=1, source_target_pairs={{0,4},{1,5},{2,6},{3,7},{4,0},{5,1},{6,2},{7,3},{8,12},{9,13},{10,... | collective-permute-start | bytes 64520 | tf_op jit(solution)/shard_map/ppermute | solution.py:36
  91.7 4.1 %collective-permute-start.32 = (f32[1,1792]{1,0:T(1,128)S(1)}, f32[1,1792]{1,0:T(1,128)S(1)}, u32[]{:S(2)}, u32[]{:S(2)}) collective-permute-start(f32[1,1792]{1,0:T(1,128)S(1)} %broadcast_select_fusion.8), channel_id=1, source_target_pairs={{0,20},{1,21},{2,22},{3,23},{4,16},{5,17},{6,18},{7,19},{8,28},{9,... | collective-permute-start | bytes 21512 | tf_op jit(solution)/shard_map/ppermute | solution.py:40
  94.5 11.8 %collective-permute-start.30 = (bf16[64,3584]{1,0:T(8,128)(2,1)S(1)}, bf16[64,3584]{1,0:T(8,128)(2,1)S(1)}, u32[]{:S(2)}, u32[]{:S(2)}) collective-permute-start(bf16[64,3584]{1,0:T(8,128)(2,1)S(1)} %pad_maximum_fusion.3), channel_id=1, source_target_pairs={{0,4},{1,5},{2,6},{3,7},{4,0},{5,1},{6,2},{7,3},{8,12},{9,13},{10,... | collective-permute-start | bytes 1376264 | tf_op jit(solution)/shard_map/ppermute | solution.py:36
  (17 other events, 63.7 us)

commit v2 on v1

v2 whole, which is shorter than its diff:
```python
import jax
import jax.numpy as jnp
from jax import lax
from jax.sharding import PartitionSpec as P

sparsity_weight = 1.0
AXES = ("lat", "row")
CHUNKS = 2
f32 = jnp.float32
bf16 = jnp.bfloat16


def bits_below(n):
    return [1 << k for k in range(n.bit_length() - 1)]


class Grid:
    def __init__(self, mesh):
        self.lats, self.rows = mesh.shape["lat"], mesh.shape["row"]
        self.size = self.lats * self.rows
        self.core = self.rows
        self.row_bits = bits_below(self.rows)
        self.chip_bits = [2 * self.rows * b for b in bits_below(self.lats // 2)]
        self.chips = self.lats // 2

    def stream_of(self, i):
        parity = (i // self.core) % 2
        for b in self.row_bits + self.chip_bits:
            parity = parity ^ ((i // b) % 2)
        return parity

    def orders(self, bits):
        return list(zip(bits, bits[::-1]))

    def swap_core(self, v):
        return lax.ppermute(v, AXES, [(i, i ^ self.core) for i in range(self.size)])

    def step(self, v, pair):
        target = [i ^ self.core ^ pair[self.stream_of(i)] for i in range(self.size)]
        return lax.ppermute(v, AXES, list(enumerate(target)))


def dot_rows(v, w):
    return lax.dot_general(v, w, (((1,), (1,)), ((), ())), preferred_element_type=f32)


def on_device(grid, inputs, encoder, latent_bias, decoder, center_bias):
    me = lax.axis_index("lat") * grid.rows + lax.axis_index("row")
    core = (me // grid.core) % 2
    stream = grid.stream_of(me)
    chip = me // (2 * grid.core)
    nl, width = encoder.shape
    half, block = inputs.shape[0] // 2, 2 * inputs.shape[1]
    part = half // CHUNKS

    encoders = [encoder, grid.swap_core(encoder)]
    decoders = [decoder, grid.swap_core(decoder)]
    biases = [latent_bias, grid.swap_core(latent_bias)]
    norms = [jnp.sqrt(jnp.sum(jnp.square(d.astype(f32)), axis=1) + 1e-06) for d in decoders]

    def side_by_side(mine, theirs, axis):
        return jnp.where(
            core == 0,
            jnp.concatenate([mine, theirs], axis=axis),
            jnp.concatenate([theirs, mine], axis=axis),
        )

    raw = side_by_side(inputs, grid.swap_core(inputs), 1)
    center = side_by_side(center_bias, grid.swap_core(center_bias), 0)
    shifted = jnp.where(stream == 0, raw[:half], raw[half:]).astype(f32) - center

    def gather_columns(v):
        held = [v]
        for b in grid.chip_bits[::-1]:
            held = held + [grid.step(u, (b, b)) for u in held]
        masks = [0]
        for b in bits_below(grid.chips)[::-1]:
            masks = masks + [m ^ b for m in masks]
        held = [u for _, u in sorted(zip(masks, held), key=lambda t: t[0])]
        for b in bits_below(grid.chips):
            flip = (chip // b) % 2 == 1
            held = [jnp.where(flip, held[k ^ b], held[k]) for k in range(len(held))]
        return jnp.concatenate(held, axis=1)

    orders = grid.orders(grid.row_bits)

    def gather_rows(v):
        for pair in orders[:-1]:
            v = jnp.concatenate([v, grid.step(v, pair)], axis=0)
        return [v, grid.step(v, orders[-1])]

    def scatter_rows(near, far):
        v = near + grid.step(far, orders[-1]).astype(f32)
        for pair in orders[:-1][::-1]:
            n = v.shape[0] // 2
            v = v[:n] + grid.step(v[n:].astype(bf16), pair).astype(f32)
        return v

    def sum_chips(v):
        for pair in grid.orders(grid.chip_bits):
            v = v + grid.step(v.astype(bf16), pair).astype(f32)
        return v

    columns = 0.0
    blocks = gather_columns(shifted.astype(bf16))
    parts = [slice(k * part, (k + 1) * part) for k in range(CHUNKS)]
    centered = [gather_rows(blocks[rows]) for rows in parts]
    latents, sigs, errors = [], [], []

    def forward(x):
        scaled = [4.0 * (dot_rows(x, e) + b) for e, b in zip(encoders, biases)]
        sigs.append([jax.nn.sigmoid(v) for v in scaled])
        lats = [(jax.nn.softplus(v) / 4.0).astype(bf16) for v in scaled]
        latents.append(lats)
        return sum(jnp.dot(l, d, preferred_element_type=f32) for l, d in zip(lats, decoders))

    for rows, (near, far) in zip(parts, centered):
        near, far = forward(near), forward(far).astype(bf16)
        own = scatter_rows(near, far)
        zeros = jnp.zeros((part, block), f32)
        placed = jnp.concatenate(
            [jnp.where(chip == p, shifted[rows], zeros) for p in range(grid.chips)], axis=1
        )
        error = sum_chips(own - placed)
        columns = columns + jnp.sum(error, axis=0, keepdims=True)
        errors += gather_rows(error.astype(bf16))
    centered = [c for pair in centered for c in pair]
    pres = []
    for err, sig in zip(errors, sigs):
        grads = [dot_rows(err, d) + sparsity_weight * n for d, n in zip(decoders, norms)]
        pres.append([(g * v).astype(bf16) for g, v in zip(grads, sig)])
    centered, latents, errors, pres, columns = lax.optimization_barrier(
        (centered, latents, errors, pres, columns)
    )

    terms = (1.0 / grid.chips) * columns
    for side, enc in enumerate(encoders):
        bias = sum(jnp.sum(p[side].astype(f32), axis=0) for p in pres)
        terms = terms - jnp.dot(bias, enc.astype(f32), precision=lax.Precision.HIGHEST)
    left = terms + grid.swap_core(terms)

    def halve(left, b):
        n = left.shape[1] // 2
        upper = (me // b) % 2 == 1
        kept = jnp.where(upper, left[:, n:], left[:, :n])
        sent = jnp.where(upper, left[:, :n], left[:, n:])
        return kept + grid.step(sent, (b, b))

    def all_rows(mine, theirs):
        return jnp.concatenate([*mine, grid.swap_core(jnp.concatenate(theirs, axis=0))], axis=0)

    latents = all_rows([l[0] for l in latents], [l[1] for l in latents])
    pres = all_rows([p[0] for p in pres], [p[1] for p in pres])
    errors = all_rows(errors, errors)
    centered = all_rows(centered, centered)
    latent_total = jnp.sum(latents.astype(f32), axis=0)
    scale = (sparsity_weight * latent_total / norms[0])[:, None]

    def over_rows(u, v):
        return lax.dot_general(u, v, (((0,), (0,)), ((), ())), preferred_element_type=f32)

    for k, b in enumerate((grid.row_bits + grid.chip_bits)[::-1]):
        if k == len(grid.chip_bits):
            left = left.reshape(2, width // grid.chips // 2)
        if k == 2:
            left, decoder_grad = lax.optimization_barrier((left, decoder_grad))
        if k == 3:
            left, encoder_grad = lax.optimization_barrier((left, encoder_grad))
        left = halve(left, b)
        if k == 0:
            left, latents, errors = lax.optimization_barrier((left, latents, errors))
            decoder_grad = over_rows(latents, errors) + scale * decoder.astype(f32)
            decoder_grad = decoder_grad.astype(bf16)
        if k == 1:
            left, pres, centered = lax.optimization_barrier((left, pres, centered))
            bias_grad = jnp.sum(pres.astype(f32), axis=0)
            encoder_grad = over_rows(pres, centered).astype(bf16)
    center_grad = jnp.where(core == 0, left[0], left[1])
    return (encoder_grad, decoder_grad, bias_grad, center_grad)


def solution(mesh):
    grid = Grid(mesh)
    in_specs = (P("row", "lat"), P(AXES, None), P(AXES), P(AXES, None), P("lat"))
    out_specs = (P(AXES, None), P(AXES, None), P(AXES), P(AXES))

    def device_function(*args):
        return on_device(grid, *args)

    return jax.shard_map(
        device_function, mesh=mesh, in_specs=in_specs, out_specs=out_specs, check_vma=False
    )
```

time: 110 us -> 84.5 us (0.77)
  waiting for transfers between devices: 40.3 us -> 21.1 us
  local copies, waits for them, and re-layouts: 12.7 us -> 0.45 us
  matrix products: 10.2 us -> 14.7 us
    ppermute x23, waiting for transfers between devices: 37.7 us -> 21.1 us  [step(): return lax.ppermute(v, AXES, list(enumerate(target)))]
    unnamed x23 -> x20, local copies, waits for them, and re-layouts: 8.6 us -> 0.18 us
    dot_general x9 -> x28, matrix products: 10.2 us -> 14.7 us  [the longest x16 7.73 us: dot_rows(): lax.dot_general(v, w, (((1,), (1,)), ((), ())), preferred_element_type=f32)]
    concatenate x4, local copies, waits for them, and re-layouts: 3.57 us -> 0.14 us  [all_rows(): jnp.concatenate([*mine, grid.swap_core(jnp.concatenate(theirs, axis=0))],...]
    ppermute x13 -> x10, waiting for transfers between devices: 2.57 us -> 0.04 us  [swap_core(): return lax.ppermute(v, AXES, [(i, i ^ self.core) for i in range(self.size)])]
    select_n x1 -> x2, other arithmetic: 0.01 us -> 1.86 us  [side_by_side(): jnp.where(core == 0, jnp.concatenate([mine, theirs], axis=axis), jnp.conc...]
    reduce_sum x3 -> x8, other arithmetic: 0.69 us -> 2.18 us  [the longest x2 1.92 us: on_device(): jnp.sum(jnp.square(d.astype(f32)), axis=1) + 1e-06]
    unnamed x2 -> x0, other arithmetic: 1.37 us -> none
  transfers between devices with their start and end apart: 36 -> 33, of which waited for: 20 -> 17; matrix products, arithmetic and copies ran while one was open for 16% -> 21% of each run, Pallas kernels for 0% -> 0%
where the time goes in v2:
time: 84.5 us; the launch traced here: 84.2 us
  starting transfers between devices  40.7 us (48%)
  waiting for transfers between devices  21.1 us (25%)
  matrix products  14.7 us (17%)
  other arithmetic  6.09 us (7%)
  between operations  1.13 us (1%)
    ppermute x23, starting transfers between devices, step(): return lax.ppermute(v, AXES, list(enumerate(target)))  37.8 us
    ppermute x23, waiting for transfers between devices, step(): return lax.ppermute(v, AXES, list(enumerate(target)))  21.1 us
    dot_general x16, matrix products, dot_rows(): lax.dot_general(v, w, (((1,), (1,)), ((), ())), preferred_element_type=f32)  7.73 us
    dot_general x2, matrix products, over_rows(): lax.dot_general(u, v, (((0,), (0,)), ((), ())), preferred_element_type=f32)  3.06 us
    ppermute x10, starting transfers between devices, swap_core(): return lax.ppermute(v, AXES, [(i, i ^ self.core) for i in range(self.size)])  2.91 us
    dot_general x8, matrix products, forward(): jnp.dot(l, d, preferred_element_type=f32)  2.76 us
    reduce_sum x2, other arithmetic, on_device(): jnp.sum(jnp.square(d.astype(f32)), axis=1) + 1e-06  1.92 us
    select_n x2, other arithmetic, side_by_side(): jnp.where(core == 0, jnp.concatenate([mine, theirs], axis=axis), jnp.conc...  1.86 us
  transfers between devices with their start and end apart: 33, of which 17 were waited for; matrix products, arithmetic and copies ran while one was open for 21% of the time, Pallas kernels for 0%

profile of v2, /device:TPU:0, one launch (start us, length us, event | category | flops | bytes accessed | tf_op | source)
XLA Modules:
  0.0 84.2 jit_solution(9776825636355789207)
XLA Ops:
  4.1 3.8 %collective-permute-start.2 = (bf16[32,896]{1,0:T(8,128)(2,1)S(1)}, bf16[32,896]{1,0:T(8,128)(2,1)S(1)}, u32[]{:S(2)}, u32[]{:S(2)}) collective-permute-start(bf16[32,896]{1,0:T(8,128)(2,1)S(1)} %get-tuple-element.78), channel_id=1, source_target_pairs={{0,20},{1,21},{2,22},{3,23},{4,16},{5,17},{6,18},{7,19},{8,28},{9,... | collective-permute-start | bytes 172040 | tf_op jit(solution)/shard_map/ppermute | solution.py:40
  7.8 1.6 %fusion.5 = f32[168]{0:T(256)S(1)} fusion(bf16[168,3584]{1,0:T(8,128)(2,1)} %param.8), kind=kLoop, calls=%fused_computation.13 | loop fusion | flops 1806168 | bytes 1204896 | tf_op jit(solution)/shard_map/reduce_sum | solution.py:59
  9.4 1.6 %collective-permute-start.4 = (bf16[32,896]{1,0:T(8,128)(2,1)S(1)}, bf16[32,896]{1,0:T(8,128)(2,1)S(1)}, u32[]{:S(2)}, u32[]{:S(2)}) collective-permute-start(bf16[32,896]{1,0:T(8,128)(2,1)S(1)} %get-tuple-element.78), channel_id=1, source_target_pairs={{0,12},{1,13},{2,14},{3,15},{4,8},{5,9},{6,10},{7,11},{8,4},{9,5},... | collective-permute-start | bytes 172040 | tf_op jit(solution)/shard_map/ppermute | solution.py:40
  13.3 1.7 %collective-permute-done.3 = bf16[32,896]{1,0:T(8,128)(2,1)S(1)} collective-permute-done((bf16[32,896]{1,0:T(8,128)(2,1)S(1)}, bf16[32,896]{1,0:T(8,128)(2,1)S(1)}, u32[]{:S(2)}, u32[]{:S(2)}) %collective-permute-start.3) | collective-permute-done | bytes 57376 | tf_op jit(solution)/shard_map/ppermute | solution.py:40
  17.0 2.4 %collective-permute-done.5 = bf16[16,3584]{1,0:T(8,128)(2,1)S(1)} collective-permute-done((bf16[16,3584]{1,0:T(8,128)(2,1)S(1)}, bf16[16,3584]{1,0:T(8,128)(2,1)S(1)}, u32[]{:S(2)}, u32[]{:S(2)}) %collective-permute-start.5) | collective-permute-done | bytes 114720 | tf_op jit(solution)/shard_map/ppermute | solution.py:40
  19.4 1.8 %collective-permute-start.6 = (bf16[32,3584]{1,0:T(8,128)(2,1)S(1)}, bf16[32,3584]{1,0:T(8,128)(2,1)S(1)}, u32[]{:S(2)}, u32[]{:S(2)}) collective-permute-start(bf16[32,3584]{1,0:T(8,128)(2,1)S(1)} %pad_maximum_fusion.3), channel_id=1, source_target_pairs={{0,6},{1,4},{2,7},{3,5},{4,1},{5,3},{6,0},{7,2},{8,13},{9,15},{10,... | collective-permute-start | bytes 688136 | tf_op jit(solution)/shard_map/ppermute | solution.py:40
  25.4 2.0 %collective-permute-done.8 = bf16[32,3584]{1,0:T(8,128)(2,1)S(1)} collective-permute-done((bf16[32,3584]{1,0:T(8,128)(2,1)S(1)}, bf16[32,3584]{1,0:T(8,128)(2,1)S(1)}, u32[]{:S(2)}, u32[]{:S(2)}) %collective-permute-start.8) | collective-permute-done | bytes 229408 | tf_op jit(solution)/shard_map/ppermute | solution.py:40
  29.4 1.7 %collective-permute-start.12 = (bf16[32,3584]{1,0:T(8,128)(2,1)S(1)}, bf16[32,3584]{1,0:T(8,128)(2,1)S(1)}, u32[]{:S(2)}, u32[]{:S(2)}) collective-permute-start(bf16[32,3584]{1,0:T(8,128)(2,1)S(1)} %fusion.3), channel_id=1, source_target_pairs={{0,6},{1,4},{2,7},{3,5},{4,1},{5,3},{6,0},{7,2},{8,13},{9,15},{10,... | collective-permute-start | bytes 688136 | tf_op jit(solution)/shard_map/ppermute | solution.py:40
  33.5 1.5 %collective-permute-done.12 = bf16[32,3584]{1,0:T(8,128)(2,1)S(1)} collective-permute-done((bf16[32,3584]{1,0:T(8,128)(2,1)S(1)}, bf16[32,3584]{1,0:T(8,128)(2,1)S(1)}, u32[]{:S(2)}, u32[]{:S(2)}) %collective-permute-start.12) | collective-permute-done | bytes 229408 | tf_op jit(solution)/shard_map/ppermute | solution.py:40
  35.3 2.0 %collective-permute-start.13 = (bf16[16,3584]{1,0:T(8,128)(2,1)S(1)}, bf16[16,3584]{1,0:T(8,128)(2,1)S(1)}, u32[]{:S(2)}, u32[]{:S(2)}) collective-permute-start(bf16[16,3584]{1,0:T(8,128)(2,1)S(1)} %slice.147), channel_id=1, source_target_pairs={{0,5},{1,7},{2,4},{3,6},{4,2},{5,0},{6,3},{7,1},{8,14},{9,12},{10,... | collective-permute-start | bytes 344072 | tf_op jit(solution)/shard_map/ppermute | solution.py:40
  37.9 1.6 %collective-permute-start.19 = (bf16[16,3584]{1,0:T(8,128)(2,1)S(1)}, bf16[16,3584]{1,0:T(8,128)(2,1)S(1)}, u32[]{:S(2)}, u32[]{:S(2)}) collective-permute-start(bf16[16,3584]{1,0:T(8,128)(2,1)S(1)} %slice.146), channel_id=1, source_target_pairs={{0,5},{1,7},{2,4},{3,6},{4,2},{5,0},{6,3},{7,1},{8,14},{9,12},{10,... | collective-permute-start | bytes 344072 | tf_op jit(solution)/shard_map/ppermute | solution.py:40
  39.8 1.8 %collective-permute-start.14 = (bf16[16,3584]{1,0:T(8,128)(2,1)S(1)}, bf16[16,3584]{1,0:T(8,128)(2,1)S(1)}, u32[]{:S(2)}, u32[]{:S(2)}) collective-permute-start(bf16[16,3584]{1,0:T(8,128)(2,1)S(1)} %get-tuple-element.76), channel_id=1, source_target_pairs={{0,12},{1,21},{2,22},{3,15},{4,16},{5,9},{6,10},{7,19},{8,28},{9,5... | collective-permute-start | bytes 344072 | tf_op jit(solution)/shard_map/ppermute | solution.py:40
  42.2 1.6 %collective-permute-start.20 = (bf16[16,3584]{1,0:T(8,128)(2,1)S(1)}, bf16[16,3584]{1,0:T(8,128)(2,1)S(1)}, u32[]{:S(2)}, u32[]{:S(2)}) collective-permute-start(bf16[16,3584]{1,0:T(8,128)(2,1)S(1)} %get-tuple-element.74), channel_id=1, source_target_pairs={{0,12},{1,21},{2,22},{3,15},{4,16},{5,9},{6,10},{7,19},{8,28},{9,5... | collective-permute-start | bytes 344072 | tf_op jit(solution)/shard_map/ppermute | solution.py:40
  44.9 3.6 %collective-permute-start.15 = (bf16[16,3584]{1,0:T(8,128)(2,1)S(1)}, bf16[16,3584]{1,0:T(8,128)(2,1)S(1)}, u32[]{:S(2)}, u32[]{:S(2)}) collective-permute-start(bf16[16,3584]{1,0:T(8,128)(2,1)S(1)} %fusion.32), channel_id=1, source_target_pairs={{0,20},{1,13},{2,14},{3,23},{4,8},{5,17},{6,18},{7,11},{8,4},{9,29... | collective-permute-start | bytes 344072 | tf_op jit(solution)/shard_map/ppermute | solution.py:40
  48.5 2.1 %collective-permute-start.21 = (bf16[16,3584]{1,0:T(8,128)(2,1)S(1)}, bf16[16,3584]{1,0:T(8,128)(2,1)S(1)}, u32[]{:S(2)}, u32[]{:S(2)}) collective-permute-start(bf16[16,3584]{1,0:T(8,128)(2,1)S(1)} %fusion.33), channel_id=1, source_target_pairs={{0,20},{1,13},{2,14},{3,23},{4,8},{5,17},{6,18},{7,11},{8,4},{9,29... | collective-permute-start | bytes 344072 | tf_op jit(solution)/shard_map/ppermute | solution.py:40
  50.6 2.2 %collective-permute-done.15 = bf16[16,3584]{1,0:T(8,128)(2,1)S(1)} collective-permute-done((bf16[16,3584]{1,0:T(8,128)(2,1)S(1)}, bf16[16,3584]{1,0:T(8,128)(2,1)S(1)}, u32[]{:S(2)}, u32[]{:S(2)}) %collective-permute-start.15) | collective-permute-done | bytes 114720 | tf_op jit(solution)/shard_map/ppermute | solution.py:40
  59.6 1.7 %collective-permute-start.23 = (bf16[32,3584]{1,0:T(8,128)(2,1)S(1)}, bf16[32,3584]{1,0:T(8,128)(2,1)S(1)}, u32[]{:S(2)}, u32[]{:S(2)}) collective-permute-start(bf16[32,3584]{1,0:T(8,128)(2,1)S(1)} %pad_maximum_fusion.6), channel_id=1, source_target_pairs={{0,6},{1,4},{2,7},{3,5},{4,1},{5,3},{6,0},{7,2},{8,13},{9,15},{10,... | collective-permute-start | bytes 688136 | tf_op jit(solution)/shard_map/ppermute | solution.py:40
  69.2 1.9 %collective-permute-start.25 = (f32[1,1792]{1,0:T(1,128)S(1)}, f32[1,1792]{1,0:T(1,128)S(1)}, u32[]{:S(2)}, u32[]{:S(2)}) collective-permute-start(f32[1,1792]{1,0:T(1,128)S(1)} %broadcast_select_fusion.8), channel_id=1, source_target_pairs={{0,20},{1,21},{2,22},{3,23},{4,16},{5,17},{6,18},{7,19},{8,28},{9,... | collective-permute-start | bytes 21512 | tf_op jit(solution)/shard_map/ppermute | solution.py:40
  71.2 2.1 %collective-permute-done.25 = f32[1,1792]{1,0:T(1,128)S(1)} collective-permute-done((f32[1,1792]{1,0:T(1,128)S(1)}, f32[1,1792]{1,0:T(1,128)S(1)}, u32[]{:S(2)}, u32[]{:S(2)}) %collective-permute-start.25) | collective-permute-done | bytes 7200 | tf_op jit(solution)/shard_map/ppermute | solution.py:40
  73.5 2.0 %collective-permute-start.28 = (f32[1,896]{1,0:T(1,128)S(1)}, f32[1,896]{1,0:T(1,128)S(1)}, u32[]{:S(2)}, u32[]{:S(2)}) collective-permute-start(f32[1,896]{1,0:T(1,128)S(1)} %broadcast_select_fusion.10), channel_id=1, source_target_pairs={{0,12},{1,13},{2,14},{3,15},{4,8},{5,9},{6,10},{7,11},{8,4},{9,5},... | collective-permute-start | bytes 10760 | tf_op jit(solution)/shard_map/ppermute | solution.py:40
  75.5 1.5 %fusion = bf16[168,3584]{1,0:T(8,128)(2,1)} fusion(bf16[256,168]{1,0:T(8,128)(2,1)S(1)} %constant_dynamic-update-slice_fusion, bf16[256,3584]{1,0:T(8,128)(2,1)S(1)} %constant_dynamic-update-slice_fusion.5, bf16[168,3584]{1,0:T(8,128)(2,1)S(1)} %copy-done, f32[168]{0:T(256)S(1)} %rsqrt_multiply_fusion), kind=kOutput, calls=%fused_computation.1 | convolution fusion | flops 310689792 | bytes 4330144 | tf_op jit(solution)/shard_map/dot_general | solution.py:160
  77.2 1.7 %collective-permute-start.31 = (f32[2,224]{1,0:T(2,128)S(1)}, f32[2,224]{1,0:T(2,128)S(1)}, u32[]{:S(2)}, u32[]{:S(2)}) collective-permute-start(f32[2,224]{1,0:T(2,128)S(1)} %broadcast_select_fusion.12), channel_id=1, source_target_pairs={{0,6},{1,7},{2,4},{3,5},{4,2},{5,3},{6,0},{7,1},{8,14},{9,15},{10,... | collective-permute-start | bytes 5384 | tf_op jit(solution)/shard_map/ppermute | solution.py:40
  79.0 1.5 %convolution_convert_fusion = bf16[168,3584]{1,0:T(8,128)(2,1)} fusion(bf16[256,168]{1,0:T(8,128)(2,1)S(1)} %constant_dynamic-update-slice_fusion.10, bf16[256,3584]{1,0:T(8,128)(2,1)S(1)} %constant_dynamic-update-slice_fusion.15), kind=kOutput, calls=%fused_computation.2 | convolution fusion | flops 308883456 | bytes 3125248 | tf_op jit(solution)/shard_map/dot_general | solution.py:160
  80.7 1.6 %collective-permute-start.32 = (f32[2,112]{1,0:T(2,128)S(1)}, f32[2,112]{1,0:T(2,128)S(1)}, u32[]{:S(2)}, u32[]{:S(2)}) collective-permute-start(f32[2,112]{1,0:T(2,128)S(1)} %broadcast_select_fusion.13), channel_id=1, source_target_pairs={{0,5},{1,4},{2,7},{3,6},{4,1},{5,0},{6,3},{7,2},{8,13},{9,12},{10,... | collective-permute-start | bytes 2696 | tf_op jit(solution)/shard_map/ppermute | solution.py:40
  (144 shorter events, 36.2 us)
Async XLA Ops:
  1.2 27.3 %collective-permute-start.10 = (f32[168]{0:T(256)}, f32[168]{0:T(256)S(1)}, u32[]{:S(2)}, u32[]{:S(2)}) collective-permute-start(f32[168]{0:T(256)} %param.7), channel_id=1, source_target_pairs={{0,4},{1,5},{2,6},{3,7},{4,0},{5,1},{6,2},{7,3},{8,12},{9,13},{10,... | collective-permute-start | bytes 2024 | tf_op jit(solution)/shard_map/ppermute | solution.py:36
  1.7 26.9 %collective-permute-start.9 = (bf16[168,3584]{1,0:T(8,128)(2,1)}, bf16[168,3584]{1,0:T(8,128)(2,1)S(1)}, u32[]{:S(2)}, u32[]{:S(2)}) collective-permute-start(bf16[168,3584]{1,0:T(8,128)(2,1)} %param.6), channel_id=1, source_target_pairs={{0,4},{1,5},{2,6},{3,7},{4,0},{5,1},{6,2},{7,3},{8,12},{9,13},{10,... | collective-permute-start | bytes 3612680 | tf_op jit(solution)/shard_map/ppermute | solution.py:36
  1.7 27.3 %collective-permute-start.11 = (bf16[168,3584]{1,0:T(8,128)(2,1)}, bf16[168,3584]{1,0:T(8,128)(2,1)S(1)}, u32[]{:S(2)}, u32[]{:S(2)}) collective-permute-start(bf16[168,3584]{1,0:T(8,128)(2,1)} %param.8), channel_id=1, source_target_pairs={{0,4},{1,5},{2,6},{3,7},{4,0},{5,1},{6,2},{7,3},{8,12},{9,13},{10,... | collective-permute-start | bytes 3612680 | tf_op jit(solution)/shard_map/ppermute | solution.py:36
  4.1 6.9 %collective-permute-start.2 = (bf16[32,896]{1,0:T(8,128)(2,1)S(1)}, bf16[32,896]{1,0:T(8,128)(2,1)S(1)}, u32[]{:S(2)}, u32[]{:S(2)}) collective-permute-start(bf16[32,896]{1,0:T(8,128)(2,1)S(1)} %get-tuple-element.78), channel_id=1, source_target_pairs={{0,20},{1,21},{2,22},{3,23},{4,16},{5,17},{6,18},{7,19},{8,28},{9,... | collective-permute-start | bytes 172040 | tf_op jit(solution)/shard_map/ppermute | solution.py:40
  15.1 4.3 %collective-permute-start.5 = (bf16[16,3584]{1,0:T(8,128)(2,1)S(1)}, bf16[16,3584]{1,0:T(8,128)(2,1)S(1)}, u32[]{:S(2)}, u32[]{:S(2)}) collective-permute-start(bf16[16,3584]{1,0:T(8,128)(2,1)S(1)} %get-tuple-element.85), channel_id=1, source_target_pairs={{0,5},{1,7},{2,4},{3,6},{4,2},{5,0},{6,3},{7,1},{8,14},{9,12},{10,... | collective-permute-start | bytes 344072 | tf_op jit(solution)/shard_map/ppermute | solution.py:40
  16.6 4.6 %collective-permute-start.7 = (bf16[16,3584]{1,0:T(8,128)(2,1)S(1)}, bf16[16,3584]{1,0:T(8,128)(2,1)S(1)}, u32[]{:S(2)}, u32[]{:S(2)}) collective-permute-start(bf16[16,3584]{1,0:T(8,128)(2,1)S(1)} %get-tuple-element.84), channel_id=1, source_target_pairs={{0,5},{1,7},{2,4},{3,6},{4,2},{5,0},{6,3},{7,1},{8,14},{9,12},{10,... | collective-permute-start | bytes 344072 | tf_op jit(solution)/shard_map/ppermute | solution.py:40
  19.4 5.5 %collective-permute-start.6 = (bf16[32,3584]{1,0:T(8,128)(2,1)S(1)}, bf16[32,3584]{1,0:T(8,128)(2,1)S(1)}, u32[]{:S(2)}, u32[]{:S(2)}) collective-permute-start(bf16[32,3584]{1,0:T(8,128)(2,1)S(1)} %pad_maximum_fusion.3), channel_id=1, source_target_pairs={{0,6},{1,4},{2,7},{3,5},{4,1},{5,3},{6,0},{7,2},{8,13},{9,15},{10,... | collective-permute-start | bytes 688136 | tf_op jit(solution)/shard_map/ppermute | solution.py:40
  21.2 6.2 %collective-permute-start.8 = (bf16[32,3584]{1,0:T(8,128)(2,1)S(1)}, bf16[32,3584]{1,0:T(8,128)(2,1)S(1)}, u32[]{:S(2)}, u32[]{:S(2)}) collective-permute-start(bf16[32,3584]{1,0:T(8,128)(2,1)S(1)} %pad_maximum_fusion.4), channel_id=1, source_target_pairs={{0,6},{1,4},{2,7},{3,5},{4,1},{5,3},{6,0},{7,2},{8,13},{9,15},{10,... | collective-permute-start | bytes 688136 | tf_op jit(solution)/shard_map/ppermute | solution.py:40
  29.4 5.5 %collective-permute-start.12 = (bf16[32,3584]{1,0:T(8,128)(2,1)S(1)}, bf16[32,3584]{1,0:T(8,128)(2,1)S(1)}, u32[]{:S(2)}, u32[]{:S(2)}) collective-permute-start(bf16[32,3584]{1,0:T(8,128)(2,1)S(1)} %fusion.3), channel_id=1, source_target_pairs={{0,6},{1,4},{2,7},{3,5},{4,1},{5,3},{6,0},{7,2},{8,13},{9,15},{10,... | collective-permute-start | bytes 688136 | tf_op jit(solution)/shard_map/ppermute | solution.py:40
  32.0 5.5 %collective-permute-start.18 = (bf16[32,3584]{1,0:T(8,128)(2,1)S(1)}, bf16[32,3584]{1,0:T(8,128)(2,1)S(1)}, u32[]{:S(2)}, u32[]{:S(2)}) collective-permute-start(bf16[32,3584]{1,0:T(8,128)(2,1)S(1)} %fusion.4), channel_id=1, source_target_pairs={{0,6},{1,4},{2,7},{3,5},{4,1},{5,3},{6,0},{7,2},{8,13},{9,15},{10,... | collective-permute-start | bytes 688136 | tf_op jit(solution)/shard_map/ppermute | solution.py:40
  35.3 4.5 %collective-permute-start.13 = (bf16[16,3584]{1,0:T(8,128)(2,1)S(1)}, bf16[16,3584]{1,0:T(8,128)(2,1)S(1)}, u32[]{:S(2)}, u32[]{:S(2)}) collective-permute-start(bf16[16,3584]{1,0:T(8,128)(2,1)S(1)} %slice.147), channel_id=1, source_target_pairs={{0,5},{1,7},{2,4},{3,6},{4,2},{5,0},{6,3},{7,1},{8,14},{9,12},{10,... | collective-permute-start | bytes 344072 | tf_op jit(solution)/shard_map/ppermute | solution.py:40
  37.9 4.3 %collective-permute-start.19 = (bf16[16,3584]{1,0:T(8,128)(2,1)S(1)}, bf16[16,3584]{1,0:T(8,128)(2,1)S(1)}, u32[]{:S(2)}, u32[]{:S(2)}) collective-permute-start(bf16[16,3584]{1,0:T(8,128)(2,1)S(1)} %slice.146), channel_id=1, source_target_pairs={{0,5},{1,7},{2,4},{3,6},{4,2},{5,0},{6,3},{7,1},{8,14},{9,12},{10,... | collective-permute-start | bytes 344072 | tf_op jit(solution)/shard_map/ppermute | solution.py:40
  39.8 5.0 %collective-permute-start.14 = (bf16[16,3584]{1,0:T(8,128)(2,1)S(1)}, bf16[16,3584]{1,0:T(8,128)(2,1)S(1)}, u32[]{:S(2)}, u32[]{:S(2)}) collective-permute-start(bf16[16,3584]{1,0:T(8,128)(2,1)S(1)} %get-tuple-element.76), channel_id=1, source_target_pairs={{0,12},{1,21},{2,22},{3,15},{4,16},{5,9},{6,10},{7,19},{8,28},{9,5... | collective-permute-start | bytes 344072 | tf_op jit(solution)/shard_map/ppermute | solution.py:40
  42.2 6.3 %collective-permute-start.20 = (bf16[16,3584]{1,0:T(8,128)(2,1)S(1)}, bf16[16,3584]{1,0:T(8,128)(2,1)S(1)}, u32[]{:S(2)}, u32[]{:S(2)}) collective-permute-start(bf16[16,3584]{1,0:T(8,128)(2,1)S(1)} %get-tuple-element.74), channel_id=1, source_target_pairs={{0,12},{1,21},{2,22},{3,15},{4,16},{5,9},{6,10},{7,19},{8,28},{9,5... | collective-permute-start | bytes 344072 | tf_op jit(solution)/shard_map/ppermute | solution.py:40
  44.9 7.9 %collective-permute-start.15 = (bf16[16,3584]{1,0:T(8,128)(2,1)S(1)}, bf16[16,3584]{1,0:T(8,128)(2,1)S(1)}, u32[]{:S(2)}, u32[]{:S(2)}) collective-permute-start(bf16[16,3584]{1,0:T(8,128)(2,1)S(1)} %fusion.32), channel_id=1, source_target_pairs={{0,20},{1,13},{2,14},{3,23},{4,8},{5,17},{6,18},{7,11},{8,4},{9,29... | collective-permute-start | bytes 344072 | tf_op jit(solution)/shard_map/ppermute | solution.py:40
  48.5 6.7 %collective-permute-start.21 = (bf16[16,3584]{1,0:T(8,128)(2,1)S(1)}, bf16[16,3584]{1,0:T(8,128)(2,1)S(1)}, u32[]{:S(2)}, u32[]{:S(2)}) collective-permute-start(bf16[16,3584]{1,0:T(8,128)(2,1)S(1)} %fusion.33), channel_id=1, source_target_pairs={{0,20},{1,13},{2,14},{3,23},{4,8},{5,17},{6,18},{7,11},{8,4},{9,29... | collective-permute-start | bytes 344072 | tf_op jit(solution)/shard_map/ppermute | solution.py:40
  52.9 4.3 %collective-permute-start.16 = (bf16[16,3584]{1,0:T(8,128)(2,1)S(1)}, bf16[16,3584]{1,0:T(8,128)(2,1)S(1)}, u32[]{:S(2)}, u32[]{:S(2)}) collective-permute-start(bf16[16,3584]{1,0:T(8,128)(2,1)S(1)} %get-tuple-element.83), channel_id=1, source_target_pairs={{0,5},{1,7},{2,4},{3,6},{4,2},{5,0},{6,3},{7,1},{8,14},{9,12},{10,... | collective-permute-start | bytes 344072 | tf_op jit(solution)/shard_map/ppermute | solution.py:40
  55.3 4.3 %collective-permute-start.22 = (bf16[16,3584]{1,0:T(8,128)(2,1)S(1)}, bf16[16,3584]{1,0:T(8,128)(2,1)S(1)}, u32[]{:S(2)}, u32[]{:S(2)}) collective-permute-start(bf16[16,3584]{1,0:T(8,128)(2,1)S(1)} %get-tuple-element.81), channel_id=1, source_target_pairs={{0,5},{1,7},{2,4},{3,6},{4,2},{5,0},{6,3},{7,1},{8,14},{9,12},{10,... | collective-permute-start | bytes 344072 | tf_op jit(solution)/shard_map/ppermute | solution.py:40
  57.2 6.1 %collective-permute-start.17 = (bf16[32,3584]{1,0:T(8,128)(2,1)S(1)}, bf16[32,3584]{1,0:T(8,128)(2,1)S(1)}, u32[]{:S(2)}, u32[]{:S(2)}) collective-permute-start(bf16[32,3584]{1,0:T(8,128)(2,1)S(1)} %pad_maximum_fusion.5), channel_id=1, source_target_pairs={{0,6},{1,4},{2,7},{3,5},{4,1},{5,3},{6,0},{7,2},{8,13},{9,15},{10,... | collective-permute-start | bytes 688136 | tf_op jit(solution)/shard_map/ppermute | solution.py:40
  59.6 5.5 %collective-permute-start.23 = (bf16[32,3584]{1,0:T(8,128)(2,1)S(1)}, bf16[32,3584]{1,0:T(8,128)(2,1)S(1)}, u32[]{:S(2)}, u32[]{:S(2)}) collective-permute-start(bf16[32,3584]{1,0:T(8,128)(2,1)S(1)} %pad_maximum_fusion.6), channel_id=1, source_target_pairs={{0,6},{1,4},{2,7},{3,5},{4,1},{5,3},{6,0},{7,2},{8,13},{9,15},{10,... | collective-permute-start | bytes 688136 | tf_op jit(solution)/shard_map/ppermute | solution.py:40
  67.6 5.7 %collective-permute-start.26 = (bf16[128,168]{1,0:T(8,128)(2,1)S(1)}, bf16[128,168]{1,0:T(8,128)(2,1)S(1)}, u32[]{:S(2)}, u32[]{:S(2)}) collective-permute-start(bf16[128,168]{1,0:T(8,128)(2,1)S(1)} %pad_maximum_fusion.7), channel_id=1, source_target_pairs={{0,4},{1,5},{2,6},{3,7},{4,0},{5,1},{6,2},{7,3},{8,12},{9,13},{10,... | collective-permute-start | bytes 129032 | tf_op jit(solution)/shard_map/ppermute | solution.py:36
  68.3 5.1 %collective-permute-start.27 = (bf16[128,3584]{1,0:T(8,128)(2,1)S(1)}, bf16[128,3584]{1,0:T(8,128)(2,1)S(1)}, u32[]{:S(2)}, u32[]{:S(2)}) collective-permute-start(bf16[128,3584]{1,0:T(8,128)(2,1)S(1)} %pad_maximum_fusion), channel_id=1, source_target_pairs={{0,4},{1,5},{2,6},{3,7},{4,0},{5,1},{6,2},{7,3},{8,12},{9,13},{10,... | collective-permute-start | bytes 2752520 | tf_op jit(solution)/shard_map/ppermute | solution.py:36
  68.5 4.8 %collective-permute-start.29 = (bf16[128,168]{1,0:T(8,128)(2,1)S(1)}, bf16[128,168]{1,0:T(8,128)(2,1)S(1)}, u32[]{:S(2)}, u32[]{:S(2)}) collective-permute-start(bf16[128,168]{1,0:T(8,128)(2,1)S(1)} %pad_maximum_fusion.8), channel_id=1, source_target_pairs={{0,4},{1,5},{2,6},{3,7},{4,0},{5,1},{6,2},{7,3},{8,12},{9,13},{10,... | collective-permute-start | bytes 129032 | tf_op jit(solution)/shard_map/ppermute | solution.py:36
  69.0 6.4 %collective-permute-start.30 = (bf16[128,3584]{1,0:T(8,128)(2,1)S(1)}, bf16[128,3584]{1,0:T(8,128)(2,1)S(1)}, u32[]{:S(2)}, u32[]{:S(2)}) collective-permute-start(bf16[128,3584]{1,0:T(8,128)(2,1)S(1)} %pad_maximum_fusion.1), channel_id=1, source_target_pairs={{0,4},{1,5},{2,6},{3,7},{4,0},{5,1},{6,2},{7,3},{8,12},{9,13},{10,... | collective-permute-start | bytes 2752520 | tf_op jit(solution)/shard_map/ppermute | solution.py:36
  (12 other events, 47.0 us)

commit v3 on v2

v3 whole, which is shorter than its diff:
```python
import jax
import jax.numpy as jnp
from jax import lax
from jax.sharding import PartitionSpec as P

sparsity_weight = 1.0
AXES = ("lat", "row")
CHUNKS = 2
f32 = jnp.float32
bf16 = jnp.bfloat16


def bits_below(n):
    return [1 << k for k in range(n.bit_length() - 1)]


class Grid:
    def __init__(self, mesh):
        self.lats, self.rows = mesh.shape["lat"], mesh.shape["row"]
        self.size = self.lats * self.rows
        self.core = self.rows
        self.row_bits = bits_below(self.rows)
        self.chip_bits = [2 * self.rows * b for b in bits_below(self.lats // 2)]
        self.chips = self.lats // 2

    def stream_of(self, i):
        parity = (i // self.core) % 2
        for b in self.row_bits + self.chip_bits:
            parity = parity ^ ((i // b) % 2)
        return parity

    def orders(self, bits):
        return list(zip(bits, bits[::-1]))

    def swap_core(self, v):
        return lax.ppermute(v, AXES, [(i, i ^ self.core) for i in range(self.size)])

    def step(self, v, pair):
        target = [i ^ self.core ^ pair[self.stream_of(i)] for i in range(self.size)]
        return lax.ppermute(v, AXES, list(enumerate(target)))


def dot_rows(v, w):
    return lax.dot_general(v, w, (((1,), (1,)), ((), ())), preferred_element_type=f32)


def over_rows(u, v):
    return lax.dot_general(u, v, (((0,), (0,)), ((), ())), preferred_element_type=f32)


def on_device(grid, inputs, encoder, latent_bias, decoder, center_bias):
    me = lax.axis_index("lat") * grid.rows + lax.axis_index("row")
    core = (me // grid.core) % 2
    stream = grid.stream_of(me)
    chip = me // (2 * grid.core)
    width = encoder.shape[1]
    half, block = inputs.shape[0] // 2, 2 * inputs.shape[1]
    part = half // CHUNKS
    row_steps, chip_steps = grid.orders(grid.row_bits), grid.orders(grid.chip_bits)

    theirs = grid.swap_core(inputs).astype(f32) - grid.swap_core(center_bias)
    mine = inputs.astype(f32) - center_bias
    shifted = jnp.where(
        core == 0,
        jnp.concatenate([mine, theirs], axis=1),
        jnp.concatenate([theirs, mine], axis=1),
    )
    shifted = jnp.where(stream == 0, shifted[:half], shifted[half:])

    held, masks = [shifted.astype(bf16)], [0]
    for b, mask in list(zip(grid.chip_bits, bits_below(grid.chips)))[::-1]:
        held = held + [grid.step(u, (b, b)) for u in held]
        masks = masks + [m ^ mask for m in masks]
        if b == grid.chip_bits[-1]:
            held[-1], encoder, decoder, latent_bias = lax.optimization_barrier(
                (held[-1], encoder, decoder, latent_bias)
            )
    held = [u for _, u in sorted(zip(masks, held), key=lambda t: t[0])]
    for mask in bits_below(grid.chips):
        flip = (chip // mask) % 2 == 1
        held = [jnp.where(flip, held[k ^ mask], held[k]) for k in range(len(held))]
    blocks = jnp.concatenate(held, axis=1)

    encoders = [encoder, grid.swap_core(encoder)]
    decoders = [decoder, grid.swap_core(decoder)]
    biases = [latent_bias, grid.swap_core(latent_bias)]

    def gather_rows(v):
        for pair in row_steps[:-1]:
            v = jnp.concatenate([v, grid.step(v, pair)], axis=0)
        return v, grid.step(v, row_steps[-1])

    parts = [slice(k * part, (k + 1) * part) for k in range(CHUNKS)]
    centered = [gather_rows(blocks[rows]) for rows in parts]

    latents, sigs, keeps, sends = [], [], [], []

    def forward(x):
        scaled = [4.0 * (dot_rows(x, e) + b) for e, b in zip(encoders, biases)]
        sigs.append([jax.nn.sigmoid(v) for v in scaled])
        latents.append([(jax.nn.softplus(v) / 4.0).astype(bf16) for v in scaled])
        return sum(jnp.dot(l, d, preferred_element_type=f32) for l, d in zip(latents[-1], decoders))

    for near, far in centered:
        if sends:
            sends[-1], far = lax.optimization_barrier((sends[-1], far))
        keeps.append(forward(near))
        sends.append(forward(far).astype(bf16))
    norms = [jnp.sqrt(jnp.sum(jnp.square(d.astype(f32)), axis=1) + 1e-06) for d in decoders]

    def placed(rows):
        zeros = jnp.zeros((part, block), f32)
        return jnp.concatenate(
            [jnp.where(chip == p, shifted[rows], zeros) for p in range(grid.chips)], axis=1
        )

    for i in range(len(row_steps))[::-1]:
        received = [grid.step(v, row_steps[i]) for v in sends]
        for k in range(CHUNKS):
            v = keeps[k] + received[k].astype(f32)
            n = v.shape[0] // 2
            if i > 0:
                keeps[k], sends[k] = v[:n], v[n:].astype(bf16)
            else:
                keeps[k] = v - placed(parts[k])
                sends[k] = keeps[k].astype(bf16)
    for pair in chip_steps:
        received = [grid.step(v, pair) for v in sends]
        for k in range(CHUNKS):
            keeps[k] = keeps[k] + received[k].astype(f32)
            sends[k] = keeps[k].astype(bf16)
    columns = sum(jnp.sum(v, axis=0, keepdims=True) for v in keeps)
    errors = [e for halves in [gather_rows(v) for v in sends] for e in halves]
    centered = [c for halves in centered for c in halves]

    pres = []
    for err, sig in zip(errors, sigs):
        grads = [dot_rows(err, d) + sparsity_weight * n for d, n in zip(decoders, norms)]
        pres.append([(g * v).astype(bf16) for g, v in zip(grads, sig)])
    centered, latents, errors, pres, columns = lax.optimization_barrier(
        (centered, latents, errors, pres, columns)
    )

    terms = (1.0 / grid.chips) * columns
    for side, enc in enumerate(encoders):
        bias = sum(jnp.sum(p[side].astype(f32), axis=0, keepdims=True) for p in pres)
        digits = []
        for _ in range(3):
            digits.append(lax.reduce_precision(bias, 8, 7))
            bias = bias - digits[-1]
        digits = jnp.concatenate(digits, axis=0).astype(bf16)
        products = jnp.dot(digits, enc, preferred_element_type=f32)
        terms = terms - jnp.sum(products, axis=0, keepdims=True)
    left = terms + grid.swap_core(terms)

    def halve(left, b):
        n = left.shape[1] // 2
        upper = (me // b) % 2 == 1
        kept = jnp.where(upper, left[:, n:], left[:, :n])
        sent = jnp.where(upper, left[:, :n], left[:, n:])
        return kept + grid.step(sent, (b, b))

    def all_rows(mine, theirs):
        return jnp.concatenate([*mine, grid.swap_core(jnp.concatenate(theirs, axis=0))], axis=0)

    pres = all_rows([p[0] for p in pres], [p[1] for p in pres])
    errors = all_rows(errors, errors)
    left, latents, centered = lax.optimization_barrier((left, latents, centered))
    latents = all_rows([l[0] for l in latents], [l[1] for l in latents])
    centered = all_rows(centered, centered)

    for k, b in enumerate((grid.row_bits + grid.chip_bits)[::-1]):
        if k == len(grid.chip_bits):
            left = left.reshape(2, width // grid.chips // 2)
        if k == 2:
            left, decoder_grad = lax.optimization_barrier((left, decoder_grad))
        if k == 3:
            left, encoder_grad = lax.optimization_barrier((left, encoder_grad))
        left = halve(left, b)
        if k == 0:
            left, latents, errors = lax.optimization_barrier((left, latents, errors))
            latent_total = jnp.sum(latents.astype(f32), axis=0)
            scale = (sparsity_weight * latent_total / norms[0])[:, None]
            decoder_grad = over_rows(latents, errors) + scale * decoder.astype(f32)
            decoder_grad = decoder_grad.astype(bf16)
        if k == 1:
            left, pres, centered = lax.optimization_barrier((left, pres, centered))
            bias_grad = jnp.sum(pres.astype(f32), axis=0)
            encoder_grad = over_rows(pres, centered).astype(bf16)
    center_grad = jnp.where(core == 0, left[0], left[1])
    return (encoder_grad, decoder_grad, bias_grad, center_grad)


def solution(mesh):
    grid = Grid(mesh)
    in_specs = (P("row", "lat"), P(AXES, None), P(AXES), P(AXES, None), P("lat"))
    out_specs = (P(AXES, None), P(AXES, None), P(AXES), P(AXES))

    def device_function(*args):
        return on_device(grid, *args)

    return jax.shard_map(
        device_function, mesh=mesh, in_specs=in_specs, out_specs=out_specs, check_vma=False
    )
```

time: 84.5 us -> 80.3 us (0.950)
  waiting for transfers between devices: 21.1 us -> 17.2 us
  starting transfers between devices: 40.7 us -> 43.2 us
  other arithmetic: 6.09 us -> 3.97 us
    ppermute x23, waiting for transfers between devices: 21.1 us -> 16.6 us  [step(): return lax.ppermute(v, AXES, list(enumerate(target)))]
    ppermute x23, starting transfers between devices: 37.8 us -> 40.1 us  [step(): return lax.ppermute(v, AXES, list(enumerate(target)))]
    select_n x4 -> x3, other arithmetic: 1.93 us -> 0.21 us  [the longest x1 0.14 us: on_device(): jnp.where(core == 0, jnp.concatenate([mine, theirs], axis=1), jnp.concate...]
    reduce_sum x2, other arithmetic: 1.92 us -> 0.65 us  [on_device(): jnp.sum(jnp.square(d.astype(f32)), axis=1) + 1e-06]
    sub x0 -> x3, other arithmetic: none -> 0.89 us  [the longest x1 0.85 us: on_device(): mine = inputs.astype(f32) - center_bias]
  transfers between devices with their start and end apart: 33 -> 33, of which waited for: 17 -> 19; matrix products, arithmetic and copies ran while one was open for 21% -> 19% of each run, Pallas kernels for 0% -> 0%
where the time goes in v3:
time: 80.3 us; the launch traced here: 80.2 us
  starting transfers between devices  43.2 us (54%)
  waiting for transfers between devices  17.2 us (21%)
  matrix products  14.1 us (18%)
  other arithmetic  3.97 us (5%)
  between operations  1.32 us (2%)
    ppermute x23, starting transfers between devices, step(): return lax.ppermute(v, AXES, list(enumerate(target)))  40.1 us
    ppermute x23, waiting for transfers between devices, step(): return lax.ppermute(v, AXES, list(enumerate(target)))  16.6 us
    dot_general x16, matrix products, dot_rows(): lax.dot_general(v, w, (((1,), (1,)), ((), ())), preferred_element_type=f32)  7.7 us
    ppermute x10, starting transfers between devices, swap_core(): return lax.ppermute(v, AXES, [(i, i ^ self.core) for i in range(self.size)])  3.09 us
    dot_general x2, matrix products, over_rows(): lax.dot_general(u, v, (((0,), (0,)), ((), ())), preferred_element_type=f32)  3.05 us
    dot_general x8, matrix products, forward(): jnp.dot(l, d, preferred_element_type=f32)  2.77 us
  transfers between devices with their start and end apart: 33, of which 19 were waited for; matrix products, arithmetic and copies ran while one was open for 19% of the time, Pallas kernels for 0%

profile of v3, /device:TPU:0, one launch (start us, length us, event | category | flops | bytes accessed | tf_op | source)
XLA Modules:
  0.0 80.2 jit_solution(4310285151647128729)
XLA Ops:
  2.7 3.8 %collective-permute-start.2 = (bf16[32,896]{1,0:T(8,128)(2,1)S(1)}, bf16[32,896]{1,0:T(8,128)(2,1)S(1)}, u32[]{:S(2)}, u32[]{:S(2)}) collective-permute-start(bf16[32,896]{1,0:T(8,128)(2,1)S(1)} %get-tuple-element.116), channel_id=1, source_target_pairs={{0,20},{1,21},{2,22},{3,23},{4,16},{5,17},{6,18},{7,19},{8,28},{9,... | collective-permute-start | bytes 172040 | tf_op jit(solution)/shard_map/ppermute | solution.py:40
  6.5 1.4 %collective-permute-start.4 = (bf16[32,896]{1,0:T(8,128)(2,1)S(1)}, bf16[32,896]{1,0:T(8,128)(2,1)S(1)}, u32[]{:S(2)}, u32[]{:S(2)}) collective-permute-start(bf16[32,896]{1,0:T(8,128)(2,1)S(1)} %get-tuple-element.116), channel_id=1, source_target_pairs={{0,12},{1,13},{2,14},{3,15},{4,8},{5,9},{6,10},{7,11},{8,4},{9,5},... | collective-permute-start | bytes 172040 | tf_op jit(solution)/shard_map/ppermute | solution.py:40
  8.7 1.9 %collective-permute-start.3 = (bf16[32,896]{1,0:T(8,128)(2,1)S(1)}, bf16[32,896]{1,0:T(8,128)(2,1)S(1)}, u32[]{:S(2)}, u32[]{:S(2)}) collective-permute-start(bf16[32,896]{1,0:T(8,128)(2,1)S(1)} %collective-permute-done.2), channel_id=1, source_target_pairs={{0,12},{1,13},{2,14},{3,15},{4,8},{5,9},{6,10},{7,11},{8,4},{9,5},... | collective-permute-start | bytes 172040 | tf_op jit(solution)/shard_map/ppermute | solution.py:40
  12.8 1.9 %collective-permute-start.5 = (bf16[16,3584]{1,0:T(8,128)(2,1)S(1)}, bf16[16,3584]{1,0:T(8,128)(2,1)S(1)}, u32[]{:S(2)}, u32[]{:S(2)}) collective-permute-start(bf16[16,3584]{1,0:T(8,128)(2,1)S(1)} %get-tuple-element.123), channel_id=1, source_target_pairs={{0,5},{1,7},{2,4},{3,6},{4,2},{5,0},{6,3},{7,1},{8,14},{9,12},{10,... | collective-permute-start | bytes 344072 | tf_op jit(solution)/shard_map/ppermute | solution.py:40
  14.9 2.4 %collective-permute-done.5 = bf16[16,3584]{1,0:T(8,128)(2,1)S(1)} collective-permute-done((bf16[16,3584]{1,0:T(8,128)(2,1)S(1)}, bf16[16,3584]{1,0:T(8,128)(2,1)S(1)}, u32[]{:S(2)}, u32[]{:S(2)}) %collective-permute-start.5) | collective-permute-done | bytes 114720 | tf_op jit(solution)/shard_map/ppermute | solution.py:40
  17.3 2.1 %collective-permute-start.6 = (bf16[32,3584]{1,0:T(8,128)(2,1)S(1)}, bf16[32,3584]{1,0:T(8,128)(2,1)S(1)}, u32[]{:S(2)}, u32[]{:S(2)}) collective-permute-start(bf16[32,3584]{1,0:T(8,128)(2,1)S(1)} %pad_maximum_fusion.3), channel_id=1, source_target_pairs={{0,6},{1,4},{2,7},{3,5},{4,1},{5,3},{6,0},{7,2},{8,13},{9,15},{10,... | collective-permute-start | bytes 688136 | tf_op jit(solution)/shard_map/ppermute | solution.py:40
  21.3 1.8 %collective-permute-done.6 = bf16[32,3584]{1,0:T(8,128)(2,1)S(1)} collective-permute-done((bf16[32,3584]{1,0:T(8,128)(2,1)S(1)}, bf16[32,3584]{1,0:T(8,128)(2,1)S(1)}, u32[]{:S(2)}, u32[]{:S(2)}) %collective-permute-start.6) | collective-permute-done | bytes 229408 | tf_op jit(solution)/shard_map/ppermute | solution.py:40
  26.1 1.8 %collective-permute-start.12 = (bf16[32,3584]{1,0:T(8,128)(2,1)S(1)}, bf16[32,3584]{1,0:T(8,128)(2,1)S(1)}, u32[]{:S(2)}, u32[]{:S(2)}) collective-permute-start(bf16[32,3584]{1,0:T(8,128)(2,1)S(1)} %fusion.3), channel_id=1, source_target_pairs={{0,6},{1,4},{2,7},{3,5},{4,1},{5,3},{6,0},{7,2},{8,13},{9,15},{10,... | collective-permute-start | bytes 688136 | tf_op jit(solution)/shard_map/ppermute | solution.py:40
  31.9 2.1 %collective-permute-start.13 = (bf16[16,3584]{1,0:T(8,128)(2,1)S(1)}, bf16[16,3584]{1,0:T(8,128)(2,1)S(1)}, u32[]{:S(2)}, u32[]{:S(2)}) collective-permute-start(bf16[16,3584]{1,0:T(8,128)(2,1)S(1)} %slice.143), channel_id=1, source_target_pairs={{0,5},{1,7},{2,4},{3,6},{4,2},{5,0},{6,3},{7,1},{8,14},{9,12},{10,... | collective-permute-start | bytes 344072 | tf_op jit(solution)/shard_map/ppermute | solution.py:40
  34.9 1.2 %collective-permute-start.19 = (bf16[16,3584]{1,0:T(8,128)(2,1)S(1)}, bf16[16,3584]{1,0:T(8,128)(2,1)S(1)}, u32[]{:S(2)}, u32[]{:S(2)}) collective-permute-start(bf16[16,3584]{1,0:T(8,128)(2,1)S(1)} %slice.142), channel_id=1, source_target_pairs={{0,5},{1,7},{2,4},{3,6},{4,2},{5,0},{6,3},{7,1},{8,14},{9,12},{10,... | collective-permute-start | bytes 344072 | tf_op jit(solution)/shard_map/ppermute | solution.py:40
  36.5 1.9 %collective-permute-start.14 = (bf16[16,3584]{1,0:T(8,128)(2,1)S(1)}, bf16[16,3584]{1,0:T(8,128)(2,1)S(1)}, u32[]{:S(2)}, u32[]{:S(2)}) collective-permute-start(bf16[16,3584]{1,0:T(8,128)(2,1)S(1)} %get-tuple-element.114), channel_id=1, source_target_pairs={{0,12},{1,21},{2,22},{3,15},{4,16},{5,9},{6,10},{7,19},{8,28},{9,5... | collective-permute-start | bytes 344072 | tf_op jit(solution)/shard_map/ppermute | solution.py:40
  39.2 1.4 %collective-permute-start.20 = (bf16[16,3584]{1,0:T(8,128)(2,1)S(1)}, bf16[16,3584]{1,0:T(8,128)(2,1)S(1)}, u32[]{:S(2)}, u32[]{:S(2)}) collective-permute-start(bf16[16,3584]{1,0:T(8,128)(2,1)S(1)} %get-tuple-element.112), channel_id=1, source_target_pairs={{0,12},{1,21},{2,22},{3,15},{4,16},{5,9},{6,10},{7,19},{8,28},{9,5... | collective-permute-start | bytes 344072 | tf_op jit(solution)/shard_map/ppermute | solution.py:40
  41.6 3.6 %collective-permute-start.15 = (bf16[16,3584]{1,0:T(8,128)(2,1)S(1)}, bf16[16,3584]{1,0:T(8,128)(2,1)S(1)}, u32[]{:S(2)}, u32[]{:S(2)}) collective-permute-start(bf16[16,3584]{1,0:T(8,128)(2,1)S(1)} %fusion.32), channel_id=1, source_target_pairs={{0,20},{1,13},{2,14},{3,23},{4,8},{5,17},{6,18},{7,11},{8,4},{9,29... | collective-permute-start | bytes 344072 | tf_op jit(solution)/shard_map/ppermute | solution.py:40
  45.2 2.4 %collective-permute-start.21 = (bf16[16,3584]{1,0:T(8,128)(2,1)S(1)}, bf16[16,3584]{1,0:T(8,128)(2,1)S(1)}, u32[]{:S(2)}, u32[]{:S(2)}) collective-permute-start(bf16[16,3584]{1,0:T(8,128)(2,1)S(1)} %fusion.33), channel_id=1, source_target_pairs={{0,20},{1,13},{2,14},{3,23},{4,8},{5,17},{6,18},{7,11},{8,4},{9,29... | collective-permute-start | bytes 344072 | tf_op jit(solution)/shard_map/ppermute | solution.py:40
  47.7 1.7 %collective-permute-done.15 = bf16[16,3584]{1,0:T(8,128)(2,1)S(1)} collective-permute-done((bf16[16,3584]{1,0:T(8,128)(2,1)S(1)}, bf16[16,3584]{1,0:T(8,128)(2,1)S(1)}, u32[]{:S(2)}, u32[]{:S(2)}) %collective-permute-start.15) | collective-permute-done | bytes 114720 | tf_op jit(solution)/shard_map/ppermute | solution.py:40
  49.4 1.5 %collective-permute-start.16 = (bf16[16,3584]{1,0:T(8,128)(2,1)S(1)}, bf16[16,3584]{1,0:T(8,128)(2,1)S(1)}, u32[]{:S(2)}, u32[]{:S(2)}) collective-permute-start(bf16[16,3584]{1,0:T(8,128)(2,1)S(1)} %get-tuple-element.121), channel_id=1, source_target_pairs={{0,5},{1,7},{2,4},{3,6},{4,2},{5,0},{6,3},{7,1},{8,14},{9,12},{10,... | collective-permute-start | bytes 344072 | tf_op jit(solution)/shard_map/ppermute | solution.py:40
  52.0 1.3 %collective-permute-start.22 = (bf16[16,3584]{1,0:T(8,128)(2,1)S(1)}, bf16[16,3584]{1,0:T(8,128)(2,1)S(1)}, u32[]{:S(2)}, u32[]{:S(2)}) collective-permute-start(bf16[16,3584]{1,0:T(8,128)(2,1)S(1)} %get-tuple-element.119), channel_id=1, source_target_pairs={{0,5},{1,7},{2,4},{3,6},{4,2},{5,0},{6,3},{7,1},{8,14},{9,12},{10,... | collective-permute-start | bytes 344072 | tf_op jit(solution)/shard_map/ppermute | solution.py:40
  54.9 1.3 %collective-permute-done.22 = bf16[16,3584]{1,0:T(8,128)(2,1)S(1)} collective-permute-done((bf16[16,3584]{1,0:T(8,128)(2,1)S(1)}, bf16[16,3584]{1,0:T(8,128)(2,1)S(1)}, u32[]{:S(2)}, u32[]{:S(2)}) %collective-permute-start.22) | collective-permute-done | bytes 114720 | tf_op jit(solution)/shard_map/ppermute | solution.py:40
  56.3 1.7 %collective-permute-start.23 = (bf16[32,3584]{1,0:T(8,128)(2,1)S(1)}, bf16[32,3584]{1,0:T(8,128)(2,1)S(1)}, u32[]{:S(2)}, u32[]{:S(2)}) collective-permute-start(bf16[32,3584]{1,0:T(8,128)(2,1)S(1)} %pad_maximum_fusion.6), channel_id=1, source_target_pairs={{0,6},{1,4},{2,7},{3,5},{4,1},{5,3},{6,0},{7,2},{8,13},{9,15},{10,... | collective-permute-start | bytes 688136 | tf_op jit(solution)/shard_map/ppermute | solution.py:40
  64.9 3.0 %collective-permute-start.25 = (f32[1,1792]{1,0:T(1,128)S(1)}, f32[1,1792]{1,0:T(1,128)S(1)}, u32[]{:S(2)}, u32[]{:S(2)}) collective-permute-start(f32[1,1792]{1,0:T(1,128)S(1)} %broadcast_select_fusion.8), channel_id=1, source_target_pairs={{0,20},{1,21},{2,22},{3,23},{4,16},{5,17},{6,18},{7,19},{8,28},{9,... | collective-permute-start | bytes 21512 | tf_op jit(solution)/shard_map/ppermute | solution.py:40
  69.3 1.9 %collective-permute-start.28 = (f32[1,896]{1,0:T(1,128)S(1)}, f32[1,896]{1,0:T(1,128)S(1)}, u32[]{:S(2)}, u32[]{:S(2)}) collective-permute-start(f32[1,896]{1,0:T(1,128)S(1)} %broadcast_select_fusion.10), channel_id=1, source_target_pairs={{0,12},{1,13},{2,14},{3,15},{4,8},{5,9},{6,10},{7,11},{8,4},{9,5},... | collective-permute-start | bytes 10760 | tf_op jit(solution)/shard_map/ppermute | solution.py:40
  71.3 1.5 %fusion = bf16[168,3584]{1,0:T(8,128)(2,1)} fusion(bf16[256,168]{1,0:T(8,128)(2,1)S(1)} %constant_dynamic-update-slice_fusion, bf16[256,3584]{1,0:T(8,128)(2,1)S(1)} %constant_dynamic-update-slice_fusion.5, bf16[168,3584]{1,0:T(8,128)(2,1)S(1)} %copy-done, f32[168]{0:T(256)S(1)} %rsqrt_multiply_fusion), kind=kOutput, calls=%fused_computation.1 | convolution fusion | flops 310689792 | bytes 4330144 | tf_op jit(solution)/shard_map/dot_general | solution.py:48
  73.1 1.8 %collective-permute-start.31 = (f32[2,224]{1,0:T(2,128)S(1)}, f32[2,224]{1,0:T(2,128)S(1)}, u32[]{:S(2)}, u32[]{:S(2)}) collective-permute-start(f32[2,224]{1,0:T(2,128)S(1)} %broadcast_select_fusion.12), channel_id=1, source_target_pairs={{0,6},{1,7},{2,4},{3,5},{4,2},{5,3},{6,0},{7,1},{8,14},{9,15},{10,... | collective-permute-start | bytes 5384 | tf_op jit(solution)/shard_map/ppermute | solution.py:40
  74.9 1.5 %convolution_convert_fusion = bf16[168,3584]{1,0:T(8,128)(2,1)} fusion(bf16[256,168]{1,0:T(8,128)(2,1)S(1)} %constant_dynamic-update-slice_fusion.10, bf16[256,3584]{1,0:T(8,128)(2,1)S(1)} %constant_dynamic-update-slice_fusion.15), kind=kOutput, calls=%fused_computation.2 | convolution fusion | flops 308883456 | bytes 3125248 | tf_op jit(solution)/shard_map/dot_general | solution.py:48
  (150 shorter events, 32.0 us)
Async XLA Ops:
  2.7 6.0 %collective-permute-start.2 = (bf16[32,896]{1,0:T(8,128)(2,1)S(1)}, bf16[32,896]{1,0:T(8,128)(2,1)S(1)}, u32[]{:S(2)}, u32[]{:S(2)}) collective-permute-start(bf16[32,896]{1,0:T(8,128)(2,1)S(1)} %get-tuple-element.116), channel_id=1, source_target_pairs={{0,20},{1,21},{2,22},{3,23},{4,16},{5,17},{6,18},{7,19},{8,28},{9,... | collective-permute-start | bytes 172040 | tf_op jit(solution)/shard_map/ppermute | solution.py:40
  6.5 5.5 %collective-permute-start.4 = (bf16[32,896]{1,0:T(8,128)(2,1)S(1)}, bf16[32,896]{1,0:T(8,128)(2,1)S(1)}, u32[]{:S(2)}, u32[]{:S(2)}) collective-permute-start(bf16[32,896]{1,0:T(8,128)(2,1)S(1)} %get-tuple-element.116), channel_id=1, source_target_pairs={{0,12},{1,13},{2,14},{3,15},{4,8},{5,9},{6,10},{7,11},{8,4},{9,5},... | collective-permute-start | bytes 172040 | tf_op jit(solution)/shard_map/ppermute | solution.py:40
  10.7 13.5 %collective-permute-start.11 = (bf16[168,3584]{1,0:T(8,128)(2,1)S(1)}, bf16[168,3584]{1,0:T(8,128)(2,1)S(1)}, u32[]{:S(2)}, u32[]{:S(2)}) collective-permute-start(bf16[168,3584]{1,0:T(8,128)(2,1)S(1)} %copy-done), channel_id=1, source_target_pairs={{0,4},{1,5},{2,6},{3,7},{4,0},{5,1},{6,2},{7,3},{8,12},{9,13},{10,... | collective-permute-start | bytes 3612680 | tf_op jit(solution)/shard_map/ppermute | solution.py:36
  11.4 12.2 %collective-permute-start.9 = (bf16[168,3584]{1,0:T(8,128)(2,1)S(1)}, bf16[168,3584]{1,0:T(8,128)(2,1)S(1)}, u32[]{:S(2)}, u32[]{:S(2)}) collective-permute-start(bf16[168,3584]{1,0:T(8,128)(2,1)S(1)} %copy-done.1), channel_id=1, source_target_pairs={{0,4},{1,5},{2,6},{3,7},{4,0},{5,1},{6,2},{7,3},{8,12},{9,13},{10,... | collective-permute-start | bytes 3612680 | tf_op jit(solution)/shard_map/ppermute | solution.py:36
  11.6 12.0 %collective-permute-start.10 = (f32[168]{0:T(256)S(1)}, f32[168]{0:T(256)S(1)}, u32[]{:S(2)}, u32[]{:S(2)}) collective-permute-start(f32[168]{0:T(256)S(1)} %copy-done.2), channel_id=1, source_target_pairs={{0,4},{1,5},{2,6},{3,7},{4,0},{5,1},{6,2},{7,3},{8,12},{9,13},{10,... | collective-permute-start | bytes 2024 | tf_op jit(solution)/shard_map/ppermute | solution.py:36
  12.8 4.4 %collective-permute-start.5 = (bf16[16,3584]{1,0:T(8,128)(2,1)S(1)}, bf16[16,3584]{1,0:T(8,128)(2,1)S(1)}, u32[]{:S(2)}, u32[]{:S(2)}) collective-permute-start(bf16[16,3584]{1,0:T(8,128)(2,1)S(1)} %get-tuple-element.123), channel_id=1, source_target_pairs={{0,5},{1,7},{2,4},{3,6},{4,2},{5,0},{6,3},{7,1},{8,14},{9,12},{10,... | collective-permute-start | bytes 344072 | tf_op jit(solution)/shard_map/ppermute | solution.py:40
  14.8 4.6 %collective-permute-start.7 = (bf16[16,3584]{1,0:T(8,128)(2,1)S(1)}, bf16[16,3584]{1,0:T(8,128)(2,1)S(1)}, u32[]{:S(2)}, u32[]{:S(2)}) collective-permute-start(bf16[16,3584]{1,0:T(8,128)(2,1)S(1)} %get-tuple-element.122), channel_id=1, source_target_pairs={{0,5},{1,7},{2,4},{3,6},{4,2},{5,0},{6,3},{7,1},{8,14},{9,12},{10,... | collective-permute-start | bytes 344072 | tf_op jit(solution)/shard_map/ppermute | solution.py:40
  17.3 5.8 %collective-permute-start.6 = (bf16[32,3584]{1,0:T(8,128)(2,1)S(1)}, bf16[32,3584]{1,0:T(8,128)(2,1)S(1)}, u32[]{:S(2)}, u32[]{:S(2)}) collective-permute-start(bf16[32,3584]{1,0:T(8,128)(2,1)S(1)} %pad_maximum_fusion.3), channel_id=1, source_target_pairs={{0,6},{1,4},{2,7},{3,5},{4,1},{5,3},{6,0},{7,2},{8,13},{9,15},{10,... | collective-permute-start | bytes 688136 | tf_op jit(solution)/shard_map/ppermute | solution.py:40
  19.4 6.1 %collective-permute-start.8 = (bf16[32,3584]{1,0:T(8,128)(2,1)S(1)}, bf16[32,3584]{1,0:T(8,128)(2,1)S(1)}, u32[]{:S(2)}, u32[]{:S(2)}) collective-permute-start(bf16[32,3584]{1,0:T(8,128)(2,1)S(1)} %pad_maximum_fusion.4), channel_id=1, source_target_pairs={{0,6},{1,4},{2,7},{3,5},{4,1},{5,3},{6,0},{7,2},{8,13},{9,15},{10,... | collective-permute-start | bytes 688136 | tf_op jit(solution)/shard_map/ppermute | solution.py:40
  26.1 5.5 %collective-permute-start.12 = (bf16[32,3584]{1,0:T(8,128)(2,1)S(1)}, bf16[32,3584]{1,0:T(8,128)(2,1)S(1)}, u32[]{:S(2)}, u32[]{:S(2)}) collective-permute-start(bf16[32,3584]{1,0:T(8,128)(2,1)S(1)} %fusion.3), channel_id=1, source_target_pairs={{0,6},{1,4},{2,7},{3,5},{4,1},{5,3},{6,0},{7,2},{8,13},{9,15},{10,... | collective-permute-start | bytes 688136 | tf_op jit(solution)/shard_map/ppermute | solution.py:40
  29.1 5.5 %collective-permute-start.18 = (bf16[32,3584]{1,0:T(8,128)(2,1)S(1)}, bf16[32,3584]{1,0:T(8,128)(2,1)S(1)}, u32[]{:S(2)}, u32[]{:S(2)}) collective-permute-start(bf16[32,3584]{1,0:T(8,128)(2,1)S(1)} %fusion.4), channel_id=1, source_target_pairs={{0,6},{1,4},{2,7},{3,5},{4,1},{5,3},{6,0},{7,2},{8,13},{9,15},{10,... | collective-permute-start | bytes 688136 | tf_op jit(solution)/shard_map/ppermute | solution.py:40
  31.9 4.5 %collective-permute-start.13 = (bf16[16,3584]{1,0:T(8,128)(2,1)S(1)}, bf16[16,3584]{1,0:T(8,128)(2,1)S(1)}, u32[]{:S(2)}, u32[]{:S(2)}) collective-permute-start(bf16[16,3584]{1,0:T(8,128)(2,1)S(1)} %slice.143), channel_id=1, source_target_pairs={{0,5},{1,7},{2,4},{3,6},{4,2},{5,0},{6,3},{7,1},{8,14},{9,12},{10,... | collective-permute-start | bytes 344072 | tf_op jit(solution)/shard_map/ppermute | solution.py:40
  34.9 4.3 %collective-permute-start.19 = (bf16[16,3584]{1,0:T(8,128)(2,1)S(1)}, bf16[16,3584]{1,0:T(8,128)(2,1)S(1)}, u32[]{:S(2)}, u32[]{:S(2)}) collective-permute-start(bf16[16,3584]{1,0:T(8,128)(2,1)S(1)} %slice.142), channel_id=1, source_target_pairs={{0,5},{1,7},{2,4},{3,6},{4,2},{5,0},{6,3},{7,1},{8,14},{9,12},{10,... | collective-permute-start | bytes 344072 | tf_op jit(solution)/shard_map/ppermute | solution.py:40
  36.5 5.1 %collective-permute-start.14 = (bf16[16,3584]{1,0:T(8,128)(2,1)S(1)}, bf16[16,3584]{1,0:T(8,128)(2,1)S(1)}, u32[]{:S(2)}, u32[]{:S(2)}) collective-permute-start(bf16[16,3584]{1,0:T(8,128)(2,1)S(1)} %get-tuple-element.114), channel_id=1, source_target_pairs={{0,12},{1,21},{2,22},{3,15},{4,16},{5,9},{6,10},{7,19},{8,28},{9,5... | collective-permute-start | bytes 344072 | tf_op jit(solution)/shard_map/ppermute | solution.py:40
  39.2 6.0 %collective-permute-start.20 = (bf16[16,3584]{1,0:T(8,128)(2,1)S(1)}, bf16[16,3584]{1,0:T(8,128)(2,1)S(1)}, u32[]{:S(2)}, u32[]{:S(2)}) collective-permute-start(bf16[16,3584]{1,0:T(8,128)(2,1)S(1)} %get-tuple-element.112), channel_id=1, source_target_pairs={{0,12},{1,21},{2,22},{3,15},{4,16},{5,9},{6,10},{7,19},{8,28},{9,5... | collective-permute-start | bytes 344072 | tf_op jit(solution)/shard_map/ppermute | solution.py:40
  41.6 7.7 %collective-permute-start.15 = (bf16[16,3584]{1,0:T(8,128)(2,1)S(1)}, bf16[16,3584]{1,0:T(8,128)(2,1)S(1)}, u32[]{:S(2)}, u32[]{:S(2)}) collective-permute-start(bf16[16,3584]{1,0:T(8,128)(2,1)S(1)} %fusion.32), channel_id=1, source_target_pairs={{0,20},{1,13},{2,14},{3,23},{4,8},{5,17},{6,18},{7,11},{8,4},{9,29... | collective-permute-start | bytes 344072 | tf_op jit(solution)/shard_map/ppermute | solution.py:40
  45.2 6.7 %collective-permute-start.21 = (bf16[16,3584]{1,0:T(8,128)(2,1)S(1)}, bf16[16,3584]{1,0:T(8,128)(2,1)S(1)}, u32[]{:S(2)}, u32[]{:S(2)}) collective-permute-start(bf16[16,3584]{1,0:T(8,128)(2,1)S(1)} %fusion.33), channel_id=1, source_target_pairs={{0,20},{1,13},{2,14},{3,23},{4,8},{5,17},{6,18},{7,11},{8,4},{9,29... | collective-permute-start | bytes 344072 | tf_op jit(solution)/shard_map/ppermute | solution.py:40
  52.0 4.3 %collective-permute-start.22 = (bf16[16,3584]{1,0:T(8,128)(2,1)S(1)}, bf16[16,3584]{1,0:T(8,128)(2,1)S(1)}, u32[]{:S(2)}, u32[]{:S(2)}) collective-permute-start(bf16[16,3584]{1,0:T(8,128)(2,1)S(1)} %get-tuple-element.119), channel_id=1, source_target_pairs={{0,5},{1,7},{2,4},{3,6},{4,2},{5,0},{6,3},{7,1},{8,14},{9,12},{10,... | collective-permute-start | bytes 344072 | tf_op jit(solution)/shard_map/ppermute | solution.py:40
  53.7 6.2 %collective-permute-start.17 = (bf16[32,3584]{1,0:T(8,128)(2,1)S(1)}, bf16[32,3584]{1,0:T(8,128)(2,1)S(1)}, u32[]{:S(2)}, u32[]{:S(2)}) collective-permute-start(bf16[32,3584]{1,0:T(8,128)(2,1)S(1)} %pad_maximum_fusion.5), channel_id=1, source_target_pairs={{0,6},{1,4},{2,7},{3,5},{4,1},{5,3},{6,0},{7,2},{8,13},{9,15},{10,... | collective-permute-start | bytes 688136 | tf_op jit(solution)/shard_map/ppermute | solution.py:40
  56.3 5.5 %collective-permute-start.23 = (bf16[32,3584]{1,0:T(8,128)(2,1)S(1)}, bf16[32,3584]{1,0:T(8,128)(2,1)S(1)}, u32[]{:S(2)}, u32[]{:S(2)}) collective-permute-start(bf16[32,3584]{1,0:T(8,128)(2,1)S(1)} %pad_maximum_fusion.6), channel_id=1, source_target_pairs={{0,6},{1,4},{2,7},{3,5},{4,1},{5,3},{6,0},{7,2},{8,13},{9,15},{10,... | collective-permute-start | bytes 688136 | tf_op jit(solution)/shard_map/ppermute | solution.py:40
  63.9 5.3 %collective-permute-start.27 = (bf16[128,3584]{1,0:T(8,128)(2,1)S(1)}, bf16[128,3584]{1,0:T(8,128)(2,1)S(1)}, u32[]{:S(2)}, u32[]{:S(2)}) collective-permute-start(bf16[128,3584]{1,0:T(8,128)(2,1)S(1)} %pad_maximum_fusion), channel_id=1, source_target_pairs={{0,4},{1,5},{2,6},{3,7},{4,0},{5,1},{6,2},{7,3},{8,12},{9,13},{10,... | collective-permute-start | bytes 2752520 | tf_op jit(solution)/shard_map/ppermute | solution.py:36
  64.4 4.8 %collective-permute-start.29 = (bf16[128,168]{1,0:T(8,128)(2,1)S(1)}, bf16[128,168]{1,0:T(8,128)(2,1)S(1)}, u32[]{:S(2)}, u32[]{:S(2)}) collective-permute-start(bf16[128,168]{1,0:T(8,128)(2,1)S(1)} %pad_maximum_fusion.8), channel_id=1, source_target_pairs={{0,4},{1,5},{2,6},{3,7},{4,0},{5,1},{6,2},{7,3},{8,12},{9,13},{10,... | collective-permute-start | bytes 129032 | tf_op jit(solution)/shard_map/ppermute | solution.py:36
  64.9 4.3 %collective-permute-start.25 = (f32[1,1792]{1,0:T(1,128)S(1)}, f32[1,1792]{1,0:T(1,128)S(1)}, u32[]{:S(2)}, u32[]{:S(2)}) collective-permute-start(f32[1,1792]{1,0:T(1,128)S(1)} %broadcast_select_fusion.8), channel_id=1, source_target_pairs={{0,20},{1,21},{2,22},{3,23},{4,16},{5,17},{6,18},{7,19},{8,28},{9,... | collective-permute-start | bytes 21512 | tf_op jit(solution)/shard_map/ppermute | solution.py:40
  68.2 4.6 %collective-permute-start.30 = (bf16[128,3584]{1,0:T(8,128)(2,1)S(1)}, bf16[128,3584]{1,0:T(8,128)(2,1)S(1)}, u32[]{:S(2)}, u32[]{:S(2)}) collective-permute-start(bf16[128,3584]{1,0:T(8,128)(2,1)S(1)} %pad_maximum_fusion.1), channel_id=1, source_target_pairs={{0,4},{1,5},{2,6},{3,7},{4,0},{5,1},{6,2},{7,3},{8,12},{9,13},{10,... | collective-permute-start | bytes 2752520 | tf_op jit(solution)/shard_map/ppermute | solution.py:36
  (12 other events, 51.7 us)

commit v4 on v3

--- a/solution.py
+++ b/solution.py
@@ -38,6 +38,16 @@
     def step(self, v, pair):
         target = [i ^ self.core ^ pair[self.stream_of(i)] for i in range(self.size)]
         return lax.ppermute(v, AXES, list(enumerate(target)))
+
+    def from_chip(self, v, mask):
+        across = mask * 2 * self.rows
+        if bin(mask).count("1") % 2:
+            return self.step(v, (across, across))
+        return lax.ppermute(v, AXES, [(i, i ^ across) for i in range(self.size)])
+
+
+def after(v, *others):
+    return lax.optimization_barrier((v, *others))[0]
 
 
 def dot_rows(v, w):
@@ -67,15 +77,11 @@
     )
     shifted = jnp.where(stream == 0, shifted[:half], shifted[half:])
 
-    held, masks = [shifted.astype(bf16)], [0]
-    for b, mask in list(zip(grid.chip_bits, bits_below(grid.chips)))[::-1]:
-        held = held + [grid.step(u, (b, b)) for u in held]
-        masks = masks + [m ^ mask for m in masks]
-        if b == grid.chip_bits[-1]:
-            held[-1], encoder, decoder, latent_bias = lax.optimization_barrier(
-                (held[-1], encoder, decoder, latent_bias)
-            )
-    held = [u for _, u in sorted(zip(masks, held), key=lambda t: t[0])]
+    held = {0: shifted.astype(bf16)}
+    for mask in range(1, grid.chips)[::-1]:
+        held[mask] = grid.from_chip(held[0], mask)
+    held = [held[mask] for mask in range(grid.chips)]
+    encoder, decoder, latent_bias = (after(w, held[-1]) for w in (encoder, decoder, latent_bias))
     for mask in bits_below(grid.chips):
         flip = (chip // mask) % 2 == 1
         held = [jnp.where(flip, held[k ^ mask], held[k]) for k in range(len(held))]
@@ -103,7 +109,7 @@
 
     for near, far in centered:
         if sends:
-            sends[-1], far = lax.optimization_barrier((sends[-1], far))
+            far = after(far, sends[-1])
         keeps.append(forward(near))
         sends.append(forward(far).astype(bf16))
     norms = [jnp.sqrt(jnp.sum(jnp.square(d.astype(f32)), axis=1) + 1e-06) for d in decoders]
@@ -117,6 +123,8 @@
     for i in range(len(row_steps))[::-1]:
         received = [grid.step(v, row_steps[i]) for v in sends]
         for k in range(CHUNKS):
+            if k > 0:
+                received[k] = after(received[k], sends[k - 1])
             v = keeps[k] + received[k].astype(f32)
             n = v.shape[0] // 2
             if i > 0:
@@ -127,6 +135,8 @@
     for pair in chip_steps:
         received = [grid.step(v, pair) for v in sends]
         for k in range(CHUNKS):
+            if k > 0:
+                received[k] = after(received[k], sends[k - 1])
             keeps[k] = keeps[k] + received[k].astype(f32)
             sends[k] = keeps[k].astype(bf16)
     columns = sum(jnp.sum(v, axis=0, keepdims=True) for v in keeps)

time: 80.3 us -> 79 us (0.984)
  starting transfers between devices: 43.2 us -> 33.7 us
  waiting for transfers between devices: 17.2 us -> 25.3 us
    ppermute x23 -> x22, starting transfers between devices: 40.1 us -> 25 us  [step(): return lax.ppermute(v, AXES, list(enumerate(target)))]
    ppermute x23 -> x22, waiting for transfers between devices: 16.6 us -> 22.8 us  [step(): return lax.ppermute(v, AXES, list(enumerate(target)))]
    ppermute x0 -> x1, starting transfers between devices: none -> 4.84 us  [from_chip(): return lax.ppermute(v, AXES, [(i, i ^ across) for i in range(self.size)])]
    ppermute x0 -> x1, waiting for transfers between devices: none -> 2.12 us  [from_chip(): return lax.ppermute(v, AXES, [(i, i ^ across) for i in range(self.size)])]
  transfers between devices with their start and end apart: 33 -> 33, of which waited for: 19 -> 20; matrix products, arithmetic and copies ran while one was open for 19% -> 20% of each run, Pallas kernels for 0% -> 0%
where the time goes in v4:
time: 79 us; the launch traced here: 78.8 us
  starting transfers between devices  33.7 us (43%)
  waiting for transfers between devices  25.3 us (32%)
  matrix products  14.1 us (18%)
  other arithmetic  3.97 us (5%)
  between operations  1.33 us (2%)
    ppermute x22, starting transfers between devices, step(): return lax.ppermute(v, AXES, list(enumerate(target)))  25 us
    ppermute x22, waiting for transfers between devices, step(): return lax.ppermute(v, AXES, list(enumerate(target)))  22.8 us
    dot_general x16, matrix products, dot_rows(): lax.dot_general(v, w, (((1,), (1,)), ((), ())), preferred_element_type=f32)  7.71 us
    ppermute x1, starting transfers between devices, from_chip(): return lax.ppermute(v, AXES, [(i, i ^ across) for i in range(self.size)])  4.84 us
    ppermute x10, starting transfers between devices, swap_core(): return lax.ppermute(v, AXES, [(i, i ^ self.core) for i in range(self.size)])  3.86 us
    dot_general x2, matrix products, over_rows(): lax.dot_general(u, v, (((0,), (0,)), ((), ())), preferred_element_type=f32)  3.05 us
    dot_general x8, matrix products, forward(): jnp.dot(l, d, preferred_element_type=f32)  2.78 us
    ppermute x1, waiting for transfers between devices, from_chip(): return lax.ppermute(v, AXES, [(i, i ^ across) for i in range(self.size)])  2.12 us
  transfers between devices with their start and end apart: 33, of which 20 were waited for; matrix products, arithmetic and copies ran while one was open for 20% of the time, Pallas kernels for 0%

profile of v4, /device:TPU:0, one launch (start us, length us, event | category | flops | bytes accessed | tf_op | source)
XLA Modules:
  0.0 78.8 jit_solution(7005533347789769112)
XLA Ops:
  2.7 4.8 %collective-permute-start.2 = (bf16[32,896]{1,0:T(8,128)(2,1)S(1)}, bf16[32,896]{1,0:T(8,128)(2,1)S(1)}, u32[]{:S(2)}, u32[]{:S(2)}) collective-permute-start(bf16[32,896]{1,0:T(8,128)(2,1)S(1)} %get-tuple-element.120), channel_id=1, source_target_pairs={{0,24},{1,25},{2,26},{3,27},{4,28},{5,29},{6,30},{7,31},{8,16},{9,... | collective-permute-start | bytes 172040 | tf_op jit(solution)/shard_map/ppermute | solution.py:46
  8.0 2.1 %collective-permute-done.2 = bf16[32,896]{1,0:T(8,128)(2,1)S(1)} collective-permute-done((bf16[32,896]{1,0:T(8,128)(2,1)S(1)}, bf16[32,896]{1,0:T(8,128)(2,1)S(1)}, u32[]{:S(2)}, u32[]{:S(2)}) %collective-permute-start.2) | collective-permute-done | bytes 57376 | tf_op jit(solution)/shard_map/ppermute | solution.py:46
  11.0 2.0 %collective-permute-done.3 = bf16[32,896]{1,0:T(8,128)(2,1)S(1)} collective-permute-done((bf16[32,896]{1,0:T(8,128)(2,1)S(1)}, bf16[32,896]{1,0:T(8,128)(2,1)S(1)}, u32[]{:S(2)}, u32[]{:S(2)}) %collective-permute-start.3) | collective-permute-done | bytes 57376 | tf_op jit(solution)/shard_map/ppermute | solution.py:40
  13.1 1.2 %collective-permute-start.5 = (bf16[16,3584]{1,0:T(8,128)(2,1)S(1)}, bf16[16,3584]{1,0:T(8,128)(2,1)S(1)}, u32[]{:S(2)}, u32[]{:S(2)}) collective-permute-start(bf16[16,3584]{1,0:T(8,128)(2,1)S(1)} %get-tuple-element.127), channel_id=1, source_target_pairs={{0,5},{1,7},{2,4},{3,6},{4,2},{5,0},{6,3},{7,1},{8,14},{9,12},{10,... | collective-permute-start | bytes 344072 | tf_op jit(solution)/shard_map/ppermute | solution.py:40
  15.0 2.4 %collective-permute-done.5 = bf16[16,3584]{1,0:T(8,128)(2,1)S(1)} collective-permute-done((bf16[16,3584]{1,0:T(8,128)(2,1)S(1)}, bf16[16,3584]{1,0:T(8,128)(2,1)S(1)}, u32[]{:S(2)}, u32[]{:S(2)}) %collective-permute-start.5) | collective-permute-done | bytes 114720 | tf_op jit(solution)/shard_map/ppermute | solution.py:40
  17.4 1.5 %collective-permute-start.6 = (bf16[32,3584]{1,0:T(8,128)(2,1)S(1)}, bf16[32,3584]{1,0:T(8,128)(2,1)S(1)}, u32[]{:S(2)}, u32[]{:S(2)}) collective-permute-start(bf16[32,3584]{1,0:T(8,128)(2,1)S(1)} %pad_maximum_fusion.3), channel_id=1, source_target_pairs={{0,6},{1,4},{2,7},{3,5},{4,1},{5,3},{6,0},{7,2},{8,13},{9,15},{10,... | collective-permute-start | bytes 688136 | tf_op jit(solution)/shard_map/ppermute | solution.py:40
  18.9 1.2 %collective-permute-start.8 = (bf16[32,3584]{1,0:T(8,128)(2,1)S(1)}, bf16[32,3584]{1,0:T(8,128)(2,1)S(1)}, u32[]{:S(2)}, u32[]{:S(2)}) collective-permute-start(bf16[32,3584]{1,0:T(8,128)(2,1)S(1)} %pad_maximum_fusion.4), channel_id=1, source_target_pairs={{0,6},{1,4},{2,7},{3,5},{4,1},{5,3},{6,0},{7,2},{8,13},{9,15},{10,... | collective-permute-start | bytes 688136 | tf_op jit(solution)/shard_map/ppermute | solution.py:40
  21.2 1.7 %collective-permute-done.6 = bf16[32,3584]{1,0:T(8,128)(2,1)S(1)} collective-permute-done((bf16[32,3584]{1,0:T(8,128)(2,1)S(1)}, bf16[32,3584]{1,0:T(8,128)(2,1)S(1)}, u32[]{:S(2)}, u32[]{:S(2)}) %collective-permute-start.6) | collective-permute-done | bytes 229408 | tf_op jit(solution)/shard_map/ppermute | solution.py:40
  24.6 1.8 %collective-permute-start.12 = (bf16[32,3584]{1,0:T(8,128)(2,1)S(1)}, bf16[32,3584]{1,0:T(8,128)(2,1)S(1)}, u32[]{:S(2)}, u32[]{:S(2)}) collective-permute-start(bf16[32,3584]{1,0:T(8,128)(2,1)S(1)} %fusion.3), channel_id=1, source_target_pairs={{0,6},{1,4},{2,7},{3,5},{4,1},{5,3},{6,0},{7,2},{8,13},{9,15},{10,... | collective-permute-start | bytes 688136 | tf_op jit(solution)/shard_map/ppermute | solution.py:40
  31.0 1.6 %collective-permute-start.13 = (bf16[16,3584]{1,0:T(8,128)(2,1)S(1)}, bf16[16,3584]{1,0:T(8,128)(2,1)S(1)}, u32[]{:S(2)}, u32[]{:S(2)}) collective-permute-start(bf16[16,3584]{1,0:T(8,128)(2,1)S(1)} %slice.143), channel_id=1, source_target_pairs={{0,5},{1,7},{2,4},{3,6},{4,2},{5,0},{6,3},{7,1},{8,14},{9,12},{10,... | collective-permute-start | bytes 344072 | tf_op jit(solution)/shard_map/ppermute | solution.py:40
  36.4 1.9 %collective-permute-done.19 = bf16[16,3584]{1,0:T(8,128)(2,1)S(1)} collective-permute-done((bf16[16,3584]{1,0:T(8,128)(2,1)S(1)}, bf16[16,3584]{1,0:T(8,128)(2,1)S(1)}, u32[]{:S(2)}, u32[]{:S(2)}) %collective-permute-start.19) | collective-permute-done | bytes 114720 | tf_op jit(solution)/shard_map/ppermute | solution.py:40
  39.6 2.8 %collective-permute-start.15 = (bf16[16,3584]{1,0:T(8,128)(2,1)S(1)}, bf16[16,3584]{1,0:T(8,128)(2,1)S(1)}, u32[]{:S(2)}, u32[]{:S(2)}) collective-permute-start(bf16[16,3584]{1,0:T(8,128)(2,1)S(1)} %fusion.32), channel_id=1, source_target_pairs={{0,20},{1,13},{2,14},{3,23},{4,8},{5,17},{6,18},{7,11},{8,4},{9,29... | collective-permute-start | bytes 344072 | tf_op jit(solution)/shard_map/ppermute | solution.py:40
  43.3 1.6 %collective-permute-start.21 = (bf16[16,3584]{1,0:T(8,128)(2,1)S(1)}, bf16[16,3584]{1,0:T(8,128)(2,1)S(1)}, u32[]{:S(2)}, u32[]{:S(2)}) collective-permute-start(bf16[16,3584]{1,0:T(8,128)(2,1)S(1)} %fusion.33), channel_id=1, source_target_pairs={{0,20},{1,13},{2,14},{3,23},{4,8},{5,17},{6,18},{7,11},{8,4},{9,29... | collective-permute-start | bytes 344072 | tf_op jit(solution)/shard_map/ppermute | solution.py:40
  44.9 2.2 %collective-permute-done.15 = bf16[16,3584]{1,0:T(8,128)(2,1)S(1)} collective-permute-done((bf16[16,3584]{1,0:T(8,128)(2,1)S(1)}, bf16[16,3584]{1,0:T(8,128)(2,1)S(1)}, u32[]{:S(2)}, u32[]{:S(2)}) %collective-permute-start.15) | collective-permute-done | bytes 114720 | tf_op jit(solution)/shard_map/ppermute | solution.py:40
  48.3 1.3 %collective-permute-done.21 = bf16[16,3584]{1,0:T(8,128)(2,1)S(1)} collective-permute-done((bf16[16,3584]{1,0:T(8,128)(2,1)S(1)}, bf16[16,3584]{1,0:T(8,128)(2,1)S(1)}, u32[]{:S(2)}, u32[]{:S(2)}) %collective-permute-start.21) | collective-permute-done | bytes 114720 | tf_op jit(solution)/shard_map/ppermute | solution.py:40
  49.7 1.6 %collective-permute-start.22 = (bf16[16,3584]{1,0:T(8,128)(2,1)S(1)}, bf16[16,3584]{1,0:T(8,128)(2,1)S(1)}, u32[]{:S(2)}, u32[]{:S(2)}) collective-permute-start(bf16[16,3584]{1,0:T(8,128)(2,1)S(1)} %get-tuple-element.123), channel_id=1, source_target_pairs={{0,5},{1,7},{2,4},{3,6},{4,2},{5,0},{6,3},{7,1},{8,14},{9,12},{10,... | collective-permute-start | bytes 344072 | tf_op jit(solution)/shard_map/ppermute | solution.py:40
  51.5 2.3 %collective-permute-start.17 = (bf16[32,3584]{1,0:T(8,128)(2,1)S(1)}, bf16[32,3584]{1,0:T(8,128)(2,1)S(1)}, u32[]{:S(2)}, u32[]{:S(2)}) collective-permute-start(bf16[32,3584]{1,0:T(8,128)(2,1)S(1)} %pad_maximum_fusion.5), channel_id=1, source_target_pairs={{0,6},{1,4},{2,7},{3,5},{4,1},{5,3},{6,0},{7,2},{8,13},{9,15},{10,... | collective-permute-start | bytes 688136 | tf_op jit(solution)/shard_map/ppermute | solution.py:40
  54.0 1.3 %collective-permute-start.23 = (bf16[32,3584]{1,0:T(8,128)(2,1)S(1)}, bf16[32,3584]{1,0:T(8,128)(2,1)S(1)}, u32[]{:S(2)}, u32[]{:S(2)}) collective-permute-start(bf16[32,3584]{1,0:T(8,128)(2,1)S(1)} %pad_maximum_fusion.6), channel_id=1, source_target_pairs={{0,6},{1,4},{2,7},{3,5},{4,1},{5,3},{6,0},{7,2},{8,13},{9,15},{10,... | collective-permute-start | bytes 688136 | tf_op jit(solution)/shard_map/ppermute | solution.py:40
  59.0 1.5 %collective-permute-done.23 = bf16[32,3584]{1,0:T(8,128)(2,1)S(1)} collective-permute-done((bf16[32,3584]{1,0:T(8,128)(2,1)S(1)}, bf16[32,3584]{1,0:T(8,128)(2,1)S(1)}, u32[]{:S(2)}, u32[]{:S(2)}) %collective-permute-start.23) | collective-permute-done | bytes 229408 | tf_op jit(solution)/shard_map/ppermute | solution.py:40
  62.3 1.4 %collective-permute-start.24 = (f32[1,3584]{1,0:T(1,128)S(1)}, f32[1,3584]{1,0:T(1,128)S(1)}, u32[]{:S(2)}, u32[]{:S(2)}) collective-permute-start(f32[1,3584]{1,0:T(1,128)S(1)} %reshape_subtract_fusion), channel_id=1, source_target_pairs={{0,4},{1,5},{2,6},{3,7},{4,0},{5,1},{6,2},{7,3},{8,12},{9,13},{10,... | collective-permute-start | bytes 43016 | tf_op jit(solution)/shard_map/ppermute | solution.py:36
  66.4 2.2 %collective-permute-done.25 = f32[1,1792]{1,0:T(1,128)S(1)} collective-permute-done((f32[1,1792]{1,0:T(1,128)S(1)}, f32[1,1792]{1,0:T(1,128)S(1)}, u32[]{:S(2)}, u32[]{:S(2)}) %collective-permute-start.25) | collective-permute-done | bytes 7200 | tf_op jit(solution)/shard_map/ppermute | solution.py:40
  69.6 1.5 %fusion = bf16[168,3584]{1,0:T(8,128)(2,1)} fusion(bf16[256,168]{1,0:T(8,128)(2,1)S(1)} %constant_dynamic-update-slice_fusion, bf16[256,3584]{1,0:T(8,128)(2,1)S(1)} %constant_dynamic-update-slice_fusion.5, bf16[168,3584]{1,0:T(8,128)(2,1)S(1)} %copy-done, f32[168]{0:T(256)S(1)} %rsqrt_multiply_fusion), kind=kOutput, calls=%fused_computation.1 | convolution fusion | flops 310689792 | bytes 4330144 | tf_op jit(solution)/shard_map/dot_general | solution.py:58
  72.7 1.5 %convolution_convert_fusion = bf16[168,3584]{1,0:T(8,128)(2,1)} fusion(bf16[256,168]{1,0:T(8,128)(2,1)S(1)} %constant_dynamic-update-slice_fusion.10, bf16[256,3584]{1,0:T(8,128)(2,1)S(1)} %constant_dynamic-update-slice_fusion.15), kind=kOutput, calls=%fused_computation.2 | convolution fusion | flops 308883456 | bytes 3125248 | tf_op jit(solution)/shard_map/dot_general | solution.py:58
  76.1 2.1 %collective-permute-done.32 = f32[2,112]{1,0:T(2,128)S(1)} collective-permute-done((f32[2,112]{1,0:T(2,128)S(1)}, f32[2,112]{1,0:T(2,128)S(1)}, u32[]{:S(2)}, u32[]{:S(2)}) %collective-permute-start.32) | collective-permute-done | bytes 928 | tf_op jit(solution)/shard_map/ppermute | solution.py:40
  (150 shorter events, 31.7 us)
Async XLA Ops:
  2.7 7.4 %collective-permute-start.2 = (bf16[32,896]{1,0:T(8,128)(2,1)S(1)}, bf16[32,896]{1,0:T(8,128)(2,1)S(1)}, u32[]{:S(2)}, u32[]{:S(2)}) collective-permute-start(bf16[32,896]{1,0:T(8,128)(2,1)S(1)} %get-tuple-element.120), channel_id=1, source_target_pairs={{0,24},{1,25},{2,26},{3,27},{4,28},{5,29},{6,30},{7,31},{8,16},{9,... | collective-permute-start | bytes 172040 | tf_op jit(solution)/shard_map/ppermute | solution.py:46
  7.6 5.4 %collective-permute-start.3 = (bf16[32,896]{1,0:T(8,128)(2,1)S(1)}, bf16[32,896]{1,0:T(8,128)(2,1)S(1)}, u32[]{:S(2)}, u32[]{:S(2)}) collective-permute-start(bf16[32,896]{1,0:T(8,128)(2,1)S(1)} %get-tuple-element.120), channel_id=1, source_target_pairs={{0,20},{1,21},{2,22},{3,23},{4,16},{5,17},{6,18},{7,19},{8,28},{9,... | collective-permute-start | bytes 172040 | tf_op jit(solution)/shard_map/ppermute | solution.py:40
  7.6 5.4 %collective-permute-start.4 = (bf16[32,896]{1,0:T(8,128)(2,1)S(1)}, bf16[32,896]{1,0:T(8,128)(2,1)S(1)}, u32[]{:S(2)}, u32[]{:S(2)}) collective-permute-start(bf16[32,896]{1,0:T(8,128)(2,1)S(1)} %get-tuple-element.120), channel_id=1, source_target_pairs={{0,12},{1,13},{2,14},{3,15},{4,8},{5,9},{6,10},{7,11},{8,4},{9,5},... | collective-permute-start | bytes 172040 | tf_op jit(solution)/shard_map/ppermute | solution.py:40
  10.1 13.8 %collective-permute-start.11 = (bf16[168,3584]{1,0:T(8,128)(2,1)S(1)}, bf16[168,3584]{1,0:T(8,128)(2,1)S(1)}, u32[]{:S(2)}, u32[]{:S(2)}) collective-permute-start(bf16[168,3584]{1,0:T(8,128)(2,1)S(1)} %copy-done), channel_id=1, source_target_pairs={{0,4},{1,5},{2,6},{3,7},{4,0},{5,1},{6,2},{7,3},{8,12},{9,13},{10,... | collective-permute-start | bytes 3612680 | tf_op jit(solution)/shard_map/ppermute | solution.py:36
  10.4 13.0 %collective-permute-start.9 = (bf16[168,3584]{1,0:T(8,128)(2,1)S(1)}, bf16[168,3584]{1,0:T(8,128)(2,1)S(1)}, u32[]{:S(2)}, u32[]{:S(2)}) collective-permute-start(bf16[168,3584]{1,0:T(8,128)(2,1)S(1)} %copy-done.1), channel_id=1, source_target_pairs={{0,4},{1,5},{2,6},{3,7},{4,0},{5,1},{6,2},{7,3},{8,12},{9,13},{10,... | collective-permute-start | bytes 3612680 | tf_op jit(solution)/shard_map/ppermute | solution.py:36
  13.1 4.3 %collective-permute-start.5 = (bf16[16,3584]{1,0:T(8,128)(2,1)S(1)}, bf16[16,3584]{1,0:T(8,128)(2,1)S(1)}, u32[]{:S(2)}, u32[]{:S(2)}) collective-permute-start(bf16[16,3584]{1,0:T(8,128)(2,1)S(1)} %get-tuple-element.127), channel_id=1, source_target_pairs={{0,5},{1,7},{2,4},{3,6},{4,2},{5,0},{6,3},{7,1},{8,14},{9,12},{10,... | collective-permute-start | bytes 344072 | tf_op jit(solution)/shard_map/ppermute | solution.py:40
  14.3 4.6 %collective-permute-start.7 = (bf16[16,3584]{1,0:T(8,128)(2,1)S(1)}, bf16[16,3584]{1,0:T(8,128)(2,1)S(1)}, u32[]{:S(2)}, u32[]{:S(2)}) collective-permute-start(bf16[16,3584]{1,0:T(8,128)(2,1)S(1)} %get-tuple-element.126), channel_id=1, source_target_pairs={{0,5},{1,7},{2,4},{3,6},{4,2},{5,0},{6,3},{7,1},{8,14},{9,12},{10,... | collective-permute-start | bytes 344072 | tf_op jit(solution)/shard_map/ppermute | solution.py:40
  14.9 8.5 %collective-permute-start.10 = (f32[168]{0:T(256)S(1)}, f32[168]{0:T(256)S(1)}, u32[]{:S(2)}, u32[]{:S(2)}) collective-permute-start(f32[168]{0:T(256)S(1)} %copy-done.2), channel_id=1, source_target_pairs={{0,4},{1,5},{2,6},{3,7},{4,0},{5,1},{6,2},{7,3},{8,12},{9,13},{10,... | collective-permute-start | bytes 2024 | tf_op jit(solution)/shard_map/ppermute | solution.py:36
  17.4 5.5 %collective-permute-start.6 = (bf16[32,3584]{1,0:T(8,128)(2,1)S(1)}, bf16[32,3584]{1,0:T(8,128)(2,1)S(1)}, u32[]{:S(2)}, u32[]{:S(2)}) collective-permute-start(bf16[32,3584]{1,0:T(8,128)(2,1)S(1)} %pad_maximum_fusion.3), channel_id=1, source_target_pairs={{0,6},{1,4},{2,7},{3,5},{4,1},{5,3},{6,0},{7,2},{8,13},{9,15},{10,... | collective-permute-start | bytes 688136 | tf_op jit(solution)/shard_map/ppermute | solution.py:40
  18.9 7.5 %collective-permute-start.8 = (bf16[32,3584]{1,0:T(8,128)(2,1)S(1)}, bf16[32,3584]{1,0:T(8,128)(2,1)S(1)}, u32[]{:S(2)}, u32[]{:S(2)}) collective-permute-start(bf16[32,3584]{1,0:T(8,128)(2,1)S(1)} %pad_maximum_fusion.4), channel_id=1, source_target_pairs={{0,6},{1,4},{2,7},{3,5},{4,1},{5,3},{6,0},{7,2},{8,13},{9,15},{10,... | collective-permute-start | bytes 688136 | tf_op jit(solution)/shard_map/ppermute | solution.py:40
  24.6 6.0 %collective-permute-start.12 = (bf16[32,3584]{1,0:T(8,128)(2,1)S(1)}, bf16[32,3584]{1,0:T(8,128)(2,1)S(1)}, u32[]{:S(2)}, u32[]{:S(2)}) collective-permute-start(bf16[32,3584]{1,0:T(8,128)(2,1)S(1)} %fusion.3), channel_id=1, source_target_pairs={{0,6},{1,4},{2,7},{3,5},{4,1},{5,3},{6,0},{7,2},{8,13},{9,15},{10,... | collective-permute-start | bytes 688136 | tf_op jit(solution)/shard_map/ppermute | solution.py:40
  28.1 5.5 %collective-permute-start.18 = (bf16[32,3584]{1,0:T(8,128)(2,1)S(1)}, bf16[32,3584]{1,0:T(8,128)(2,1)S(1)}, u32[]{:S(2)}, u32[]{:S(2)}) collective-permute-start(bf16[32,3584]{1,0:T(8,128)(2,1)S(1)} %fusion.4), channel_id=1, source_target_pairs={{0,6},{1,4},{2,7},{3,5},{4,1},{5,3},{6,0},{7,2},{8,13},{9,15},{10,... | collective-permute-start | bytes 688136 | tf_op jit(solution)/shard_map/ppermute | solution.py:40
  31.0 4.3 %collective-permute-start.13 = (bf16[16,3584]{1,0:T(8,128)(2,1)S(1)}, bf16[16,3584]{1,0:T(8,128)(2,1)S(1)}, u32[]{:S(2)}, u32[]{:S(2)}) collective-permute-start(bf16[16,3584]{1,0:T(8,128)(2,1)S(1)} %slice.143), channel_id=1, source_target_pairs={{0,5},{1,7},{2,4},{3,6},{4,2},{5,0},{6,3},{7,1},{8,14},{9,12},{10,... | collective-permute-start | bytes 344072 | tf_op jit(solution)/shard_map/ppermute | solution.py:40
  34.0 4.3 %collective-permute-start.19 = (bf16[16,3584]{1,0:T(8,128)(2,1)S(1)}, bf16[16,3584]{1,0:T(8,128)(2,1)S(1)}, u32[]{:S(2)}, u32[]{:S(2)}) collective-permute-start(bf16[16,3584]{1,0:T(8,128)(2,1)S(1)} %slice.142), channel_id=1, source_target_pairs={{0,5},{1,7},{2,4},{3,6},{4,2},{5,0},{6,3},{7,1},{8,14},{9,12},{10,... | collective-permute-start | bytes 344072 | tf_op jit(solution)/shard_map/ppermute | solution.py:40
  35.3 4.3 %collective-permute-start.14 = (bf16[16,3584]{1,0:T(8,128)(2,1)S(1)}, bf16[16,3584]{1,0:T(8,128)(2,1)S(1)}, u32[]{:S(2)}, u32[]{:S(2)}) collective-permute-start(bf16[16,3584]{1,0:T(8,128)(2,1)S(1)} %get-tuple-element.118), channel_id=1, source_target_pairs={{0,12},{1,21},{2,22},{3,15},{4,16},{5,9},{6,10},{7,19},{8,28},{9,5... | collective-permute-start | bytes 344072 | tf_op jit(solution)/shard_map/ppermute | solution.py:40
  38.3 5.0 %collective-permute-start.20 = (bf16[16,3584]{1,0:T(8,128)(2,1)S(1)}, bf16[16,3584]{1,0:T(8,128)(2,1)S(1)}, u32[]{:S(2)}, u32[]{:S(2)}) collective-permute-start(bf16[16,3584]{1,0:T(8,128)(2,1)S(1)} %get-tuple-element.116), channel_id=1, source_target_pairs={{0,12},{1,21},{2,22},{3,15},{4,16},{5,9},{6,10},{7,19},{8,28},{9,5... | collective-permute-start | bytes 344072 | tf_op jit(solution)/shard_map/ppermute | solution.py:40
  39.6 7.5 %collective-permute-start.15 = (bf16[16,3584]{1,0:T(8,128)(2,1)S(1)}, bf16[16,3584]{1,0:T(8,128)(2,1)S(1)}, u32[]{:S(2)}, u32[]{:S(2)}) collective-permute-start(bf16[16,3584]{1,0:T(8,128)(2,1)S(1)} %fusion.32), channel_id=1, source_target_pairs={{0,20},{1,13},{2,14},{3,23},{4,8},{5,17},{6,18},{7,11},{8,4},{9,29... | collective-permute-start | bytes 344072 | tf_op jit(solution)/shard_map/ppermute | solution.py:40
  43.3 6.3 %collective-permute-start.21 = (bf16[16,3584]{1,0:T(8,128)(2,1)S(1)}, bf16[16,3584]{1,0:T(8,128)(2,1)S(1)}, u32[]{:S(2)}, u32[]{:S(2)}) collective-permute-start(bf16[16,3584]{1,0:T(8,128)(2,1)S(1)} %fusion.33), channel_id=1, source_target_pairs={{0,20},{1,13},{2,14},{3,23},{4,8},{5,17},{6,18},{7,11},{8,4},{9,29... | collective-permute-start | bytes 344072 | tf_op jit(solution)/shard_map/ppermute | solution.py:40
  49.7 4.3 %collective-permute-start.22 = (bf16[16,3584]{1,0:T(8,128)(2,1)S(1)}, bf16[16,3584]{1,0:T(8,128)(2,1)S(1)}, u32[]{:S(2)}, u32[]{:S(2)}) collective-permute-start(bf16[16,3584]{1,0:T(8,128)(2,1)S(1)} %get-tuple-element.123), channel_id=1, source_target_pairs={{0,5},{1,7},{2,4},{3,6},{4,2},{5,0},{6,3},{7,1},{8,14},{9,12},{10,... | collective-permute-start | bytes 344072 | tf_op jit(solution)/shard_map/ppermute | solution.py:40
  51.5 6.6 %collective-permute-start.17 = (bf16[32,3584]{1,0:T(8,128)(2,1)S(1)}, bf16[32,3584]{1,0:T(8,128)(2,1)S(1)}, u32[]{:S(2)}, u32[]{:S(2)}) collective-permute-start(bf16[32,3584]{1,0:T(8,128)(2,1)S(1)} %pad_maximum_fusion.5), channel_id=1, source_target_pairs={{0,6},{1,4},{2,7},{3,5},{4,1},{5,3},{6,0},{7,2},{8,13},{9,15},{10,... | collective-permute-start | bytes 688136 | tf_op jit(solution)/shard_map/ppermute | solution.py:40
  54.0 6.5 %collective-permute-start.23 = (bf16[32,3584]{1,0:T(8,128)(2,1)S(1)}, bf16[32,3584]{1,0:T(8,128)(2,1)S(1)}, u32[]{:S(2)}, u32[]{:S(2)}) collective-permute-start(bf16[32,3584]{1,0:T(8,128)(2,1)S(1)} %pad_maximum_fusion.6), channel_id=1, source_target_pairs={{0,6},{1,4},{2,7},{3,5},{4,1},{5,3},{6,0},{7,2},{8,13},{9,15},{10,... | collective-permute-start | bytes 688136 | tf_op jit(solution)/shard_map/ppermute | solution.py:40
  63.8 4.8 %collective-permute-start.27 = (bf16[128,3584]{1,0:T(8,128)(2,1)S(1)}, bf16[128,3584]{1,0:T(8,128)(2,1)S(1)}, u32[]{:S(2)}, u32[]{:S(2)}) collective-permute-start(bf16[128,3584]{1,0:T(8,128)(2,1)S(1)} %pad_maximum_fusion), channel_id=1, source_target_pairs={{0,4},{1,5},{2,6},{3,7},{4,0},{5,1},{6,2},{7,3},{8,12},{9,13},{10,... | collective-permute-start | bytes 2752520 | tf_op jit(solution)/shard_map/ppermute | solution.py:36
  64.0 4.6 %collective-permute-start.29 = (bf16[128,168]{1,0:T(8,128)(2,1)S(1)}, bf16[128,168]{1,0:T(8,128)(2,1)S(1)}, u32[]{:S(2)}, u32[]{:S(2)}) collective-permute-start(bf16[128,168]{1,0:T(8,128)(2,1)S(1)} %pad_maximum_fusion.8), channel_id=1, source_target_pairs={{0,4},{1,5},{2,6},{3,7},{4,0},{5,1},{6,2},{7,3},{8,12},{9,13},{10,... | collective-permute-start | bytes 129032 | tf_op jit(solution)/shard_map/ppermute | solution.py:36
  66.1 5.7 %collective-permute-start.30 = (bf16[128,3584]{1,0:T(8,128)(2,1)S(1)}, bf16[128,3584]{1,0:T(8,128)(2,1)S(1)}, u32[]{:S(2)}, u32[]{:S(2)}) collective-permute-start(bf16[128,3584]{1,0:T(8,128)(2,1)S(1)} %pad_maximum_fusion.1), channel_id=1, source_target_pairs={{0,4},{1,5},{2,6},{3,7},{4,0},{5,1},{6,2},{7,3},{8,12},{9,13},{10,... | collective-permute-start | bytes 2752520 | tf_op jit(solution)/shard_map/ppermute | solution.py:36
  (12 other events, 50.1 us)

commit v5 on v4

--- a/solution.py
+++ b/solution.py
@@ -66,7 +66,8 @@
     width = encoder.shape[1]
     half, block = inputs.shape[0] // 2, 2 * inputs.shape[1]
     part = half // CHUNKS
-    row_steps, chip_steps = grid.orders(grid.row_bits), grid.orders(grid.chip_bits)
+    row_steps, chip_steps = grid.orders(grid.row_bits)[::-1], grid.orders(grid.chip_bits)
+    chip_steps = [chip_steps[::-1] if k % 2 == 0 else chip_steps for k in range(CHUNKS)]
 
     theirs = grid.swap_core(inputs).astype(f32) - grid.swap_core(center_bias)
     mine = inputs.astype(f32) - center_bias
@@ -78,7 +79,7 @@
     shifted = jnp.where(stream == 0, shifted[:half], shifted[half:])
 
     held = {0: shifted.astype(bf16)}
-    for mask in range(1, grid.chips)[::-1]:
+    for mask in [grid.chips - 1, *range(1, grid.chips - 1)]:
         held[mask] = grid.from_chip(held[0], mask)
     held = [held[mask] for mask in range(grid.chips)]
     encoder, decoder, latent_bias = (after(w, held[-1]) for w in (encoder, decoder, latent_bias))
@@ -88,7 +89,7 @@
     blocks = jnp.concatenate(held, axis=1)
 
     encoders = [encoder, grid.swap_core(encoder)]
-    decoders = [decoder, grid.swap_core(decoder)]
+    decoders = [decoder, grid.swap_core(after(decoder, held[1]))]
     biases = [latent_bias, grid.swap_core(latent_bias)]
 
     def gather_rows(v):
@@ -107,6 +108,7 @@
         latents.append([(jax.nn.softplus(v) / 4.0).astype(bf16) for v in scaled])
         return sum(jnp.dot(l, d, preferred_element_type=f32) for l, d in zip(latents[-1], decoders))
 
+    centered[0] = (centered[0][0], after(centered[0][1], centered[-1][0]))
     for near, far in centered:
         if sends:
             far = after(far, sends[-1])
@@ -123,8 +125,6 @@
     for i in range(len(row_steps))[::-1]:
         received = [grid.step(v, row_steps[i]) for v in sends]
         for k in range(CHUNKS):
-            if k > 0:
-                received[k] = after(received[k], sends[k - 1])
             v = keeps[k] + received[k].astype(f32)
             n = v.shape[0] // 2
             if i > 0:
@@ -132,11 +132,9 @@
             else:
                 keeps[k] = v - placed(parts[k])
                 sends[k] = keeps[k].astype(bf16)
-    for pair in chip_steps:
-        received = [grid.step(v, pair) for v in sends]
+    for pairs in zip(*chip_steps):
+        received = [grid.step(v, pair) for v, pair in zip(sends, pairs)]
         for k in range(CHUNKS):
-            if k > 0:
-                received[k] = after(received[k], sends[k - 1])
             keeps[k] = keeps[k] + received[k].astype(f32)
             sends[k] = keeps[k].astype(bf16)
     columns = sum(jnp.sum(v, axis=0, keepdims=True) for v in keeps)

time: 79 us -> 78.1 us (0.989)
  waiting for transfers between devices: 25.3 us -> 24.1 us
    ppermute x22, waiting for transfers between devices: 22.8 us -> 21.7 us  [step(): return lax.ppermute(v, AXES, list(enumerate(target)))]
  transfers between devices with their start and end apart: 33 -> 33, of which waited for: 20 -> 18; matrix products, arithmetic and copies ran while one was open for 20% -> 20% of each run, Pallas kernels for 0% -> 0%
where the time goes in v5:
time: 78.1 us; the launch traced here: 77.9 us
  starting transfers between devices  33.9 us (43%)
  waiting for transfers between devices  24.1 us (31%)
  matrix products  14.1 us (18%)
  other arithmetic  3.97 us (5%)
  between operations  1.35 us (2%)
    ppermute x22, starting transfers between devices, step(): return lax.ppermute(v, AXES, list(enumerate(target)))  25.8 us
    ppermute x22, waiting for transfers between devices, step(): return lax.ppermute(v, AXES, list(enumerate(target)))  21.7 us
    dot_general x16, matrix products, dot_rows(): lax.dot_general(v, w, (((1,), (1,)), ((), ())), preferred_element_type=f32)  7.71 us
    ppermute x1, starting transfers between devices, from_chip(): return lax.ppermute(v, AXES, [(i, i ^ across) for i in range(self.size)])  4.84 us
    ppermute x10, starting transfers between devices, swap_core(): return lax.ppermute(v, AXES, [(i, i ^ self.core) for i in range(self.size)])  3.27 us
    dot_general x2, matrix products, over_rows(): lax.dot_general(u, v, (((0,), (0,)), ((), ())), preferred_element_type=f32)  3.05 us
    dot_general x8, matrix products, forward(): jnp.dot(l, d, preferred_element_type=f32)  2.78 us
    ppermute x1, waiting for transfers between devices, from_chip(): return lax.ppermute(v, AXES, [(i, i ^ across) for i in range(self.size)])  2.12 us
  transfers between devices with their start and end apart: 33, of which 18 were waited for; matrix products, arithmetic and copies ran while one was open for 20% of the time, Pallas kernels for 0%

profile of v5, /device:TPU:0, one launch (start us, length us, event | category | flops | bytes accessed | tf_op | source)
XLA Modules:
  0.0 77.9 jit_solution(3199471741662402360)
XLA Ops:
  2.7 4.8 %collective-permute-start.2 = (bf16[32,896]{1,0:T(8,128)(2,1)S(1)}, bf16[32,896]{1,0:T(8,128)(2,1)S(1)}, u32[]{:S(2)}, u32[]{:S(2)}) collective-permute-start(bf16[32,896]{1,0:T(8,128)(2,1)S(1)} %get-tuple-element.116), channel_id=1, source_target_pairs={{0,24},{1,25},{2,26},{3,27},{4,28},{5,29},{6,30},{7,31},{8,16},{9,... | collective-permute-start | bytes 172040 | tf_op jit(solution)/shard_map/ppermute | solution.py:46
  8.0 2.1 %collective-permute-done.2 = bf16[32,896]{1,0:T(8,128)(2,1)S(1)} collective-permute-done((bf16[32,896]{1,0:T(8,128)(2,1)S(1)}, bf16[32,896]{1,0:T(8,128)(2,1)S(1)}, u32[]{:S(2)}, u32[]{:S(2)}) %collective-permute-start.2) | collective-permute-done | bytes 57376 | tf_op jit(solution)/shard_map/ppermute | solution.py:46
  10.4 2.6 %collective-permute-done.3 = bf16[32,896]{1,0:T(8,128)(2,1)S(1)} collective-permute-done((bf16[32,896]{1,0:T(8,128)(2,1)S(1)}, bf16[32,896]{1,0:T(8,128)(2,1)S(1)}, u32[]{:S(2)}, u32[]{:S(2)}) %collective-permute-start.3) | collective-permute-done | bytes 57376 | tf_op jit(solution)/shard_map/ppermute | solution.py:40
  15.4 2.0 %collective-permute-done.5 = bf16[16,3584]{1,0:T(8,128)(2,1)S(1)} collective-permute-done((bf16[16,3584]{1,0:T(8,128)(2,1)S(1)}, bf16[16,3584]{1,0:T(8,128)(2,1)S(1)}, u32[]{:S(2)}, u32[]{:S(2)}) %collective-permute-start.5) | collective-permute-done | bytes 114720 | tf_op jit(solution)/shard_map/ppermute | solution.py:40
  17.4 1.5 %collective-permute-start.6 = (bf16[32,3584]{1,0:T(8,128)(2,1)S(1)}, bf16[32,3584]{1,0:T(8,128)(2,1)S(1)}, u32[]{:S(2)}, u32[]{:S(2)}) collective-permute-start(bf16[32,3584]{1,0:T(8,128)(2,1)S(1)} %pad_maximum_fusion.3), channel_id=1, source_target_pairs={{0,5},{1,7},{2,4},{3,6},{4,2},{5,0},{6,3},{7,1},{8,14},{9,12},{10,... | collective-permute-start | bytes 688136 | tf_op jit(solution)/shard_map/ppermute | solution.py:40
  18.9 1.3 %collective-permute-start.8 = (bf16[32,3584]{1,0:T(8,128)(2,1)S(1)}, bf16[32,3584]{1,0:T(8,128)(2,1)S(1)}, u32[]{:S(2)}, u32[]{:S(2)}) collective-permute-start(bf16[32,3584]{1,0:T(8,128)(2,1)S(1)} %pad_maximum_fusion.4), channel_id=1, source_target_pairs={{0,5},{1,7},{2,4},{3,6},{4,2},{5,0},{6,3},{7,1},{8,14},{9,12},{10,... | collective-permute-start | bytes 688136 | tf_op jit(solution)/shard_map/ppermute | solution.py:40
  21.2 1.7 %collective-permute-done.6 = bf16[32,3584]{1,0:T(8,128)(2,1)S(1)} collective-permute-done((bf16[32,3584]{1,0:T(8,128)(2,1)S(1)}, bf16[32,3584]{1,0:T(8,128)(2,1)S(1)}, u32[]{:S(2)}, u32[]{:S(2)}) %collective-permute-start.6) | collective-permute-done | bytes 229408 | tf_op jit(solution)/shard_map/ppermute | solution.py:40
  24.6 1.8 %collective-permute-start.12 = (bf16[32,3584]{1,0:T(8,128)(2,1)S(1)}, bf16[32,3584]{1,0:T(8,128)(2,1)S(1)}, u32[]{:S(2)}, u32[]{:S(2)}) collective-permute-start(bf16[32,3584]{1,0:T(8,128)(2,1)S(1)} %fusion.3), channel_id=1, source_target_pairs={{0,5},{1,7},{2,4},{3,6},{4,2},{5,0},{6,3},{7,1},{8,14},{9,12},{10,... | collective-permute-start | bytes 688136 | tf_op jit(solution)/shard_map/ppermute | solution.py:40
  30.9 1.7 %collective-permute-start.13 = (bf16[16,3584]{1,0:T(8,128)(2,1)S(1)}, bf16[16,3584]{1,0:T(8,128)(2,1)S(1)}, u32[]{:S(2)}, u32[]{:S(2)}) collective-permute-start(bf16[16,3584]{1,0:T(8,128)(2,1)S(1)} %slice.143), channel_id=1, source_target_pairs={{0,6},{1,4},{2,7},{3,5},{4,1},{5,3},{6,0},{7,2},{8,13},{9,15},{10,... | collective-permute-start | bytes 344072 | tf_op jit(solution)/shard_map/ppermute | solution.py:40
  35.3 1.4 %collective-permute-start.14 = (bf16[16,3584]{1,0:T(8,128)(2,1)S(1)}, bf16[16,3584]{1,0:T(8,128)(2,1)S(1)}, u32[]{:S(2)}, u32[]{:S(2)}) collective-permute-start(bf16[16,3584]{1,0:T(8,128)(2,1)S(1)} %get-tuple-element.114), channel_id=1, source_target_pairs={{0,20},{1,13},{2,14},{3,23},{4,8},{5,17},{6,18},{7,11},{8,4},{9,29... | collective-permute-start | bytes 344072 | tf_op jit(solution)/shard_map/ppermute | solution.py:40
  36.6 1.6 %collective-permute-done.19 = bf16[16,3584]{1,0:T(8,128)(2,1)S(1)} collective-permute-done((bf16[16,3584]{1,0:T(8,128)(2,1)S(1)}, bf16[16,3584]{1,0:T(8,128)(2,1)S(1)}, u32[]{:S(2)}, u32[]{:S(2)}) %collective-permute-start.19) | collective-permute-done | bytes 114720 | tf_op jit(solution)/shard_map/ppermute | solution.py:40
  39.1 2.7 %collective-permute-done.14 = bf16[16,3584]{1,0:T(8,128)(2,1)S(1)} collective-permute-done((bf16[16,3584]{1,0:T(8,128)(2,1)S(1)}, bf16[16,3584]{1,0:T(8,128)(2,1)S(1)}, u32[]{:S(2)}, u32[]{:S(2)}) %collective-permute-start.14) | collective-permute-done | bytes 114720 | tf_op jit(solution)/shard_map/ppermute | solution.py:40
  43.0 1.9 %collective-permute-start.21 = (bf16[16,3584]{1,0:T(8,128)(2,1)S(1)}, bf16[16,3584]{1,0:T(8,128)(2,1)S(1)}, u32[]{:S(2)}, u32[]{:S(2)}) collective-permute-start(bf16[16,3584]{1,0:T(8,128)(2,1)S(1)} %fusion.33), channel_id=1, source_target_pairs={{0,20},{1,13},{2,14},{3,23},{4,8},{5,17},{6,18},{7,11},{8,4},{9,29... | collective-permute-start | bytes 344072 | tf_op jit(solution)/shard_map/ppermute | solution.py:40
  44.9 1.5 %collective-permute-done.15 = bf16[16,3584]{1,0:T(8,128)(2,1)S(1)} collective-permute-done((bf16[16,3584]{1,0:T(8,128)(2,1)S(1)}, bf16[16,3584]{1,0:T(8,128)(2,1)S(1)}, u32[]{:S(2)}, u32[]{:S(2)}) %collective-permute-start.15) | collective-permute-done | bytes 114720 | tf_op jit(solution)/shard_map/ppermute | solution.py:40
  46.5 1.9 %collective-permute-start.16 = (bf16[16,3584]{1,0:T(8,128)(2,1)S(1)}, bf16[16,3584]{1,0:T(8,128)(2,1)S(1)}, u32[]{:S(2)}, u32[]{:S(2)}) collective-permute-start(bf16[16,3584]{1,0:T(8,128)(2,1)S(1)} %get-tuple-element.121), channel_id=1, source_target_pairs={{0,6},{1,4},{2,7},{3,5},{4,1},{5,3},{6,0},{7,2},{8,13},{9,15},{10,... | collective-permute-start | bytes 344072 | tf_op jit(solution)/shard_map/ppermute | solution.py:40
  48.8 3.0 %collective-permute-start.22 = (bf16[16,3584]{1,0:T(8,128)(2,1)S(1)}, bf16[16,3584]{1,0:T(8,128)(2,1)S(1)}, u32[]{:S(2)}, u32[]{:S(2)}) collective-permute-start(bf16[16,3584]{1,0:T(8,128)(2,1)S(1)} %get-tuple-element.119), channel_id=1, source_target_pairs={{0,6},{1,4},{2,7},{3,5},{4,1},{5,3},{6,0},{7,2},{8,13},{9,15},{10,... | collective-permute-start | bytes 344072 | tf_op jit(solution)/shard_map/ppermute | solution.py:40
  52.5 1.8 %collective-permute-done.22 = bf16[16,3584]{1,0:T(8,128)(2,1)S(1)} collective-permute-done((bf16[16,3584]{1,0:T(8,128)(2,1)S(1)}, bf16[16,3584]{1,0:T(8,128)(2,1)S(1)}, u32[]{:S(2)}, u32[]{:S(2)}) %collective-permute-start.22) | collective-permute-done | bytes 114720 | tf_op jit(solution)/shard_map/ppermute | solution.py:40
  54.3 1.5 %collective-permute-start.23 = (bf16[32,3584]{1,0:T(8,128)(2,1)S(1)}, bf16[32,3584]{1,0:T(8,128)(2,1)S(1)}, u32[]{:S(2)}, u32[]{:S(2)}) collective-permute-start(bf16[32,3584]{1,0:T(8,128)(2,1)S(1)} %pad_maximum_fusion.6), channel_id=1, source_target_pairs={{0,5},{1,7},{2,4},{3,6},{4,2},{5,0},{6,3},{7,1},{8,14},{9,12},{10,... | collective-permute-start | bytes 688136 | tf_op jit(solution)/shard_map/ppermute | solution.py:40
  58.7 1.3 %collective-permute-done.23 = bf16[32,3584]{1,0:T(8,128)(2,1)S(1)} collective-permute-done((bf16[32,3584]{1,0:T(8,128)(2,1)S(1)}, bf16[32,3584]{1,0:T(8,128)(2,1)S(1)}, u32[]{:S(2)}, u32[]{:S(2)}) %collective-permute-start.23) | collective-permute-done | bytes 229408 | tf_op jit(solution)/shard_map/ppermute | solution.py:40
  65.0 2.5 %collective-permute-done.25 = f32[1,1792]{1,0:T(1,128)S(1)} collective-permute-done((f32[1,1792]{1,0:T(1,128)S(1)}, f32[1,1792]{1,0:T(1,128)S(1)}, u32[]{:S(2)}, u32[]{:S(2)}) %collective-permute-start.25) | collective-permute-done | bytes 7200 | tf_op jit(solution)/shard_map/ppermute | solution.py:40
  68.7 1.5 %fusion = bf16[168,3584]{1,0:T(8,128)(2,1)} fusion(bf16[256,168]{1,0:T(8,128)(2,1)S(1)} %constant_dynamic-update-slice_fusion, bf16[256,3584]{1,0:T(8,128)(2,1)S(1)} %constant_dynamic-update-slice_fusion.5, bf16[168,3584]{1,0:T(8,128)(2,1)S(1)} %copy-done, f32[168]{0:T(256)S(1)} %rsqrt_multiply_fusion), kind=kOutput, calls=%fused_computation.1 | convolution fusion | flops 310689792 | bytes 4330144 | tf_op jit(solution)/shard_map/dot_general | solution.py:58
  71.1 1.3 %collective-permute-start.31 = (f32[2,224]{1,0:T(2,128)S(1)}, f32[2,224]{1,0:T(2,128)S(1)}, u32[]{:S(2)}, u32[]{:S(2)}) collective-permute-start(f32[2,224]{1,0:T(2,128)S(1)} %broadcast_select_fusion.12), channel_id=1, source_target_pairs={{0,6},{1,7},{2,4},{3,5},{4,2},{5,3},{6,0},{7,1},{8,14},{9,15},{10,... | collective-permute-start | bytes 5384 | tf_op jit(solution)/shard_map/ppermute | solution.py:40
  72.3 1.5 %convolution_convert_fusion = bf16[168,3584]{1,0:T(8,128)(2,1)} fusion(bf16[256,168]{1,0:T(8,128)(2,1)S(1)} %constant_dynamic-update-slice_fusion.10, bf16[256,3584]{1,0:T(8,128)(2,1)S(1)} %constant_dynamic-update-slice_fusion.15), kind=kOutput, calls=%fused_computation.2 | convolution fusion | flops 308883456 | bytes 3125248 | tf_op jit(solution)/shard_map/dot_general | solution.py:58
  74.2 1.8 %collective-permute-start.32 = (f32[2,112]{1,0:T(2,128)S(1)}, f32[2,112]{1,0:T(2,128)S(1)}, u32[]{:S(2)}, u32[]{:S(2)}) collective-permute-start(f32[2,112]{1,0:T(2,128)S(1)} %broadcast_select_fusion.13), channel_id=1, source_target_pairs={{0,5},{1,4},{2,7},{3,6},{4,1},{5,0},{6,3},{7,2},{8,13},{9,12},{10,... | collective-permute-start | bytes 2696 | tf_op jit(solution)/shard_map/ppermute | solution.py:40
  (150 shorter events, 30.0 us)
Async XLA Ops:
  2.7 7.4 %collective-permute-start.2 = (bf16[32,896]{1,0:T(8,128)(2,1)S(1)}, bf16[32,896]{1,0:T(8,128)(2,1)S(1)}, u32[]{:S(2)}, u32[]{:S(2)}) collective-permute-start(bf16[32,896]{1,0:T(8,128)(2,1)S(1)} %get-tuple-element.116), channel_id=1, source_target_pairs={{0,24},{1,25},{2,26},{3,27},{4,28},{5,29},{6,30},{7,31},{8,16},{9,... | collective-permute-start | bytes 172040 | tf_op jit(solution)/shard_map/ppermute | solution.py:46
  7.6 5.4 %collective-permute-start.3 = (bf16[32,896]{1,0:T(8,128)(2,1)S(1)}, bf16[32,896]{1,0:T(8,128)(2,1)S(1)}, u32[]{:S(2)}, u32[]{:S(2)}) collective-permute-start(bf16[32,896]{1,0:T(8,128)(2,1)S(1)} %get-tuple-element.116), channel_id=1, source_target_pairs={{0,20},{1,21},{2,22},{3,23},{4,16},{5,17},{6,18},{7,19},{8,28},{9,... | collective-permute-start | bytes 172040 | tf_op jit(solution)/shard_map/ppermute | solution.py:40
  7.6 5.4 %collective-permute-start.4 = (bf16[32,896]{1,0:T(8,128)(2,1)S(1)}, bf16[32,896]{1,0:T(8,128)(2,1)S(1)}, u32[]{:S(2)}, u32[]{:S(2)}) collective-permute-start(bf16[32,896]{1,0:T(8,128)(2,1)S(1)} %get-tuple-element.116), channel_id=1, source_target_pairs={{0,12},{1,13},{2,14},{3,15},{4,8},{5,9},{6,10},{7,11},{8,4},{9,5},... | collective-permute-start | bytes 172040 | tf_op jit(solution)/shard_map/ppermute | solution.py:40
  10.1 13.3 %collective-permute-start.9 = (bf16[168,3584]{1,0:T(8,128)(2,1)}, bf16[168,3584]{1,0:T(8,128)(2,1)S(1)}, u32[]{:S(2)}, u32[]{:S(2)}) collective-permute-start(bf16[168,3584]{1,0:T(8,128)(2,1)} %param.6), channel_id=1, source_target_pairs={{0,4},{1,5},{2,6},{3,7},{4,0},{5,1},{6,2},{7,3},{8,12},{9,13},{10,... | collective-permute-start | bytes 3612680 | tf_op jit(solution)/shard_map/ppermute | solution.py:36
  13.1 4.3 %collective-permute-start.5 = (bf16[16,3584]{1,0:T(8,128)(2,1)S(1)}, bf16[16,3584]{1,0:T(8,128)(2,1)S(1)}, u32[]{:S(2)}, u32[]{:S(2)}) collective-permute-start(bf16[16,3584]{1,0:T(8,128)(2,1)S(1)} %get-tuple-element.123), channel_id=1, source_target_pairs={{0,6},{1,4},{2,7},{3,5},{4,1},{5,3},{6,0},{7,2},{8,13},{9,15},{10,... | collective-permute-start | bytes 344072 | tf_op jit(solution)/shard_map/ppermute | solution.py:40
  14.3 4.6 %collective-permute-start.7 = (bf16[16,3584]{1,0:T(8,128)(2,1)S(1)}, bf16[16,3584]{1,0:T(8,128)(2,1)S(1)}, u32[]{:S(2)}, u32[]{:S(2)}) collective-permute-start(bf16[16,3584]{1,0:T(8,128)(2,1)S(1)} %get-tuple-element.122), channel_id=1, source_target_pairs={{0,6},{1,4},{2,7},{3,5},{4,1},{5,3},{6,0},{7,2},{8,13},{9,15},{10,... | collective-permute-start | bytes 344072 | tf_op jit(solution)/shard_map/ppermute | solution.py:40
  14.9 8.5 %collective-permute-start.10 = (f32[168]{0:T(256)S(1)}, f32[168]{0:T(256)S(1)}, u32[]{:S(2)}, u32[]{:S(2)}) collective-permute-start(f32[168]{0:T(256)S(1)} %copy-done.2), channel_id=1, source_target_pairs={{0,4},{1,5},{2,6},{3,7},{4,0},{5,1},{6,2},{7,3},{8,12},{9,13},{10,... | collective-permute-start | bytes 2024 | tf_op jit(solution)/shard_map/ppermute | solution.py:36
  14.9 9.0 %collective-permute-start.11 = (bf16[168,3584]{1,0:T(8,128)(2,1)S(1)}, bf16[168,3584]{1,0:T(8,128)(2,1)S(1)}, u32[]{:S(2)}, u32[]{:S(2)}) collective-permute-start(bf16[168,3584]{1,0:T(8,128)(2,1)S(1)} %copy-done), channel_id=1, source_target_pairs={{0,4},{1,5},{2,6},{3,7},{4,0},{5,1},{6,2},{7,3},{8,12},{9,13},{10,... | collective-permute-start | bytes 3612680 | tf_op jit(solution)/shard_map/ppermute | solution.py:36
  17.4 5.5 %collective-permute-start.6 = (bf16[32,3584]{1,0:T(8,128)(2,1)S(1)}, bf16[32,3584]{1,0:T(8,128)(2,1)S(1)}, u32[]{:S(2)}, u32[]{:S(2)}) collective-permute-start(bf16[32,3584]{1,0:T(8,128)(2,1)S(1)} %pad_maximum_fusion.3), channel_id=1, source_target_pairs={{0,5},{1,7},{2,4},{3,6},{4,2},{5,0},{6,3},{7,1},{8,14},{9,12},{10,... | collective-permute-start | bytes 688136 | tf_op jit(solution)/shard_map/ppermute | solution.py:40
  18.9 7.5 %collective-permute-start.8 = (bf16[32,3584]{1,0:T(8,128)(2,1)S(1)}, bf16[32,3584]{1,0:T(8,128)(2,1)S(1)}, u32[]{:S(2)}, u32[]{:S(2)}) collective-permute-start(bf16[32,3584]{1,0:T(8,128)(2,1)S(1)} %pad_maximum_fusion.4), channel_id=1, source_target_pairs={{0,5},{1,7},{2,4},{3,6},{4,2},{5,0},{6,3},{7,1},{8,14},{9,12},{10,... | collective-permute-start | bytes 688136 | tf_op jit(solution)/shard_map/ppermute | solution.py:40
  24.6 6.0 %collective-permute-start.12 = (bf16[32,3584]{1,0:T(8,128)(2,1)S(1)}, bf16[32,3584]{1,0:T(8,128)(2,1)S(1)}, u32[]{:S(2)}, u32[]{:S(2)}) collective-permute-start(bf16[32,3584]{1,0:T(8,128)(2,1)S(1)} %fusion.3), channel_id=1, source_target_pairs={{0,5},{1,7},{2,4},{3,6},{4,2},{5,0},{6,3},{7,1},{8,14},{9,12},{10,... | collective-permute-start | bytes 688136 | tf_op jit(solution)/shard_map/ppermute | solution.py:40
  28.1 5.5 %collective-permute-start.18 = (bf16[32,3584]{1,0:T(8,128)(2,1)S(1)}, bf16[32,3584]{1,0:T(8,128)(2,1)S(1)}, u32[]{:S(2)}, u32[]{:S(2)}) collective-permute-start(bf16[32,3584]{1,0:T(8,128)(2,1)S(1)} %fusion.4), channel_id=1, source_target_pairs={{0,5},{1,7},{2,4},{3,6},{4,2},{5,0},{6,3},{7,1},{8,14},{9,12},{10,... | collective-permute-start | bytes 688136 | tf_op jit(solution)/shard_map/ppermute | solution.py:40
  30.9 4.3 %collective-permute-start.13 = (bf16[16,3584]{1,0:T(8,128)(2,1)S(1)}, bf16[16,3584]{1,0:T(8,128)(2,1)S(1)}, u32[]{:S(2)}, u32[]{:S(2)}) collective-permute-start(bf16[16,3584]{1,0:T(8,128)(2,1)S(1)} %slice.143), channel_id=1, source_target_pairs={{0,6},{1,4},{2,7},{3,5},{4,1},{5,3},{6,0},{7,2},{8,13},{9,15},{10,... | collective-permute-start | bytes 344072 | tf_op jit(solution)/shard_map/ppermute | solution.py:40
  35.3 6.6 %collective-permute-start.14 = (bf16[16,3584]{1,0:T(8,128)(2,1)S(1)}, bf16[16,3584]{1,0:T(8,128)(2,1)S(1)}, u32[]{:S(2)}, u32[]{:S(2)}) collective-permute-start(bf16[16,3584]{1,0:T(8,128)(2,1)S(1)} %get-tuple-element.114), channel_id=1, source_target_pairs={{0,20},{1,13},{2,14},{3,23},{4,8},{5,17},{6,18},{7,11},{8,4},{9,29... | collective-permute-start | bytes 344072 | tf_op jit(solution)/shard_map/ppermute | solution.py:40
  38.3 4.7 %collective-permute-start.20 = (bf16[16,3584]{1,0:T(8,128)(2,1)S(1)}, bf16[16,3584]{1,0:T(8,128)(2,1)S(1)}, u32[]{:S(2)}, u32[]{:S(2)}) collective-permute-start(bf16[16,3584]{1,0:T(8,128)(2,1)S(1)} %get-tuple-element.112), channel_id=1, source_target_pairs={{0,12},{1,21},{2,22},{3,15},{4,16},{5,9},{6,10},{7,19},{8,28},{9,5... | collective-permute-start | bytes 344072 | tf_op jit(solution)/shard_map/ppermute | solution.py:40
  41.9 4.6 %collective-permute-start.15 = (bf16[16,3584]{1,0:T(8,128)(2,1)S(1)}, bf16[16,3584]{1,0:T(8,128)(2,1)S(1)}, u32[]{:S(2)}, u32[]{:S(2)}) collective-permute-start(bf16[16,3584]{1,0:T(8,128)(2,1)S(1)} %fusion.32), channel_id=1, source_target_pairs={{0,12},{1,21},{2,22},{3,15},{4,16},{5,9},{6,10},{7,19},{8,28},{9,5... | collective-permute-start | bytes 344072 | tf_op jit(solution)/shard_map/ppermute | solution.py:40
  43.0 5.8 %collective-permute-start.21 = (bf16[16,3584]{1,0:T(8,128)(2,1)S(1)}, bf16[16,3584]{1,0:T(8,128)(2,1)S(1)}, u32[]{:S(2)}, u32[]{:S(2)}) collective-permute-start(bf16[16,3584]{1,0:T(8,128)(2,1)S(1)} %fusion.33), channel_id=1, source_target_pairs={{0,20},{1,13},{2,14},{3,23},{4,8},{5,17},{6,18},{7,11},{8,4},{9,29... | collective-permute-start | bytes 344072 | tf_op jit(solution)/shard_map/ppermute | solution.py:40
  46.5 5.3 %collective-permute-start.16 = (bf16[16,3584]{1,0:T(8,128)(2,1)S(1)}, bf16[16,3584]{1,0:T(8,128)(2,1)S(1)}, u32[]{:S(2)}, u32[]{:S(2)}) collective-permute-start(bf16[16,3584]{1,0:T(8,128)(2,1)S(1)} %get-tuple-element.121), channel_id=1, source_target_pairs={{0,6},{1,4},{2,7},{3,5},{4,1},{5,3},{6,0},{7,2},{8,13},{9,15},{10,... | collective-permute-start | bytes 344072 | tf_op jit(solution)/shard_map/ppermute | solution.py:40
  48.8 5.4 %collective-permute-start.22 = (bf16[16,3584]{1,0:T(8,128)(2,1)S(1)}, bf16[16,3584]{1,0:T(8,128)(2,1)S(1)}, u32[]{:S(2)}, u32[]{:S(2)}) collective-permute-start(bf16[16,3584]{1,0:T(8,128)(2,1)S(1)} %get-tuple-element.119), channel_id=1, source_target_pairs={{0,6},{1,4},{2,7},{3,5},{4,1},{5,3},{6,0},{7,2},{8,13},{9,15},{10,... | collective-permute-start | bytes 344072 | tf_op jit(solution)/shard_map/ppermute | solution.py:40
  51.9 5.9 %collective-permute-start.17 = (bf16[32,3584]{1,0:T(8,128)(2,1)S(1)}, bf16[32,3584]{1,0:T(8,128)(2,1)S(1)}, u32[]{:S(2)}, u32[]{:S(2)}) collective-permute-start(bf16[32,3584]{1,0:T(8,128)(2,1)S(1)} %pad_maximum_fusion.5), channel_id=1, source_target_pairs={{0,5},{1,7},{2,4},{3,6},{4,2},{5,0},{6,3},{7,1},{8,14},{9,12},{10,... | collective-permute-start | bytes 688136 | tf_op jit(solution)/shard_map/ppermute | solution.py:40
  54.3 5.7 %collective-permute-start.23 = (bf16[32,3584]{1,0:T(8,128)(2,1)S(1)}, bf16[32,3584]{1,0:T(8,128)(2,1)S(1)}, u32[]{:S(2)}, u32[]{:S(2)}) collective-permute-start(bf16[32,3584]{1,0:T(8,128)(2,1)S(1)} %pad_maximum_fusion.6), channel_id=1, source_target_pairs={{0,5},{1,7},{2,4},{3,6},{4,2},{5,0},{6,3},{7,1},{8,14},{9,12},{10,... | collective-permute-start | bytes 688136 | tf_op jit(solution)/shard_map/ppermute | solution.py:40
  62.8 4.8 %collective-permute-start.27 = (bf16[128,3584]{1,0:T(8,128)(2,1)S(1)}, bf16[128,3584]{1,0:T(8,128)(2,1)S(1)}, u32[]{:S(2)}, u32[]{:S(2)}) collective-permute-start(bf16[128,3584]{1,0:T(8,128)(2,1)S(1)} %pad_maximum_fusion), channel_id=1, source_target_pairs={{0,4},{1,5},{2,6},{3,7},{4,0},{5,1},{6,2},{7,3},{8,12},{9,13},{10,... | collective-permute-start | bytes 2752520 | tf_op jit(solution)/shard_map/ppermute | solution.py:36
  62.9 4.6 %collective-permute-start.29 = (bf16[128,168]{1,0:T(8,128)(2,1)S(1)}, bf16[128,168]{1,0:T(8,128)(2,1)S(1)}, u32[]{:S(2)}, u32[]{:S(2)}) collective-permute-start(bf16[128,168]{1,0:T(8,128)(2,1)S(1)} %pad_maximum_fusion.8), channel_id=1, source_target_pairs={{0,4},{1,5},{2,6},{3,7},{4,0},{5,1},{6,2},{7,3},{8,12},{9,13},{10,... | collective-permute-start | bytes 129032 | tf_op jit(solution)/shard_map/ppermute | solution.py:36
  64.6 6.2 %collective-permute-start.30 = (bf16[128,3584]{1,0:T(8,128)(2,1)S(1)}, bf16[128,3584]{1,0:T(8,128)(2,1)S(1)}, u32[]{:S(2)}, u32[]{:S(2)}) collective-permute-start(bf16[128,3584]{1,0:T(8,128)(2,1)S(1)} %pad_maximum_fusion.1), channel_id=1, source_target_pairs={{0,4},{1,5},{2,6},{3,7},{4,0},{5,1},{6,2},{7,3},{8,12},{9,13},{10,... | collective-permute-start | bytes 2752520 | tf_op jit(solution)/shard_map/ppermute | solution.py:36
  (12 other events, 52.0 us)

commit v6 on v5

--- a/solution.py
+++ b/solution.py
@@ -141,6 +141,7 @@
     errors = [e for halves in [gather_rows(v) for v in sends] for e in halves]
     centered = [c for halves in centered for c in halves]
 
+    errors[0] = after(errors[0], sends[-1])
     pres = []
     for err, sig in zip(errors, sigs):
         grads = [dot_rows(err, d) + sparsity_weight * n for d, n in zip(decoders, norms)]

time: 78.1 us -> 78.2 us (level)
  no operation moved by 1% of the time
where the time goes in v6:
time: 78.2 us; the launch traced here: 78 us
  starting transfers between devices  33.8 us (43%)
  waiting for transfers between devices  24.3 us (31%)
  matrix products  14.1 us (18%)
  other arithmetic  4 us (5%)
  between operations  1.34 us (2%)
    ppermute x22, starting transfers between devices, step(): return lax.ppermute(v, AXES, list(enumerate(target)))  25.7 us
    ppermute x22, waiting for transfers between devices, step(): return lax.ppermute(v, AXES, list(enumerate(target)))  21.9 us
    dot_general x16, matrix products, dot_rows(): lax.dot_general(v, w, (((1,), (1,)), ((), ())), preferred_element_type=f32)  7.71 us
    ppermute x1, starting transfers between devices, from_chip(): return lax.ppermute(v, AXES, [(i, i ^ across) for i in range(self.size)])  4.84 us
    ppermute x10, starting transfers between devices, swap_core(): return lax.ppermute(v, AXES, [(i, i ^ self.core) for i in range(self.size)])  3.29 us
    dot_general x2, matrix products, over_rows(): lax.dot_general(u, v, (((0,), (0,)), ((), ())), preferred_element_type=f32)  3.05 us
    dot_general x8, matrix products, forward(): jnp.dot(l, d, preferred_element_type=f32)  2.77 us
    ppermute x1, waiting for transfers between devices, from_chip(): return lax.ppermute(v, AXES, [(i, i ^ across) for i in range(self.size)])  2.12 us
  transfers between devices with their start and end apart: 33, of which 18 were waited for; matrix products, arithmetic and copies ran while one was open for 20% of the time, Pallas kernels for 0%

profile of v6, /device:TPU:0, one launch (start us, length us, event | category | flops | bytes accessed | tf_op | source)
XLA Modules:
  0.0 78.0 jit_solution(7513194968076641720)
XLA Ops:
  2.7 4.8 %collective-permute-start.2 = (bf16[32,896]{1,0:T(8,128)(2,1)S(1)}, bf16[32,896]{1,0:T(8,128)(2,1)S(1)}, u32[]{:S(2)}, u32[]{:S(2)}) collective-permute-start(bf16[32,896]{1,0:T(8,128)(2,1)S(1)} %get-tuple-element.118), channel_id=1, source_target_pairs={{0,24},{1,25},{2,26},{3,27},{4,28},{5,29},{6,30},{7,31},{8,16},{9,... | collective-permute-start | bytes 172040 | tf_op jit(solution)/shard_map/ppermute | solution.py:46
  8.0 2.1 %collective-permute-done.2 = bf16[32,896]{1,0:T(8,128)(2,1)S(1)} collective-permute-done((bf16[32,896]{1,0:T(8,128)(2,1)S(1)}, bf16[32,896]{1,0:T(8,128)(2,1)S(1)}, u32[]{:S(2)}, u32[]{:S(2)}) %collective-permute-start.2) | collective-permute-done | bytes 57376 | tf_op jit(solution)/shard_map/ppermute | solution.py:46
  10.4 2.6 %collective-permute-done.3 = bf16[32,896]{1,0:T(8,128)(2,1)S(1)} collective-permute-done((bf16[32,896]{1,0:T(8,128)(2,1)S(1)}, bf16[32,896]{1,0:T(8,128)(2,1)S(1)}, u32[]{:S(2)}, u32[]{:S(2)}) %collective-permute-start.3) | collective-permute-done | bytes 57376 | tf_op jit(solution)/shard_map/ppermute | solution.py:40
  15.4 2.0 %collective-permute-done.5 = bf16[16,3584]{1,0:T(8,128)(2,1)S(1)} collective-permute-done((bf16[16,3584]{1,0:T(8,128)(2,1)S(1)}, bf16[16,3584]{1,0:T(8,128)(2,1)S(1)}, u32[]{:S(2)}, u32[]{:S(2)}) %collective-permute-start.5) | collective-permute-done | bytes 114720 | tf_op jit(solution)/shard_map/ppermute | solution.py:40
  17.4 1.5 %collective-permute-start.6 = (bf16[32,3584]{1,0:T(8,128)(2,1)S(1)}, bf16[32,3584]{1,0:T(8,128)(2,1)S(1)}, u32[]{:S(2)}, u32[]{:S(2)}) collective-permute-start(bf16[32,3584]{1,0:T(8,128)(2,1)S(1)} %pad_maximum_fusion.3), channel_id=1, source_target_pairs={{0,5},{1,7},{2,4},{3,6},{4,2},{5,0},{6,3},{7,1},{8,14},{9,12},{10,... | collective-permute-start | bytes 688136 | tf_op jit(solution)/shard_map/ppermute | solution.py:40
  18.9 1.3 %collective-permute-start.8 = (bf16[32,3584]{1,0:T(8,128)(2,1)S(1)}, bf16[32,3584]{1,0:T(8,128)(2,1)S(1)}, u32[]{:S(2)}, u32[]{:S(2)}) collective-permute-start(bf16[32,3584]{1,0:T(8,128)(2,1)S(1)} %pad_maximum_fusion.4), channel_id=1, source_target_pairs={{0,5},{1,7},{2,4},{3,6},{4,2},{5,0},{6,3},{7,1},{8,14},{9,12},{10,... | collective-permute-start | bytes 688136 | tf_op jit(solution)/shard_map/ppermute | solution.py:40
  21.2 1.7 %collective-permute-done.6 = bf16[32,3584]{1,0:T(8,128)(2,1)S(1)} collective-permute-done((bf16[32,3584]{1,0:T(8,128)(2,1)S(1)}, bf16[32,3584]{1,0:T(8,128)(2,1)S(1)}, u32[]{:S(2)}, u32[]{:S(2)}) %collective-permute-start.6) | collective-permute-done | bytes 229408 | tf_op jit(solution)/shard_map/ppermute | solution.py:40
  24.6 1.8 %collective-permute-start.12 = (bf16[32,3584]{1,0:T(8,128)(2,1)S(1)}, bf16[32,3584]{1,0:T(8,128)(2,1)S(1)}, u32[]{:S(2)}, u32[]{:S(2)}) collective-permute-start(bf16[32,3584]{1,0:T(8,128)(2,1)S(1)} %fusion.3), channel_id=1, source_target_pairs={{0,5},{1,7},{2,4},{3,6},{4,2},{5,0},{6,3},{7,1},{8,14},{9,12},{10,... | collective-permute-start | bytes 688136 | tf_op jit(solution)/shard_map/ppermute | solution.py:40
  30.9 1.7 %collective-permute-start.13 = (bf16[16,3584]{1,0:T(8,128)(2,1)S(1)}, bf16[16,3584]{1,0:T(8,128)(2,1)S(1)}, u32[]{:S(2)}, u32[]{:S(2)}) collective-permute-start(bf16[16,3584]{1,0:T(8,128)(2,1)S(1)} %slice.143), channel_id=1, source_target_pairs={{0,6},{1,4},{2,7},{3,5},{4,1},{5,3},{6,0},{7,2},{8,13},{9,15},{10,... | collective-permute-start | bytes 344072 | tf_op jit(solution)/shard_map/ppermute | solution.py:40
  35.3 1.4 %collective-permute-start.14 = (bf16[16,3584]{1,0:T(8,128)(2,1)S(1)}, bf16[16,3584]{1,0:T(8,128)(2,1)S(1)}, u32[]{:S(2)}, u32[]{:S(2)}) collective-permute-start(bf16[16,3584]{1,0:T(8,128)(2,1)S(1)} %get-tuple-element.116), channel_id=1, source_target_pairs={{0,20},{1,13},{2,14},{3,23},{4,8},{5,17},{6,18},{7,11},{8,4},{9,29... | collective-permute-start | bytes 344072 | tf_op jit(solution)/shard_map/ppermute | solution.py:40
  36.6 1.6 %collective-permute-done.18 = bf16[16,3584]{1,0:T(8,128)(2,1)S(1)} collective-permute-done((bf16[16,3584]{1,0:T(8,128)(2,1)S(1)}, bf16[16,3584]{1,0:T(8,128)(2,1)S(1)}, u32[]{:S(2)}, u32[]{:S(2)}) %collective-permute-start.18) | collective-permute-done | bytes 114720 | tf_op jit(solution)/shard_map/ppermute | solution.py:40
  39.1 2.7 %collective-permute-done.14 = bf16[16,3584]{1,0:T(8,128)(2,1)S(1)} collective-permute-done((bf16[16,3584]{1,0:T(8,128)(2,1)S(1)}, bf16[16,3584]{1,0:T(8,128)(2,1)S(1)}, u32[]{:S(2)}, u32[]{:S(2)}) %collective-permute-start.14) | collective-permute-done | bytes 114720 | tf_op jit(solution)/shard_map/ppermute | solution.py:40
  43.0 1.9 %collective-permute-start.20 = (bf16[16,3584]{1,0:T(8,128)(2,1)S(1)}, bf16[16,3584]{1,0:T(8,128)(2,1)S(1)}, u32[]{:S(2)}, u32[]{:S(2)}) collective-permute-start(bf16[16,3584]{1,0:T(8,128)(2,1)S(1)} %fusion.33), channel_id=1, source_target_pairs={{0,20},{1,13},{2,14},{3,23},{4,8},{5,17},{6,18},{7,11},{8,4},{9,29... | collective-permute-start | bytes 344072 | tf_op jit(solution)/shard_map/ppermute | solution.py:40
  44.9 1.5 %collective-permute-done.15 = bf16[16,3584]{1,0:T(8,128)(2,1)S(1)} collective-permute-done((bf16[16,3584]{1,0:T(8,128)(2,1)S(1)}, bf16[16,3584]{1,0:T(8,128)(2,1)S(1)}, u32[]{:S(2)}, u32[]{:S(2)}) %collective-permute-start.15) | collective-permute-done | bytes 114720 | tf_op jit(solution)/shard_map/ppermute | solution.py:40
  46.5 1.9 %collective-permute-start.16 = (bf16[16,3584]{1,0:T(8,128)(2,1)S(1)}, bf16[16,3584]{1,0:T(8,128)(2,1)S(1)}, u32[]{:S(2)}, u32[]{:S(2)}) collective-permute-start(bf16[16,3584]{1,0:T(8,128)(2,1)S(1)} %get-tuple-element.123), channel_id=1, source_target_pairs={{0,6},{1,4},{2,7},{3,5},{4,1},{5,3},{6,0},{7,2},{8,13},{9,15},{10,... | collective-permute-start | bytes 344072 | tf_op jit(solution)/shard_map/ppermute | solution.py:40
  48.9 3.0 %collective-permute-start.22 = (bf16[16,3584]{1,0:T(8,128)(2,1)S(1)}, bf16[16,3584]{1,0:T(8,128)(2,1)S(1)}, u32[]{:S(2)}, u32[]{:S(2)}) collective-permute-start(bf16[16,3584]{1,0:T(8,128)(2,1)S(1)} %get-tuple-element.121), channel_id=1, source_target_pairs={{0,6},{1,4},{2,7},{3,5},{4,1},{5,3},{6,0},{7,2},{8,13},{9,15},{10,... | collective-permute-start | bytes 344072 | tf_op jit(solution)/shard_map/ppermute | solution.py:40
  52.5 1.8 %collective-permute-done.22 = bf16[16,3584]{1,0:T(8,128)(2,1)S(1)} collective-permute-done((bf16[16,3584]{1,0:T(8,128)(2,1)S(1)}, bf16[16,3584]{1,0:T(8,128)(2,1)S(1)}, u32[]{:S(2)}, u32[]{:S(2)}) %collective-permute-start.22) | collective-permute-done | bytes 114720 | tf_op jit(solution)/shard_map/ppermute | solution.py:40
  54.3 1.5 %collective-permute-start.23 = (bf16[32,3584]{1,0:T(8,128)(2,1)S(1)}, bf16[32,3584]{1,0:T(8,128)(2,1)S(1)}, u32[]{:S(2)}, u32[]{:S(2)}) collective-permute-start(bf16[32,3584]{1,0:T(8,128)(2,1)S(1)} %pad_maximum_fusion.6), channel_id=1, source_target_pairs={{0,5},{1,7},{2,4},{3,6},{4,2},{5,0},{6,3},{7,1},{8,14},{9,12},{10,... | collective-permute-start | bytes 688136 | tf_op jit(solution)/shard_map/ppermute | solution.py:40
  58.7 1.3 %collective-permute-done.23 = bf16[32,3584]{1,0:T(8,128)(2,1)S(1)} collective-permute-done((bf16[32,3584]{1,0:T(8,128)(2,1)S(1)}, bf16[32,3584]{1,0:T(8,128)(2,1)S(1)}, u32[]{:S(2)}, u32[]{:S(2)}) %collective-permute-start.23) | collective-permute-done | bytes 229408 | tf_op jit(solution)/shard_map/ppermute | solution.py:40
  64.9 2.7 %collective-permute-done.25 = f32[1,1792]{1,0:T(1,128)S(1)} collective-permute-done((f32[1,1792]{1,0:T(1,128)S(1)}, f32[1,1792]{1,0:T(1,128)S(1)}, u32[]{:S(2)}, u32[]{:S(2)}) %collective-permute-start.25) | collective-permute-done | bytes 7200 | tf_op jit(solution)/shard_map/ppermute | solution.py:40
  68.7 1.5 %fusion = bf16[168,3584]{1,0:T(8,128)(2,1)} fusion(bf16[256,168]{1,0:T(8,128)(2,1)S(1)} %constant_dynamic-update-slice_fusion, bf16[256,3584]{1,0:T(8,128)(2,1)S(1)} %constant_dynamic-update-slice_fusion.5, bf16[168,3584]{1,0:T(8,128)(2,1)S(1)} %copy-done, f32[168]{0:T(256)S(1)} %rsqrt_multiply_fusion), kind=kOutput, calls=%fused_computation.1 | convolution fusion | flops 310689792 | bytes 4330144 | tf_op jit(solution)/shard_map/dot_general | solution.py:58
  71.1 1.3 %collective-permute-start.31 = (f32[2,224]{1,0:T(2,128)S(1)}, f32[2,224]{1,0:T(2,128)S(1)}, u32[]{:S(2)}, u32[]{:S(2)}) collective-permute-start(f32[2,224]{1,0:T(2,128)S(1)} %broadcast_select_fusion.12), channel_id=1, source_target_pairs={{0,6},{1,7},{2,4},{3,5},{4,2},{5,3},{6,0},{7,1},{8,14},{9,15},{10,... | collective-permute-start | bytes 5384 | tf_op jit(solution)/shard_map/ppermute | solution.py:40
  72.4 1.5 %convolution_convert_fusion = bf16[168,3584]{1,0:T(8,128)(2,1)} fusion(bf16[256,168]{1,0:T(8,128)(2,1)S(1)} %constant_dynamic-update-slice_fusion.10, bf16[256,3584]{1,0:T(8,128)(2,1)S(1)} %constant_dynamic-update-slice_fusion.15), kind=kOutput, calls=%fused_computation.2 | convolution fusion | flops 308883456 | bytes 3125248 | tf_op jit(solution)/shard_map/dot_general | solution.py:58
  74.3 1.8 %collective-permute-start.32 = (f32[2,112]{1,0:T(2,128)S(1)}, f32[2,112]{1,0:T(2,128)S(1)}, u32[]{:S(2)}, u32[]{:S(2)}) collective-permute-start(f32[2,112]{1,0:T(2,128)S(1)} %broadcast_select_fusion.13), channel_id=1, source_target_pairs={{0,5},{1,4},{2,7},{3,6},{4,1},{5,0},{6,3},{7,2},{8,13},{9,12},{10,... | collective-permute-start | bytes 2696 | tf_op jit(solution)/shard_map/ppermute | solution.py:40
  (150 shorter events, 29.8 us)
Async XLA Ops:
  2.7 7.4 %collective-permute-start.2 = (bf16[32,896]{1,0:T(8,128)(2,1)S(1)}, bf16[32,896]{1,0:T(8,128)(2,1)S(1)}, u32[]{:S(2)}, u32[]{:S(2)}) collective-permute-start(bf16[32,896]{1,0:T(8,128)(2,1)S(1)} %get-tuple-element.118), channel_id=1, source_target_pairs={{0,24},{1,25},{2,26},{3,27},{4,28},{5,29},{6,30},{7,31},{8,16},{9,... | collective-permute-start | bytes 172040 | tf_op jit(solution)/shard_map/ppermute | solution.py:46
  7.6 5.4 %collective-permute-start.3 = (bf16[32,896]{1,0:T(8,128)(2,1)S(1)}, bf16[32,896]{1,0:T(8,128)(2,1)S(1)}, u32[]{:S(2)}, u32[]{:S(2)}) collective-permute-start(bf16[32,896]{1,0:T(8,128)(2,1)S(1)} %get-tuple-element.118), channel_id=1, source_target_pairs={{0,20},{1,21},{2,22},{3,23},{4,16},{5,17},{6,18},{7,19},{8,28},{9,... | collective-permute-start | bytes 172040 | tf_op jit(solution)/shard_map/ppermute | solution.py:40
  7.6 5.4 %collective-permute-start.4 = (bf16[32,896]{1,0:T(8,128)(2,1)S(1)}, bf16[32,896]{1,0:T(8,128)(2,1)S(1)}, u32[]{:S(2)}, u32[]{:S(2)}) collective-permute-start(bf16[32,896]{1,0:T(8,128)(2,1)S(1)} %get-tuple-element.118), channel_id=1, source_target_pairs={{0,12},{1,13},{2,14},{3,15},{4,8},{5,9},{6,10},{7,11},{8,4},{9,5},... | collective-permute-start | bytes 172040 | tf_op jit(solution)/shard_map/ppermute | solution.py:40
  10.1 13.3 %collective-permute-start.9 = (bf16[168,3584]{1,0:T(8,128)(2,1)}, bf16[168,3584]{1,0:T(8,128)(2,1)S(1)}, u32[]{:S(2)}, u32[]{:S(2)}) collective-permute-start(bf16[168,3584]{1,0:T(8,128)(2,1)} %param.6), channel_id=1, source_target_pairs={{0,4},{1,5},{2,6},{3,7},{4,0},{5,1},{6,2},{7,3},{8,12},{9,13},{10,... | collective-permute-start | bytes 3612680 | tf_op jit(solution)/shard_map/ppermute | solution.py:36
  13.1 4.3 %collective-permute-start.5 = (bf16[16,3584]{1,0:T(8,128)(2,1)S(1)}, bf16[16,3584]{1,0:T(8,128)(2,1)S(1)}, u32[]{:S(2)}, u32[]{:S(2)}) collective-permute-start(bf16[16,3584]{1,0:T(8,128)(2,1)S(1)} %get-tuple-element.125), channel_id=1, source_target_pairs={{0,6},{1,4},{2,7},{3,5},{4,1},{5,3},{6,0},{7,2},{8,13},{9,15},{10,... | collective-permute-start | bytes 344072 | tf_op jit(solution)/shard_map/ppermute | solution.py:40
  14.3 4.6 %collective-permute-start.7 = (bf16[16,3584]{1,0:T(8,128)(2,1)S(1)}, bf16[16,3584]{1,0:T(8,128)(2,1)S(1)}, u32[]{:S(2)}, u32[]{:S(2)}) collective-permute-start(bf16[16,3584]{1,0:T(8,128)(2,1)S(1)} %get-tuple-element.124), channel_id=1, source_target_pairs={{0,6},{1,4},{2,7},{3,5},{4,1},{5,3},{6,0},{7,2},{8,13},{9,15},{10,... | collective-permute-start | bytes 344072 | tf_op jit(solution)/shard_map/ppermute | solution.py:40
  14.9 8.5 %collective-permute-start.10 = (f32[168]{0:T(256)S(1)}, f32[168]{0:T(256)S(1)}, u32[]{:S(2)}, u32[]{:S(2)}) collective-permute-start(f32[168]{0:T(256)S(1)} %copy-done.2), channel_id=1, source_target_pairs={{0,4},{1,5},{2,6},{3,7},{4,0},{5,1},{6,2},{7,3},{8,12},{9,13},{10,... | collective-permute-start | bytes 2024 | tf_op jit(solution)/shard_map/ppermute | solution.py:36
  14.9 9.0 %collective-permute-start.11 = (bf16[168,3584]{1,0:T(8,128)(2,1)S(1)}, bf16[168,3584]{1,0:T(8,128)(2,1)S(1)}, u32[]{:S(2)}, u32[]{:S(2)}) collective-permute-start(bf16[168,3584]{1,0:T(8,128)(2,1)S(1)} %copy-done), channel_id=1, source_target_pairs={{0,4},{1,5},{2,6},{3,7},{4,0},{5,1},{6,2},{7,3},{8,12},{9,13},{10,... | collective-permute-start | bytes 3612680 | tf_op jit(solution)/shard_map/ppermute | solution.py:36
  17.4 5.5 %collective-permute-start.6 = (bf16[32,3584]{1,0:T(8,128)(2,1)S(1)}, bf16[32,3584]{1,0:T(8,128)(2,1)S(1)}, u32[]{:S(2)}, u32[]{:S(2)}) collective-permute-start(bf16[32,3584]{1,0:T(8,128)(2,1)S(1)} %pad_maximum_fusion.3), channel_id=1, source_target_pairs={{0,5},{1,7},{2,4},{3,6},{4,2},{5,0},{6,3},{7,1},{8,14},{9,12},{10,... | collective-permute-start | bytes 688136 | tf_op jit(solution)/shard_map/ppermute | solution.py:40
  18.9 7.5 %collective-permute-start.8 = (bf16[32,3584]{1,0:T(8,128)(2,1)S(1)}, bf16[32,3584]{1,0:T(8,128)(2,1)S(1)}, u32[]{:S(2)}, u32[]{:S(2)}) collective-permute-start(bf16[32,3584]{1,0:T(8,128)(2,1)S(1)} %pad_maximum_fusion.4), channel_id=1, source_target_pairs={{0,5},{1,7},{2,4},{3,6},{4,2},{5,0},{6,3},{7,1},{8,14},{9,12},{10,... | collective-permute-start | bytes 688136 | tf_op jit(solution)/shard_map/ppermute | solution.py:40
  24.6 5.9 %collective-permute-start.12 = (bf16[32,3584]{1,0:T(8,128)(2,1)S(1)}, bf16[32,3584]{1,0:T(8,128)(2,1)S(1)}, u32[]{:S(2)}, u32[]{:S(2)}) collective-permute-start(bf16[32,3584]{1,0:T(8,128)(2,1)S(1)} %fusion.3), channel_id=1, source_target_pairs={{0,5},{1,7},{2,4},{3,6},{4,2},{5,0},{6,3},{7,1},{8,14},{9,12},{10,... | collective-permute-start | bytes 688136 | tf_op jit(solution)/shard_map/ppermute | solution.py:40
  28.1 5.5 %collective-permute-start.17 = (bf16[32,3584]{1,0:T(8,128)(2,1)S(1)}, bf16[32,3584]{1,0:T(8,128)(2,1)S(1)}, u32[]{:S(2)}, u32[]{:S(2)}) collective-permute-start(bf16[32,3584]{1,0:T(8,128)(2,1)S(1)} %fusion.4), channel_id=1, source_target_pairs={{0,5},{1,7},{2,4},{3,6},{4,2},{5,0},{6,3},{7,1},{8,14},{9,12},{10,... | collective-permute-start | bytes 688136 | tf_op jit(solution)/shard_map/ppermute | solution.py:40
  34.0 4.3 %collective-permute-start.18 = (bf16[16,3584]{1,0:T(8,128)(2,1)S(1)}, bf16[16,3584]{1,0:T(8,128)(2,1)S(1)}, u32[]{:S(2)}, u32[]{:S(2)}) collective-permute-start(bf16[16,3584]{1,0:T(8,128)(2,1)S(1)} %slice.142), channel_id=1, source_target_pairs={{0,6},{1,4},{2,7},{3,5},{4,1},{5,3},{6,0},{7,2},{8,13},{9,15},{10,... | collective-permute-start | bytes 344072 | tf_op jit(solution)/shard_map/ppermute | solution.py:40
  35.3 6.6 %collective-permute-start.14 = (bf16[16,3584]{1,0:T(8,128)(2,1)S(1)}, bf16[16,3584]{1,0:T(8,128)(2,1)S(1)}, u32[]{:S(2)}, u32[]{:S(2)}) collective-permute-start(bf16[16,3584]{1,0:T(8,128)(2,1)S(1)} %get-tuple-element.116), channel_id=1, source_target_pairs={{0,20},{1,13},{2,14},{3,23},{4,8},{5,17},{6,18},{7,11},{8,4},{9,29... | collective-permute-start | bytes 344072 | tf_op jit(solution)/shard_map/ppermute | solution.py:40
  38.3 4.7 %collective-permute-start.19 = (bf16[16,3584]{1,0:T(8,128)(2,1)S(1)}, bf16[16,3584]{1,0:T(8,128)(2,1)S(1)}, u32[]{:S(2)}, u32[]{:S(2)}) collective-permute-start(bf16[16,3584]{1,0:T(8,128)(2,1)S(1)} %get-tuple-element.114), channel_id=1, source_target_pairs={{0,12},{1,21},{2,22},{3,15},{4,16},{5,9},{6,10},{7,19},{8,28},{9,5... | collective-permute-start | bytes 344072 | tf_op jit(solution)/shard_map/ppermute | solution.py:40
  41.8 4.6 %collective-permute-start.15 = (bf16[16,3584]{1,0:T(8,128)(2,1)S(1)}, bf16[16,3584]{1,0:T(8,128)(2,1)S(1)}, u32[]{:S(2)}, u32[]{:S(2)}) collective-permute-start(bf16[16,3584]{1,0:T(8,128)(2,1)S(1)} %fusion.32), channel_id=1, source_target_pairs={{0,12},{1,21},{2,22},{3,15},{4,16},{5,9},{6,10},{7,19},{8,28},{9,5... | collective-permute-start | bytes 344072 | tf_op jit(solution)/shard_map/ppermute | solution.py:40
  43.0 5.8 %collective-permute-start.20 = (bf16[16,3584]{1,0:T(8,128)(2,1)S(1)}, bf16[16,3584]{1,0:T(8,128)(2,1)S(1)}, u32[]{:S(2)}, u32[]{:S(2)}) collective-permute-start(bf16[16,3584]{1,0:T(8,128)(2,1)S(1)} %fusion.33), channel_id=1, source_target_pairs={{0,20},{1,13},{2,14},{3,23},{4,8},{5,17},{6,18},{7,11},{8,4},{9,29... | collective-permute-start | bytes 344072 | tf_op jit(solution)/shard_map/ppermute | solution.py:40
  46.5 5.3 %collective-permute-start.16 = (bf16[16,3584]{1,0:T(8,128)(2,1)S(1)}, bf16[16,3584]{1,0:T(8,128)(2,1)S(1)}, u32[]{:S(2)}, u32[]{:S(2)}) collective-permute-start(bf16[16,3584]{1,0:T(8,128)(2,1)S(1)} %get-tuple-element.123), channel_id=1, source_target_pairs={{0,6},{1,4},{2,7},{3,5},{4,1},{5,3},{6,0},{7,2},{8,13},{9,15},{10,... | collective-permute-start | bytes 344072 | tf_op jit(solution)/shard_map/ppermute | solution.py:40
  48.9 5.4 %collective-permute-start.22 = (bf16[16,3584]{1,0:T(8,128)(2,1)S(1)}, bf16[16,3584]{1,0:T(8,128)(2,1)S(1)}, u32[]{:S(2)}, u32[]{:S(2)}) collective-permute-start(bf16[16,3584]{1,0:T(8,128)(2,1)S(1)} %get-tuple-element.121), channel_id=1, source_target_pairs={{0,6},{1,4},{2,7},{3,5},{4,1},{5,3},{6,0},{7,2},{8,13},{9,15},{10,... | collective-permute-start | bytes 344072 | tf_op jit(solution)/shard_map/ppermute | solution.py:40
  51.9 5.9 %collective-permute-start.21 = (bf16[32,3584]{1,0:T(8,128)(2,1)S(1)}, bf16[32,3584]{1,0:T(8,128)(2,1)S(1)}, u32[]{:S(2)}, u32[]{:S(2)}) collective-permute-start(bf16[32,3584]{1,0:T(8,128)(2,1)S(1)} %pad_maximum_fusion.5), channel_id=1, source_target_pairs={{0,5},{1,7},{2,4},{3,6},{4,2},{5,0},{6,3},{7,1},{8,14},{9,12},{10,... | collective-permute-start | bytes 688136 | tf_op jit(solution)/shard_map/ppermute | solution.py:40
  54.3 5.7 %collective-permute-start.23 = (bf16[32,3584]{1,0:T(8,128)(2,1)S(1)}, bf16[32,3584]{1,0:T(8,128)(2,1)S(1)}, u32[]{:S(2)}, u32[]{:S(2)}) collective-permute-start(bf16[32,3584]{1,0:T(8,128)(2,1)S(1)} %pad_maximum_fusion.6), channel_id=1, source_target_pairs={{0,5},{1,7},{2,4},{3,6},{4,2},{5,0},{6,3},{7,1},{8,14},{9,12},{10,... | collective-permute-start | bytes 688136 | tf_op jit(solution)/shard_map/ppermute | solution.py:40
  62.8 4.8 %collective-permute-start.27 = (bf16[128,3584]{1,0:T(8,128)(2,1)S(1)}, bf16[128,3584]{1,0:T(8,128)(2,1)S(1)}, u32[]{:S(2)}, u32[]{:S(2)}) collective-permute-start(bf16[128,3584]{1,0:T(8,128)(2,1)S(1)} %pad_maximum_fusion), channel_id=1, source_target_pairs={{0,4},{1,5},{2,6},{3,7},{4,0},{5,1},{6,2},{7,3},{8,12},{9,13},{10,... | collective-permute-start | bytes 2752520 | tf_op jit(solution)/shard_map/ppermute | solution.py:36
  63.0 4.6 %collective-permute-start.29 = (bf16[128,168]{1,0:T(8,128)(2,1)S(1)}, bf16[128,168]{1,0:T(8,128)(2,1)S(1)}, u32[]{:S(2)}, u32[]{:S(2)}) collective-permute-start(bf16[128,168]{1,0:T(8,128)(2,1)S(1)} %pad_maximum_fusion.8), channel_id=1, source_target_pairs={{0,4},{1,5},{2,6},{3,7},{4,0},{5,1},{6,2},{7,3},{8,12},{9,13},{10,... | collective-permute-start | bytes 129032 | tf_op jit(solution)/shard_map/ppermute | solution.py:36
  64.6 6.2 %collective-permute-start.30 = (bf16[128,3584]{1,0:T(8,128)(2,1)S(1)}, bf16[128,3584]{1,0:T(8,128)(2,1)S(1)}, u32[]{:S(2)}, u32[]{:S(2)}) collective-permute-start(bf16[128,3584]{1,0:T(8,128)(2,1)S(1)} %pad_maximum_fusion.1), channel_id=1, source_target_pairs={{0,4},{1,5},{2,6},{3,7},{4,0},{5,1},{6,2},{7,3},{8,12},{9,13},{10,... | collective-permute-start | bytes 2752520 | tf_op jit(solution)/shard_map/ppermute | solution.py:36
  (12 other events, 52.3 us)

commit v7 on v5

--- a/solution.py
+++ b/solution.py
@@ -67,7 +67,7 @@
     half, block = inputs.shape[0] // 2, 2 * inputs.shape[1]
     part = half // CHUNKS
     row_steps, chip_steps = grid.orders(grid.row_bits)[::-1], grid.orders(grid.chip_bits)
-    chip_steps = [chip_steps[::-1] if k % 2 == 0 else chip_steps for k in range(CHUNKS)]
+    chip_steps = [chip_steps[::-1]] * CHUNKS
 
     theirs = grid.swap_core(inputs).astype(f32) - grid.swap_core(center_bias)
     mine = inputs.astype(f32) - center_bias
@@ -89,7 +89,7 @@
     blocks = jnp.concatenate(held, axis=1)
 
     encoders = [encoder, grid.swap_core(encoder)]
-    decoders = [decoder, grid.swap_core(after(decoder, held[1]))]
+    decoders = [decoder, grid.swap_core(decoder)]
     biases = [latent_bias, grid.swap_core(latent_bias)]
 
     def gather_rows(v):
@@ -114,7 +114,8 @@
             far = after(far, sends[-1])
         keeps.append(forward(near))
         sends.append(forward(far).astype(bf16))
-    norms = [jnp.sqrt(jnp.sum(jnp.square(d.astype(f32)), axis=1) + 1e-06) for d in decoders]
+    late = [decoders[0], after(decoders[1], keeps[-1])]
+    norms = [jnp.sqrt(jnp.sum(jnp.square(d.astype(f32)), axis=1) + 1e-06) for d in late]
 
     def placed(rows):
         zeros = jnp.zeros((part, block), f32)
@@ -125,6 +126,8 @@
     for i in range(len(row_steps))[::-1]:
         received = [grid.step(v, row_steps[i]) for v in sends]
         for k in range(CHUNKS):
+            if k > 0:
+                received[k] = after(received[k], sends[k - 1])
             v = keeps[k] + received[k].astype(f32)
             n = v.shape[0] // 2
             if i > 0:
@@ -135,6 +138,8 @@
     for pairs in zip(*chip_steps):
         received = [grid.step(v, pair) for v, pair in zip(sends, pairs)]
         for k in range(CHUNKS):
+            if k > 0:
+                received[k] = after(received[k], sends[k - 1])
             keeps[k] = keeps[k] + received[k].astype(f32)
             sends[k] = keeps[k].astype(bf16)
     columns = sum(jnp.sum(v, axis=0, keepdims=True) for v in keeps)

time: 78.1 us -> 78.1 us (level)
  starting transfers between devices: 33.9 us -> 32.4 us
  waiting for transfers between devices: 24.1 us -> 25.6 us
    ppermute x22, waiting for transfers between devices: 21.7 us -> 22.9 us  [step(): return lax.ppermute(v, AXES, list(enumerate(target)))]
    ppermute x22, starting transfers between devices: 25.8 us -> 24.9 us  [step(): return lax.ppermute(v, AXES, list(enumerate(target)))]
where the time goes in v7:
time: 78.1 us; the launch traced here: 77.9 us
  starting transfers between devices  32.4 us (41%)
  waiting for transfers between devices  25.6 us (33%)
  matrix products  14.1 us (18%)
  other arithmetic  4.01 us (5%)
  between operations  1.33 us (2%)
    ppermute x22, starting transfers between devices, step(): return lax.ppermute(v, AXES, list(enumerate(target)))  24.9 us
    ppermute x22, waiting for transfers between devices, step(): return lax.ppermute(v, AXES, list(enumerate(target)))  22.9 us
    dot_general x16, matrix products, dot_rows(): lax.dot_general(v, w, (((1,), (1,)), ((), ())), preferred_element_type=f32)  7.73 us
    ppermute x1, starting transfers between devices, from_chip(): return lax.ppermute(v, AXES, [(i, i ^ across) for i in range(self.size)])  4.84 us
    dot_general x2, matrix products, over_rows(): lax.dot_general(u, v, (((0,), (0,)), ((), ())), preferred_element_type=f32)  3.05 us
    dot_general x8, matrix products, forward(): jnp.dot(l, d, preferred_element_type=f32)  2.76 us
    ppermute x10, starting transfers between devices, swap_core(): return lax.ppermute(v, AXES, [(i, i ^ self.core) for i in range(self.size)])  2.69 us
    ppermute x1, waiting for transfers between devices, from_chip(): return lax.ppermute(v, AXES, [(i, i ^ across) for i in range(self.size)])  2.12 us
  transfers between devices with their start and end apart: 33, of which 18 were waited for; matrix products, arithmetic and copies ran while one was open for 20% of the time, Pallas kernels for 0%

profile of v7, /device:TPU:0, one launch (start us, length us, event | category | flops | bytes accessed | tf_op | source)
XLA Modules:
  0.0 77.9 jit_solution(9434564649854037503)
XLA Ops:
  2.7 4.8 %collective-permute-start.2 = (bf16[32,896]{1,0:T(8,128)(2,1)S(1)}, bf16[32,896]{1,0:T(8,128)(2,1)S(1)}, u32[]{:S(2)}, u32[]{:S(2)}) collective-permute-start(bf16[32,896]{1,0:T(8,128)(2,1)S(1)} %get-tuple-element.124), channel_id=1, source_target_pairs={{0,24},{1,25},{2,26},{3,27},{4,28},{5,29},{6,30},{7,31},{8,16},{9,... | collective-permute-start | bytes 172040 | tf_op jit(solution)/shard_map/ppermute | solution.py:46
  8.0 2.1 %collective-permute-done.2 = bf16[32,896]{1,0:T(8,128)(2,1)S(1)} collective-permute-done((bf16[32,896]{1,0:T(8,128)(2,1)S(1)}, bf16[32,896]{1,0:T(8,128)(2,1)S(1)}, u32[]{:S(2)}, u32[]{:S(2)}) %collective-permute-start.2) | collective-permute-done | bytes 57376 | tf_op jit(solution)/shard_map/ppermute | solution.py:46
  11.0 2.0 %collective-permute-done.3 = bf16[32,896]{1,0:T(8,128)(2,1)S(1)} collective-permute-done((bf16[32,896]{1,0:T(8,128)(2,1)S(1)}, bf16[32,896]{1,0:T(8,128)(2,1)S(1)}, u32[]{:S(2)}, u32[]{:S(2)}) %collective-permute-start.3) | collective-permute-done | bytes 57376 | tf_op jit(solution)/shard_map/ppermute | solution.py:40
  13.1 1.2 %collective-permute-start.5 = (bf16[16,3584]{1,0:T(8,128)(2,1)S(1)}, bf16[16,3584]{1,0:T(8,128)(2,1)S(1)}, u32[]{:S(2)}, u32[]{:S(2)}) collective-permute-start(bf16[16,3584]{1,0:T(8,128)(2,1)S(1)} %get-tuple-element.131), channel_id=1, source_target_pairs={{0,6},{1,4},{2,7},{3,5},{4,1},{5,3},{6,0},{7,2},{8,13},{9,15},{10,... | collective-permute-start | bytes 344072 | tf_op jit(solution)/shard_map/ppermute | solution.py:40
  15.0 2.4 %collective-permute-done.5 = bf16[16,3584]{1,0:T(8,128)(2,1)S(1)} collective-permute-done((bf16[16,3584]{1,0:T(8,128)(2,1)S(1)}, bf16[16,3584]{1,0:T(8,128)(2,1)S(1)}, u32[]{:S(2)}, u32[]{:S(2)}) %collective-permute-start.5) | collective-permute-done | bytes 114720 | tf_op jit(solution)/shard_map/ppermute | solution.py:40
  17.4 1.5 %collective-permute-start.6 = (bf16[32,3584]{1,0:T(8,128)(2,1)S(1)}, bf16[32,3584]{1,0:T(8,128)(2,1)S(1)}, u32[]{:S(2)}, u32[]{:S(2)}) collective-permute-start(bf16[32,3584]{1,0:T(8,128)(2,1)S(1)} %pad_maximum_fusion.3), channel_id=1, source_target_pairs={{0,5},{1,7},{2,4},{3,6},{4,2},{5,0},{6,3},{7,1},{8,14},{9,12},{10,... | collective-permute-start | bytes 688136 | tf_op jit(solution)/shard_map/ppermute | solution.py:40
  18.9 1.3 %collective-permute-start.8 = (bf16[32,3584]{1,0:T(8,128)(2,1)S(1)}, bf16[32,3584]{1,0:T(8,128)(2,1)S(1)}, u32[]{:S(2)}, u32[]{:S(2)}) collective-permute-start(bf16[32,3584]{1,0:T(8,128)(2,1)S(1)} %pad_maximum_fusion.4), channel_id=1, source_target_pairs={{0,5},{1,7},{2,4},{3,6},{4,2},{5,0},{6,3},{7,1},{8,14},{9,12},{10,... | collective-permute-start | bytes 688136 | tf_op jit(solution)/shard_map/ppermute | solution.py:40
  21.2 1.7 %collective-permute-done.6 = bf16[32,3584]{1,0:T(8,128)(2,1)S(1)} collective-permute-done((bf16[32,3584]{1,0:T(8,128)(2,1)S(1)}, bf16[32,3584]{1,0:T(8,128)(2,1)S(1)}, u32[]{:S(2)}, u32[]{:S(2)}) %collective-permute-start.6) | collective-permute-done | bytes 229408 | tf_op jit(solution)/shard_map/ppermute | solution.py:40
  24.6 1.8 %collective-permute-start.12 = (bf16[32,3584]{1,0:T(8,128)(2,1)S(1)}, bf16[32,3584]{1,0:T(8,128)(2,1)S(1)}, u32[]{:S(2)}, u32[]{:S(2)}) collective-permute-start(bf16[32,3584]{1,0:T(8,128)(2,1)S(1)} %fusion.2), channel_id=1, source_target_pairs={{0,5},{1,7},{2,4},{3,6},{4,2},{5,0},{6,3},{7,1},{8,14},{9,12},{10,... | collective-permute-start | bytes 688136 | tf_op jit(solution)/shard_map/ppermute | solution.py:40
  31.3 1.4 %collective-permute-start.13 = (bf16[16,3584]{1,0:T(8,128)(2,1)S(1)}, bf16[16,3584]{1,0:T(8,128)(2,1)S(1)}, u32[]{:S(2)}, u32[]{:S(2)}) collective-permute-start(bf16[16,3584]{1,0:T(8,128)(2,1)S(1)} %slice.143), channel_id=1, source_target_pairs={{0,6},{1,4},{2,7},{3,5},{4,1},{5,3},{6,0},{7,2},{8,13},{9,15},{10,... | collective-permute-start | bytes 344072 | tf_op jit(solution)/shard_map/ppermute | solution.py:40
  35.6 1.2 %collective-permute-start.14 = (bf16[16,3584]{1,0:T(8,128)(2,1)S(1)}, bf16[16,3584]{1,0:T(8,128)(2,1)S(1)}, u32[]{:S(2)}, u32[]{:S(2)}) collective-permute-start(bf16[16,3584]{1,0:T(8,128)(2,1)S(1)} %get-tuple-element.122), channel_id=1, source_target_pairs={{0,20},{1,13},{2,14},{3,23},{4,8},{5,17},{6,18},{7,11},{8,4},{9,29... | collective-permute-start | bytes 344072 | tf_op jit(solution)/shard_map/ppermute | solution.py:40
  36.8 1.1 %collective-permute-done.19 = bf16[16,3584]{1,0:T(8,128)(2,1)S(1)} collective-permute-done((bf16[16,3584]{1,0:T(8,128)(2,1)S(1)}, bf16[16,3584]{1,0:T(8,128)(2,1)S(1)}, u32[]{:S(2)}, u32[]{:S(2)}) %collective-permute-start.19) | collective-permute-done | bytes 114720 | tf_op jit(solution)/shard_map/ppermute | solution.py:40
  39.1 3.1 %collective-permute-done.14 = bf16[16,3584]{1,0:T(8,128)(2,1)S(1)} collective-permute-done((bf16[16,3584]{1,0:T(8,128)(2,1)S(1)}, bf16[16,3584]{1,0:T(8,128)(2,1)S(1)}, u32[]{:S(2)}, u32[]{:S(2)}) %collective-permute-start.14) | collective-permute-done | bytes 114720 | tf_op jit(solution)/shard_map/ppermute | solution.py:40
  42.2 2.3 %collective-permute-done.20 = bf16[16,3584]{1,0:T(8,128)(2,1)S(1)} collective-permute-done((bf16[16,3584]{1,0:T(8,128)(2,1)S(1)}, bf16[16,3584]{1,0:T(8,128)(2,1)S(1)}, u32[]{:S(2)}, u32[]{:S(2)}) %collective-permute-start.20) | collective-permute-done | bytes 114720 | tf_op jit(solution)/shard_map/ppermute | solution.py:40
  45.0 2.6 %collective-permute-done.15 = bf16[16,3584]{1,0:T(8,128)(2,1)S(1)} collective-permute-done((bf16[16,3584]{1,0:T(8,128)(2,1)S(1)}, bf16[16,3584]{1,0:T(8,128)(2,1)S(1)}, u32[]{:S(2)}, u32[]{:S(2)}) %collective-permute-start.15) | collective-permute-done | bytes 114720 | tf_op jit(solution)/shard_map/ppermute | solution.py:40
  47.7 1.8 %collective-permute-start.16 = (bf16[16,3584]{1,0:T(8,128)(2,1)S(1)}, bf16[16,3584]{1,0:T(8,128)(2,1)S(1)}, u32[]{:S(2)}, u32[]{:S(2)}) collective-permute-start(bf16[16,3584]{1,0:T(8,128)(2,1)S(1)} %get-tuple-element.129), channel_id=1, source_target_pairs={{0,6},{1,4},{2,7},{3,5},{4,1},{5,3},{6,0},{7,2},{8,13},{9,15},{10,... | collective-permute-start | bytes 344072 | tf_op jit(solution)/shard_map/ppermute | solution.py:40
  49.6 1.8 %collective-permute-start.22 = (bf16[16,3584]{1,0:T(8,128)(2,1)S(1)}, bf16[16,3584]{1,0:T(8,128)(2,1)S(1)}, u32[]{:S(2)}, u32[]{:S(2)}) collective-permute-start(bf16[16,3584]{1,0:T(8,128)(2,1)S(1)} %get-tuple-element.127), channel_id=1, source_target_pairs={{0,6},{1,4},{2,7},{3,5},{4,1},{5,3},{6,0},{7,2},{8,13},{9,15},{10,... | collective-permute-start | bytes 344072 | tf_op jit(solution)/shard_map/ppermute | solution.py:40
  53.9 1.9 %collective-permute-start.23 = (bf16[32,3584]{1,0:T(8,128)(2,1)S(1)}, bf16[32,3584]{1,0:T(8,128)(2,1)S(1)}, u32[]{:S(2)}, u32[]{:S(2)}) collective-permute-start(bf16[32,3584]{1,0:T(8,128)(2,1)S(1)} %pad_maximum_fusion.6), channel_id=1, source_target_pairs={{0,5},{1,7},{2,4},{3,6},{4,2},{5,0},{6,3},{7,1},{8,14},{9,12},{10,... | collective-permute-start | bytes 688136 | tf_op jit(solution)/shard_map/ppermute | solution.py:40
  58.7 1.3 %collective-permute-done.23 = bf16[32,3584]{1,0:T(8,128)(2,1)S(1)} collective-permute-done((bf16[32,3584]{1,0:T(8,128)(2,1)S(1)}, bf16[32,3584]{1,0:T(8,128)(2,1)S(1)}, u32[]{:S(2)}, u32[]{:S(2)}) %collective-permute-start.23) | collective-permute-done | bytes 229408 | tf_op jit(solution)/shard_map/ppermute | solution.py:40
  63.1 2.3 %collective-permute-start.25 = (f32[1,1792]{1,0:T(1,128)S(1)}, f32[1,1792]{1,0:T(1,128)S(1)}, u32[]{:S(2)}, u32[]{:S(2)}) collective-permute-start(f32[1,1792]{1,0:T(1,128)S(1)} %broadcast_select_fusion.8), channel_id=1, source_target_pairs={{0,20},{1,21},{2,22},{3,23},{4,16},{5,17},{6,18},{7,19},{8,28},{9,... | collective-permute-start | bytes 21512 | tf_op jit(solution)/shard_map/ppermute | solution.py:40
  67.9 1.5 %fusion = bf16[168,3584]{1,0:T(8,128)(2,1)} fusion(bf16[256,168]{1,0:T(8,128)(2,1)S(1)} %constant_dynamic-update-slice_fusion, bf16[256,3584]{1,0:T(8,128)(2,1)S(1)} %constant_dynamic-update-slice_fusion.5, bf16[168,3584]{1,0:T(8,128)(2,1)S(1)} %copy-done, f32[168]{0:T(256)S(1)} %rsqrt_multiply_fusion), kind=kOutput, calls=%fused_computation.1 | convolution fusion | flops 310689792 | bytes 4330144 | tf_op jit(solution)/shard_map/dot_general | solution.py:58
  70.6 2.0 %collective-permute-start.31 = (f32[2,224]{1,0:T(2,128)S(1)}, f32[2,224]{1,0:T(2,128)S(1)}, u32[]{:S(2)}, u32[]{:S(2)}) collective-permute-start(f32[2,224]{1,0:T(2,128)S(1)} %broadcast_select_fusion.12), channel_id=1, source_target_pairs={{0,6},{1,7},{2,4},{3,5},{4,2},{5,3},{6,0},{7,1},{8,14},{9,15},{10,... | collective-permute-start | bytes 5384 | tf_op jit(solution)/shard_map/ppermute | solution.py:40
  72.6 1.5 %convolution_convert_fusion = bf16[168,3584]{1,0:T(8,128)(2,1)} fusion(bf16[256,168]{1,0:T(8,128)(2,1)S(1)} %constant_dynamic-update-slice_fusion.10, bf16[256,3584]{1,0:T(8,128)(2,1)S(1)} %constant_dynamic-update-slice_fusion.15), kind=kOutput, calls=%fused_computation.2 | convolution fusion | flops 308883456 | bytes 3125248 | tf_op jit(solution)/shard_map/dot_general | solution.py:58
  75.9 1.4 %collective-permute-done.32 = f32[2,112]{1,0:T(2,128)S(1)} collective-permute-done((f32[2,112]{1,0:T(2,128)S(1)}, f32[2,112]{1,0:T(2,128)S(1)}, u32[]{:S(2)}, u32[]{:S(2)}) %collective-permute-start.32) | collective-permute-done | bytes 928 | tf_op jit(solution)/shard_map/ppermute | solution.py:40
  (151 shorter events, 30.4 us)
Async XLA Ops:
  2.7 7.4 %collective-permute-start.2 = (bf16[32,896]{1,0:T(8,128)(2,1)S(1)}, bf16[32,896]{1,0:T(8,128)(2,1)S(1)}, u32[]{:S(2)}, u32[]{:S(2)}) collective-permute-start(bf16[32,896]{1,0:T(8,128)(2,1)S(1)} %get-tuple-element.124), channel_id=1, source_target_pairs={{0,24},{1,25},{2,26},{3,27},{4,28},{5,29},{6,30},{7,31},{8,16},{9,... | collective-permute-start | bytes 172040 | tf_op jit(solution)/shard_map/ppermute | solution.py:46
  7.6 5.4 %collective-permute-start.3 = (bf16[32,896]{1,0:T(8,128)(2,1)S(1)}, bf16[32,896]{1,0:T(8,128)(2,1)S(1)}, u32[]{:S(2)}, u32[]{:S(2)}) collective-permute-start(bf16[32,896]{1,0:T(8,128)(2,1)S(1)} %get-tuple-element.124), channel_id=1, source_target_pairs={{0,20},{1,21},{2,22},{3,23},{4,16},{5,17},{6,18},{7,19},{8,28},{9,... | collective-permute-start | bytes 172040 | tf_op jit(solution)/shard_map/ppermute | solution.py:40
  7.6 5.4 %collective-permute-start.4 = (bf16[32,896]{1,0:T(8,128)(2,1)S(1)}, bf16[32,896]{1,0:T(8,128)(2,1)S(1)}, u32[]{:S(2)}, u32[]{:S(2)}) collective-permute-start(bf16[32,896]{1,0:T(8,128)(2,1)S(1)} %get-tuple-element.124), channel_id=1, source_target_pairs={{0,12},{1,13},{2,14},{3,15},{4,8},{5,9},{6,10},{7,11},{8,4},{9,5},... | collective-permute-start | bytes 172040 | tf_op jit(solution)/shard_map/ppermute | solution.py:40
  10.1 13.8 %collective-permute-start.11 = (bf16[168,3584]{1,0:T(8,128)(2,1)S(1)}, bf16[168,3584]{1,0:T(8,128)(2,1)S(1)}, u32[]{:S(2)}, u32[]{:S(2)}) collective-permute-start(bf16[168,3584]{1,0:T(8,128)(2,1)S(1)} %copy-done), channel_id=1, source_target_pairs={{0,4},{1,5},{2,6},{3,7},{4,0},{5,1},{6,2},{7,3},{8,12},{9,13},{10,... | collective-permute-start | bytes 3612680 | tf_op jit(solution)/shard_map/ppermute | solution.py:36
  10.4 13.0 %collective-permute-start.9 = (bf16[168,3584]{1,0:T(8,128)(2,1)S(1)}, bf16[168,3584]{1,0:T(8,128)(2,1)S(1)}, u32[]{:S(2)}, u32[]{:S(2)}) collective-permute-start(bf16[168,3584]{1,0:T(8,128)(2,1)S(1)} %copy-done.1), channel_id=1, source_target_pairs={{0,4},{1,5},{2,6},{3,7},{4,0},{5,1},{6,2},{7,3},{8,12},{9,13},{10,... | collective-permute-start | bytes 3612680 | tf_op jit(solution)/shard_map/ppermute | solution.py:36
  13.1 4.3 %collective-permute-start.5 = (bf16[16,3584]{1,0:T(8,128)(2,1)S(1)}, bf16[16,3584]{1,0:T(8,128)(2,1)S(1)}, u32[]{:S(2)}, u32[]{:S(2)}) collective-permute-start(bf16[16,3584]{1,0:T(8,128)(2,1)S(1)} %get-tuple-element.131), channel_id=1, source_target_pairs={{0,6},{1,4},{2,7},{3,5},{4,1},{5,3},{6,0},{7,2},{8,13},{9,15},{10,... | collective-permute-start | bytes 344072 | tf_op jit(solution)/shard_map/ppermute | solution.py:40
  14.3 4.6 %collective-permute-start.7 = (bf16[16,3584]{1,0:T(8,128)(2,1)S(1)}, bf16[16,3584]{1,0:T(8,128)(2,1)S(1)}, u32[]{:S(2)}, u32[]{:S(2)}) collective-permute-start(bf16[16,3584]{1,0:T(8,128)(2,1)S(1)} %get-tuple-element.130), channel_id=1, source_target_pairs={{0,6},{1,4},{2,7},{3,5},{4,1},{5,3},{6,0},{7,2},{8,13},{9,15},{10,... | collective-permute-start | bytes 344072 | tf_op jit(solution)/shard_map/ppermute | solution.py:40
  14.9 8.5 %collective-permute-start.10 = (f32[168]{0:T(256)S(1)}, f32[168]{0:T(256)S(1)}, u32[]{:S(2)}, u32[]{:S(2)}) collective-permute-start(f32[168]{0:T(256)S(1)} %copy-done.2), channel_id=1, source_target_pairs={{0,4},{1,5},{2,6},{3,7},{4,0},{5,1},{6,2},{7,3},{8,12},{9,13},{10,... | collective-permute-start | bytes 2024 | tf_op jit(solution)/shard_map/ppermute | solution.py:36
  17.4 5.5 %collective-permute-start.6 = (bf16[32,3584]{1,0:T(8,128)(2,1)S(1)}, bf16[32,3584]{1,0:T(8,128)(2,1)S(1)}, u32[]{:S(2)}, u32[]{:S(2)}) collective-permute-start(bf16[32,3584]{1,0:T(8,128)(2,1)S(1)} %pad_maximum_fusion.3), channel_id=1, source_target_pairs={{0,5},{1,7},{2,4},{3,6},{4,2},{5,0},{6,3},{7,1},{8,14},{9,12},{10,... | collective-permute-start | bytes 688136 | tf_op jit(solution)/shard_map/ppermute | solution.py:40
  18.9 7.5 %collective-permute-start.8 = (bf16[32,3584]{1,0:T(8,128)(2,1)S(1)}, bf16[32,3584]{1,0:T(8,128)(2,1)S(1)}, u32[]{:S(2)}, u32[]{:S(2)}) collective-permute-start(bf16[32,3584]{1,0:T(8,128)(2,1)S(1)} %pad_maximum_fusion.4), channel_id=1, source_target_pairs={{0,5},{1,7},{2,4},{3,6},{4,2},{5,0},{6,3},{7,1},{8,14},{9,12},{10,... | collective-permute-start | bytes 688136 | tf_op jit(solution)/shard_map/ppermute | solution.py:40
  24.6 6.3 %collective-permute-start.12 = (bf16[32,3584]{1,0:T(8,128)(2,1)S(1)}, bf16[32,3584]{1,0:T(8,128)(2,1)S(1)}, u32[]{:S(2)}, u32[]{:S(2)}) collective-permute-start(bf16[32,3584]{1,0:T(8,128)(2,1)S(1)} %fusion.2), channel_id=1, source_target_pairs={{0,5},{1,7},{2,4},{3,6},{4,2},{5,0},{6,3},{7,1},{8,14},{9,12},{10,... | collective-permute-start | bytes 688136 | tf_op jit(solution)/shard_map/ppermute | solution.py:40
  28.1 5.5 %collective-permute-start.18 = (bf16[32,3584]{1,0:T(8,128)(2,1)S(1)}, bf16[32,3584]{1,0:T(8,128)(2,1)S(1)}, u32[]{:S(2)}, u32[]{:S(2)}) collective-permute-start(bf16[32,3584]{1,0:T(8,128)(2,1)S(1)} %fusion.3), channel_id=1, source_target_pairs={{0,5},{1,7},{2,4},{3,6},{4,2},{5,0},{6,3},{7,1},{8,14},{9,12},{10,... | collective-permute-start | bytes 688136 | tf_op jit(solution)/shard_map/ppermute | solution.py:40
  31.3 4.3 %collective-permute-start.13 = (bf16[16,3584]{1,0:T(8,128)(2,1)S(1)}, bf16[16,3584]{1,0:T(8,128)(2,1)S(1)}, u32[]{:S(2)}, u32[]{:S(2)}) collective-permute-start(bf16[16,3584]{1,0:T(8,128)(2,1)S(1)} %slice.143), channel_id=1, source_target_pairs={{0,6},{1,4},{2,7},{3,5},{4,1},{5,3},{6,0},{7,2},{8,13},{9,15},{10,... | collective-permute-start | bytes 344072 | tf_op jit(solution)/shard_map/ppermute | solution.py:40
  33.7 4.3 %collective-permute-start.19 = (bf16[16,3584]{1,0:T(8,128)(2,1)S(1)}, bf16[16,3584]{1,0:T(8,128)(2,1)S(1)}, u32[]{:S(2)}, u32[]{:S(2)}) collective-permute-start(bf16[16,3584]{1,0:T(8,128)(2,1)S(1)} %slice.142), channel_id=1, source_target_pairs={{0,6},{1,4},{2,7},{3,5},{4,1},{5,3},{6,0},{7,2},{8,13},{9,15},{10,... | collective-permute-start | bytes 344072 | tf_op jit(solution)/shard_map/ppermute | solution.py:40
  35.6 6.5 %collective-permute-start.14 = (bf16[16,3584]{1,0:T(8,128)(2,1)S(1)}, bf16[16,3584]{1,0:T(8,128)(2,1)S(1)}, u32[]{:S(2)}, u32[]{:S(2)}) collective-permute-start(bf16[16,3584]{1,0:T(8,128)(2,1)S(1)} %get-tuple-element.122), channel_id=1, source_target_pairs={{0,20},{1,13},{2,14},{3,23},{4,8},{5,17},{6,18},{7,11},{8,4},{9,29... | collective-permute-start | bytes 344072 | tf_op jit(solution)/shard_map/ppermute | solution.py:40
  38.0 6.5 %collective-permute-start.20 = (bf16[16,3584]{1,0:T(8,128)(2,1)S(1)}, bf16[16,3584]{1,0:T(8,128)(2,1)S(1)}, u32[]{:S(2)}, u32[]{:S(2)}) collective-permute-start(bf16[16,3584]{1,0:T(8,128)(2,1)S(1)} %get-tuple-element.120), channel_id=1, source_target_pairs={{0,20},{1,13},{2,14},{3,23},{4,8},{5,17},{6,18},{7,11},{8,4},{9,29... | collective-permute-start | bytes 344072 | tf_op jit(solution)/shard_map/ppermute | solution.py:40
  42.2 5.5 %collective-permute-start.15 = (bf16[16,3584]{1,0:T(8,128)(2,1)S(1)}, bf16[16,3584]{1,0:T(8,128)(2,1)S(1)}, u32[]{:S(2)}, u32[]{:S(2)}) collective-permute-start(bf16[16,3584]{1,0:T(8,128)(2,1)S(1)} %fusion.31), channel_id=1, source_target_pairs={{0,12},{1,21},{2,22},{3,15},{4,16},{5,9},{6,10},{7,19},{8,28},{9,5... | collective-permute-start | bytes 344072 | tf_op jit(solution)/shard_map/ppermute | solution.py:40
  44.5 5.0 %collective-permute-start.21 = (bf16[16,3584]{1,0:T(8,128)(2,1)S(1)}, bf16[16,3584]{1,0:T(8,128)(2,1)S(1)}, u32[]{:S(2)}, u32[]{:S(2)}) collective-permute-start(bf16[16,3584]{1,0:T(8,128)(2,1)S(1)} %fusion.32), channel_id=1, source_target_pairs={{0,12},{1,21},{2,22},{3,15},{4,16},{5,9},{6,10},{7,19},{8,28},{9,5... | collective-permute-start | bytes 344072 | tf_op jit(solution)/shard_map/ppermute | solution.py:40
  47.7 4.3 %collective-permute-start.16 = (bf16[16,3584]{1,0:T(8,128)(2,1)S(1)}, bf16[16,3584]{1,0:T(8,128)(2,1)S(1)}, u32[]{:S(2)}, u32[]{:S(2)}) collective-permute-start(bf16[16,3584]{1,0:T(8,128)(2,1)S(1)} %get-tuple-element.129), channel_id=1, source_target_pairs={{0,6},{1,4},{2,7},{3,5},{4,1},{5,3},{6,0},{7,2},{8,13},{9,15},{10,... | collective-permute-start | bytes 344072 | tf_op jit(solution)/shard_map/ppermute | solution.py:40
  52.0 5.7 %collective-permute-start.17 = (bf16[32,3584]{1,0:T(8,128)(2,1)S(1)}, bf16[32,3584]{1,0:T(8,128)(2,1)S(1)}, u32[]{:S(2)}, u32[]{:S(2)}) collective-permute-start(bf16[32,3584]{1,0:T(8,128)(2,1)S(1)} %pad_maximum_fusion.5), channel_id=1, source_target_pairs={{0,5},{1,7},{2,4},{3,6},{4,2},{5,0},{6,3},{7,1},{8,14},{9,12},{10,... | collective-permute-start | bytes 688136 | tf_op jit(solution)/shard_map/ppermute | solution.py:40
  53.9 6.1 %collective-permute-start.23 = (bf16[32,3584]{1,0:T(8,128)(2,1)S(1)}, bf16[32,3584]{1,0:T(8,128)(2,1)S(1)}, u32[]{:S(2)}, u32[]{:S(2)}) collective-permute-start(bf16[32,3584]{1,0:T(8,128)(2,1)S(1)} %pad_maximum_fusion.6), channel_id=1, source_target_pairs={{0,5},{1,7},{2,4},{3,6},{4,2},{5,0},{6,3},{7,1},{8,14},{9,12},{10,... | collective-permute-start | bytes 688136 | tf_op jit(solution)/shard_map/ppermute | solution.py:40
  62.1 5.0 %collective-permute-start.27 = (bf16[128,3584]{1,0:T(8,128)(2,1)S(1)}, bf16[128,3584]{1,0:T(8,128)(2,1)S(1)}, u32[]{:S(2)}, u32[]{:S(2)}) collective-permute-start(bf16[128,3584]{1,0:T(8,128)(2,1)S(1)} %pad_maximum_fusion), channel_id=1, source_target_pairs={{0,4},{1,5},{2,6},{3,7},{4,0},{5,1},{6,2},{7,3},{8,12},{9,13},{10,... | collective-permute-start | bytes 2752520 | tf_op jit(solution)/shard_map/ppermute | solution.py:36
  62.6 4.5 %collective-permute-start.29 = (bf16[128,168]{1,0:T(8,128)(2,1)S(1)}, bf16[128,168]{1,0:T(8,128)(2,1)S(1)}, u32[]{:S(2)}, u32[]{:S(2)}) collective-permute-start(bf16[128,168]{1,0:T(8,128)(2,1)S(1)} %pad_maximum_fusion.8), channel_id=1, source_target_pairs={{0,4},{1,5},{2,6},{3,7},{4,0},{5,1},{6,2},{7,3},{8,12},{9,13},{10,... | collective-permute-start | bytes 129032 | tf_op jit(solution)/shard_map/ppermute | solution.py:36
  65.8 4.6 %collective-permute-start.30 = (bf16[128,3584]{1,0:T(8,128)(2,1)S(1)}, bf16[128,3584]{1,0:T(8,128)(2,1)S(1)}, u32[]{:S(2)}, u32[]{:S(2)}) collective-permute-start(bf16[128,3584]{1,0:T(8,128)(2,1)S(1)} %pad_maximum_fusion.1), channel_id=1, source_target_pairs={{0,4},{1,5},{2,6},{3,7},{4,0},{5,1},{6,2},{7,3},{8,12},{9,13},{10,... | collective-permute-start | bytes 2752520 | tf_op jit(solution)/shard_map/ppermute | solution.py:36
  (12 other events, 48.4 us)

commit v8 on v7

--- a/solution.py
+++ b/solution.py
@@ -176,10 +176,10 @@
     def all_rows(mine, theirs):
         return jnp.concatenate([*mine, grid.swap_core(jnp.concatenate(theirs, axis=0))], axis=0)
 
+    latents = all_rows([l[0] for l in latents], [l[1] for l in latents])
+    errors = all_rows(errors, errors)
+    left, pres, centered = lax.optimization_barrier((left, pres, centered))
     pres = all_rows([p[0] for p in pres], [p[1] for p in pres])
-    errors = all_rows(errors, errors)
-    left, latents, centered = lax.optimization_barrier((left, latents, centered))
-    latents = all_rows([l[0] for l in latents], [l[1] for l in latents])
     centered = all_rows(centered, centered)
 
     for k, b in enumerate((grid.row_bits + grid.chip_bits)[::-1]):

time: 78.1 us -> 78 us (level)
  no operation moved by 1% of the time
where the time goes in v8:
time: 78 us; the launch traced here: 77.9 us
  starting transfers between devices  32.5 us (42%)
  waiting for transfers between devices  25.5 us (33%)
  matrix products  14.1 us (18%)
  other arithmetic  4 us (5%)
  between operations  1.32 us (2%)
    ppermute x22, starting transfers between devices, step(): return lax.ppermute(v, AXES, list(enumerate(target)))  24.9 us
    ppermute x22, waiting for transfers between devices, step(): return lax.ppermute(v, AXES, list(enumerate(target)))  22.9 us
    dot_general x16, matrix products, dot_rows(): lax.dot_general(v, w, (((1,), (1,)), ((), ())), preferred_element_type=f32)  7.73 us
    ppermute x1, starting transfers between devices, from_chip(): return lax.ppermute(v, AXES, [(i, i ^ across) for i in range(self.size)])  4.84 us
    dot_general x2, matrix products, over_rows(): lax.dot_general(u, v, (((0,), (0,)), ((), ())), preferred_element_type=f32)  3.05 us
    dot_general x8, matrix products, forward(): jnp.dot(l, d, preferred_element_type=f32)  2.76 us
    ppermute x10, starting transfers between devices, swap_core(): return lax.ppermute(v, AXES, [(i, i ^ self.core) for i in range(self.size)])  2.69 us
    ppermute x1, waiting for transfers between devices, from_chip(): return lax.ppermute(v, AXES, [(i, i ^ across) for i in range(self.size)])  2.12 us
  transfers between devices with their start and end apart: 33, of which 18 were waited for; matrix products, arithmetic and copies ran while one was open for 20% of the time, Pallas kernels for 0%

profile of v8, /device:TPU:0, one launch (start us, length us, event | category | flops | bytes accessed | tf_op | source)
XLA Modules:
  0.0 77.9 jit_solution(7490195069029052644)
XLA Ops:
  2.7 4.8 %collective-permute-start.2 = (bf16[32,896]{1,0:T(8,128)(2,1)S(1)}, bf16[32,896]{1,0:T(8,128)(2,1)S(1)}, u32[]{:S(2)}, u32[]{:S(2)}) collective-permute-start(bf16[32,896]{1,0:T(8,128)(2,1)S(1)} %get-tuple-element.124), channel_id=1, source_target_pairs={{0,24},{1,25},{2,26},{3,27},{4,28},{5,29},{6,30},{7,31},{8,16},{9,... | collective-permute-start | bytes 172040 | tf_op jit(solution)/shard_map/ppermute | solution.py:46
  8.0 2.1 %collective-permute-done.2 = bf16[32,896]{1,0:T(8,128)(2,1)S(1)} collective-permute-done((bf16[32,896]{1,0:T(8,128)(2,1)S(1)}, bf16[32,896]{1,0:T(8,128)(2,1)S(1)}, u32[]{:S(2)}, u32[]{:S(2)}) %collective-permute-start.2) | collective-permute-done | bytes 57376 | tf_op jit(solution)/shard_map/ppermute | solution.py:46
  11.0 2.0 %collective-permute-done.3 = bf16[32,896]{1,0:T(8,128)(2,1)S(1)} collective-permute-done((bf16[32,896]{1,0:T(8,128)(2,1)S(1)}, bf16[32,896]{1,0:T(8,128)(2,1)S(1)}, u32[]{:S(2)}, u32[]{:S(2)}) %collective-permute-start.3) | collective-permute-done | bytes 57376 | tf_op jit(solution)/shard_map/ppermute | solution.py:40
  13.1 1.2 %collective-permute-start.5 = (bf16[16,3584]{1,0:T(8,128)(2,1)S(1)}, bf16[16,3584]{1,0:T(8,128)(2,1)S(1)}, u32[]{:S(2)}, u32[]{:S(2)}) collective-permute-start(bf16[16,3584]{1,0:T(8,128)(2,1)S(1)} %get-tuple-element.131), channel_id=1, source_target_pairs={{0,6},{1,4},{2,7},{3,5},{4,1},{5,3},{6,0},{7,2},{8,13},{9,15},{10,... | collective-permute-start | bytes 344072 | tf_op jit(solution)/shard_map/ppermute | solution.py:40
  15.0 2.4 %collective-permute-done.5 = bf16[16,3584]{1,0:T(8,128)(2,1)S(1)} collective-permute-done((bf16[16,3584]{1,0:T(8,128)(2,1)S(1)}, bf16[16,3584]{1,0:T(8,128)(2,1)S(1)}, u32[]{:S(2)}, u32[]{:S(2)}) %collective-permute-start.5) | collective-permute-done | bytes 114720 | tf_op jit(solution)/shard_map/ppermute | solution.py:40
  17.4 1.5 %collective-permute-start.6 = (bf16[32,3584]{1,0:T(8,128)(2,1)S(1)}, bf16[32,3584]{1,0:T(8,128)(2,1)S(1)}, u32[]{:S(2)}, u32[]{:S(2)}) collective-permute-start(bf16[32,3584]{1,0:T(8,128)(2,1)S(1)} %pad_maximum_fusion.3), channel_id=1, source_target_pairs={{0,5},{1,7},{2,4},{3,6},{4,2},{5,0},{6,3},{7,1},{8,14},{9,12},{10,... | collective-permute-start | bytes 688136 | tf_op jit(solution)/shard_map/ppermute | solution.py:40
  18.9 1.3 %collective-permute-start.8 = (bf16[32,3584]{1,0:T(8,128)(2,1)S(1)}, bf16[32,3584]{1,0:T(8,128)(2,1)S(1)}, u32[]{:S(2)}, u32[]{:S(2)}) collective-permute-start(bf16[32,3584]{1,0:T(8,128)(2,1)S(1)} %pad_maximum_fusion.4), channel_id=1, source_target_pairs={{0,5},{1,7},{2,4},{3,6},{4,2},{5,0},{6,3},{7,1},{8,14},{9,12},{10,... | collective-permute-start | bytes 688136 | tf_op jit(solution)/shard_map/ppermute | solution.py:40
  21.2 1.7 %collective-permute-done.6 = bf16[32,3584]{1,0:T(8,128)(2,1)S(1)} collective-permute-done((bf16[32,3584]{1,0:T(8,128)(2,1)S(1)}, bf16[32,3584]{1,0:T(8,128)(2,1)S(1)}, u32[]{:S(2)}, u32[]{:S(2)}) %collective-permute-start.6) | collective-permute-done | bytes 229408 | tf_op jit(solution)/shard_map/ppermute | solution.py:40
  24.6 1.8 %collective-permute-start.12 = (bf16[32,3584]{1,0:T(8,128)(2,1)S(1)}, bf16[32,3584]{1,0:T(8,128)(2,1)S(1)}, u32[]{:S(2)}, u32[]{:S(2)}) collective-permute-start(bf16[32,3584]{1,0:T(8,128)(2,1)S(1)} %fusion.2), channel_id=1, source_target_pairs={{0,5},{1,7},{2,4},{3,6},{4,2},{5,0},{6,3},{7,1},{8,14},{9,12},{10,... | collective-permute-start | bytes 688136 | tf_op jit(solution)/shard_map/ppermute | solution.py:40
  31.3 1.4 %collective-permute-start.13 = (bf16[16,3584]{1,0:T(8,128)(2,1)S(1)}, bf16[16,3584]{1,0:T(8,128)(2,1)S(1)}, u32[]{:S(2)}, u32[]{:S(2)}) collective-permute-start(bf16[16,3584]{1,0:T(8,128)(2,1)S(1)} %slice.143), channel_id=1, source_target_pairs={{0,6},{1,4},{2,7},{3,5},{4,1},{5,3},{6,0},{7,2},{8,13},{9,15},{10,... | collective-permute-start | bytes 344072 | tf_op jit(solution)/shard_map/ppermute | solution.py:40
  35.6 1.2 %collective-permute-start.14 = (bf16[16,3584]{1,0:T(8,128)(2,1)S(1)}, bf16[16,3584]{1,0:T(8,128)(2,1)S(1)}, u32[]{:S(2)}, u32[]{:S(2)}) collective-permute-start(bf16[16,3584]{1,0:T(8,128)(2,1)S(1)} %get-tuple-element.122), channel_id=1, source_target_pairs={{0,20},{1,13},{2,14},{3,23},{4,8},{5,17},{6,18},{7,11},{8,4},{9,29... | collective-permute-start | bytes 344072 | tf_op jit(solution)/shard_map/ppermute | solution.py:40
  36.8 1.1 %collective-permute-done.19 = bf16[16,3584]{1,0:T(8,128)(2,1)S(1)} collective-permute-done((bf16[16,3584]{1,0:T(8,128)(2,1)S(1)}, bf16[16,3584]{1,0:T(8,128)(2,1)S(1)}, u32[]{:S(2)}, u32[]{:S(2)}) %collective-permute-start.19) | collective-permute-done | bytes 114720 | tf_op jit(solution)/shard_map/ppermute | solution.py:40
  39.1 3.1 %collective-permute-done.14 = bf16[16,3584]{1,0:T(8,128)(2,1)S(1)} collective-permute-done((bf16[16,3584]{1,0:T(8,128)(2,1)S(1)}, bf16[16,3584]{1,0:T(8,128)(2,1)S(1)}, u32[]{:S(2)}, u32[]{:S(2)}) %collective-permute-start.14) | collective-permute-done | bytes 114720 | tf_op jit(solution)/shard_map/ppermute | solution.py:40
  42.2 2.3 %collective-permute-done.20 = bf16[16,3584]{1,0:T(8,128)(2,1)S(1)} collective-permute-done((bf16[16,3584]{1,0:T(8,128)(2,1)S(1)}, bf16[16,3584]{1,0:T(8,128)(2,1)S(1)}, u32[]{:S(2)}, u32[]{:S(2)}) %collective-permute-start.20) | collective-permute-done | bytes 114720 | tf_op jit(solution)/shard_map/ppermute | solution.py:40
  45.0 2.6 %collective-permute-done.15 = bf16[16,3584]{1,0:T(8,128)(2,1)S(1)} collective-permute-done((bf16[16,3584]{1,0:T(8,128)(2,1)S(1)}, bf16[16,3584]{1,0:T(8,128)(2,1)S(1)}, u32[]{:S(2)}, u32[]{:S(2)}) %collective-permute-start.15) | collective-permute-done | bytes 114720 | tf_op jit(solution)/shard_map/ppermute | solution.py:40
  47.7 1.8 %collective-permute-start.16 = (bf16[16,3584]{1,0:T(8,128)(2,1)S(1)}, bf16[16,3584]{1,0:T(8,128)(2,1)S(1)}, u32[]{:S(2)}, u32[]{:S(2)}) collective-permute-start(bf16[16,3584]{1,0:T(8,128)(2,1)S(1)} %get-tuple-element.129), channel_id=1, source_target_pairs={{0,6},{1,4},{2,7},{3,5},{4,1},{5,3},{6,0},{7,2},{8,13},{9,15},{10,... | collective-permute-start | bytes 344072 | tf_op jit(solution)/shard_map/ppermute | solution.py:40
  49.6 1.8 %collective-permute-start.22 = (bf16[16,3584]{1,0:T(8,128)(2,1)S(1)}, bf16[16,3584]{1,0:T(8,128)(2,1)S(1)}, u32[]{:S(2)}, u32[]{:S(2)}) collective-permute-start(bf16[16,3584]{1,0:T(8,128)(2,1)S(1)} %get-tuple-element.127), channel_id=1, source_target_pairs={{0,6},{1,4},{2,7},{3,5},{4,1},{5,3},{6,0},{7,2},{8,13},{9,15},{10,... | collective-permute-start | bytes 344072 | tf_op jit(solution)/shard_map/ppermute | solution.py:40
  53.9 1.9 %collective-permute-start.23 = (bf16[32,3584]{1,0:T(8,128)(2,1)S(1)}, bf16[32,3584]{1,0:T(8,128)(2,1)S(1)}, u32[]{:S(2)}, u32[]{:S(2)}) collective-permute-start(bf16[32,3584]{1,0:T(8,128)(2,1)S(1)} %pad_maximum_fusion.6), channel_id=1, source_target_pairs={{0,5},{1,7},{2,4},{3,6},{4,2},{5,0},{6,3},{7,1},{8,14},{9,12},{10,... | collective-permute-start | bytes 688136 | tf_op jit(solution)/shard_map/ppermute | solution.py:40
  58.7 1.3 %collective-permute-done.23 = bf16[32,3584]{1,0:T(8,128)(2,1)S(1)} collective-permute-done((bf16[32,3584]{1,0:T(8,128)(2,1)S(1)}, bf16[32,3584]{1,0:T(8,128)(2,1)S(1)}, u32[]{:S(2)}, u32[]{:S(2)}) %collective-permute-start.23) | collective-permute-done | bytes 229408 | tf_op jit(solution)/shard_map/ppermute | solution.py:40
  63.0 2.3 %collective-permute-start.25 = (f32[1,1792]{1,0:T(1,128)S(1)}, f32[1,1792]{1,0:T(1,128)S(1)}, u32[]{:S(2)}, u32[]{:S(2)}) collective-permute-start(f32[1,1792]{1,0:T(1,128)S(1)} %broadcast_select_fusion.8), channel_id=1, source_target_pairs={{0,20},{1,21},{2,22},{3,23},{4,16},{5,17},{6,18},{7,19},{8,28},{9,... | collective-permute-start | bytes 21512 | tf_op jit(solution)/shard_map/ppermute | solution.py:40
  67.9 1.5 %fusion = bf16[168,3584]{1,0:T(8,128)(2,1)} fusion(bf16[256,168]{1,0:T(8,128)(2,1)S(1)} %constant_dynamic-update-slice_fusion, bf16[256,3584]{1,0:T(8,128)(2,1)S(1)} %constant_dynamic-update-slice_fusion.5, bf16[168,3584]{1,0:T(8,128)(2,1)S(1)} %copy-done, f32[168]{0:T(256)S(1)} %rsqrt_multiply_fusion), kind=kOutput, calls=%fused_computation.1 | convolution fusion | flops 310689792 | bytes 4330144 | tf_op jit(solution)/shard_map/dot_general | solution.py:58
  70.6 2.0 %collective-permute-start.31 = (f32[2,224]{1,0:T(2,128)S(1)}, f32[2,224]{1,0:T(2,128)S(1)}, u32[]{:S(2)}, u32[]{:S(2)}) collective-permute-start(f32[2,224]{1,0:T(2,128)S(1)} %broadcast_select_fusion.12), channel_id=1, source_target_pairs={{0,6},{1,7},{2,4},{3,5},{4,2},{5,3},{6,0},{7,1},{8,14},{9,15},{10,... | collective-permute-start | bytes 5384 | tf_op jit(solution)/shard_map/ppermute | solution.py:40
  72.6 1.5 %convolution_convert_fusion = bf16[168,3584]{1,0:T(8,128)(2,1)} fusion(bf16[256,168]{1,0:T(8,128)(2,1)S(1)} %constant_dynamic-update-slice_fusion.10, bf16[256,3584]{1,0:T(8,128)(2,1)S(1)} %constant_dynamic-update-slice_fusion.15), kind=kOutput, calls=%fused_computation.2 | convolution fusion | flops 308883456 | bytes 3125248 | tf_op jit(solution)/shard_map/dot_general | solution.py:58
  75.9 1.4 %collective-permute-done.32 = f32[2,112]{1,0:T(2,128)S(1)} collective-permute-done((f32[2,112]{1,0:T(2,128)S(1)}, f32[2,112]{1,0:T(2,128)S(1)}, u32[]{:S(2)}, u32[]{:S(2)}) %collective-permute-start.32) | collective-permute-done | bytes 928 | tf_op jit(solution)/shard_map/ppermute | solution.py:40
  (151 shorter events, 30.4 us)
Async XLA Ops:
  2.7 7.4 %collective-permute-start.2 = (bf16[32,896]{1,0:T(8,128)(2,1)S(1)}, bf16[32,896]{1,0:T(8,128)(2,1)S(1)}, u32[]{:S(2)}, u32[]{:S(2)}) collective-permute-start(bf16[32,896]{1,0:T(8,128)(2,1)S(1)} %get-tuple-element.124), channel_id=1, source_target_pairs={{0,24},{1,25},{2,26},{3,27},{4,28},{5,29},{6,30},{7,31},{8,16},{9,... | collective-permute-start | bytes 172040 | tf_op jit(solution)/shard_map/ppermute | solution.py:46
  7.6 5.4 %collective-permute-start.3 = (bf16[32,896]{1,0:T(8,128)(2,1)S(1)}, bf16[32,896]{1,0:T(8,128)(2,1)S(1)}, u32[]{:S(2)}, u32[]{:S(2)}) collective-permute-start(bf16[32,896]{1,0:T(8,128)(2,1)S(1)} %get-tuple-element.124), channel_id=1, source_target_pairs={{0,20},{1,21},{2,22},{3,23},{4,16},{5,17},{6,18},{7,19},{8,28},{9,... | collective-permute-start | bytes 172040 | tf_op jit(solution)/shard_map/ppermute | solution.py:40
  7.6 5.4 %collective-permute-start.4 = (bf16[32,896]{1,0:T(8,128)(2,1)S(1)}, bf16[32,896]{1,0:T(8,128)(2,1)S(1)}, u32[]{:S(2)}, u32[]{:S(2)}) collective-permute-start(bf16[32,896]{1,0:T(8,128)(2,1)S(1)} %get-tuple-element.124), channel_id=1, source_target_pairs={{0,12},{1,13},{2,14},{3,15},{4,8},{5,9},{6,10},{7,11},{8,4},{9,5},... | collective-permute-start | bytes 172040 | tf_op jit(solution)/shard_map/ppermute | solution.py:40
  10.1 13.8 %collective-permute-start.11 = (bf16[168,3584]{1,0:T(8,128)(2,1)S(1)}, bf16[168,3584]{1,0:T(8,128)(2,1)S(1)}, u32[]{:S(2)}, u32[]{:S(2)}) collective-permute-start(bf16[168,3584]{1,0:T(8,128)(2,1)S(1)} %copy-done), channel_id=1, source_target_pairs={{0,4},{1,5},{2,6},{3,7},{4,0},{5,1},{6,2},{7,3},{8,12},{9,13},{10,... | collective-permute-start | bytes 3612680 | tf_op jit(solution)/shard_map/ppermute | solution.py:36
  10.4 13.0 %collective-permute-start.9 = (bf16[168,3584]{1,0:T(8,128)(2,1)S(1)}, bf16[168,3584]{1,0:T(8,128)(2,1)S(1)}, u32[]{:S(2)}, u32[]{:S(2)}) collective-permute-start(bf16[168,3584]{1,0:T(8,128)(2,1)S(1)} %copy-done.1), channel_id=1, source_target_pairs={{0,4},{1,5},{2,6},{3,7},{4,0},{5,1},{6,2},{7,3},{8,12},{9,13},{10,... | collective-permute-start | bytes 3612680 | tf_op jit(solution)/shard_map/ppermute | solution.py:36
  13.1 4.3 %collective-permute-start.5 = (bf16[16,3584]{1,0:T(8,128)(2,1)S(1)}, bf16[16,3584]{1,0:T(8,128)(2,1)S(1)}, u32[]{:S(2)}, u32[]{:S(2)}) collective-permute-start(bf16[16,3584]{1,0:T(8,128)(2,1)S(1)} %get-tuple-element.131), channel_id=1, source_target_pairs={{0,6},{1,4},{2,7},{3,5},{4,1},{5,3},{6,0},{7,2},{8,13},{9,15},{10,... | collective-permute-start | bytes 344072 | tf_op jit(solution)/shard_map/ppermute | solution.py:40
  14.3 4.6 %collective-permute-start.7 = (bf16[16,3584]{1,0:T(8,128)(2,1)S(1)}, bf16[16,3584]{1,0:T(8,128)(2,1)S(1)}, u32[]{:S(2)}, u32[]{:S(2)}) collective-permute-start(bf16[16,3584]{1,0:T(8,128)(2,1)S(1)} %get-tuple-element.130), channel_id=1, source_target_pairs={{0,6},{1,4},{2,7},{3,5},{4,1},{5,3},{6,0},{7,2},{8,13},{9,15},{10,... | collective-permute-start | bytes 344072 | tf_op jit(solution)/shard_map/ppermute | solution.py:40
  14.9 8.5 %collective-permute-start.10 = (f32[168]{0:T(256)S(1)}, f32[168]{0:T(256)S(1)}, u32[]{:S(2)}, u32[]{:S(2)}) collective-permute-start(f32[168]{0:T(256)S(1)} %copy-done.2), channel_id=1, source_target_pairs={{0,4},{1,5},{2,6},{3,7},{4,0},{5,1},{6,2},{7,3},{8,12},{9,13},{10,... | collective-permute-start | bytes 2024 | tf_op jit(solution)/shard_map/ppermute | solution.py:36
  17.4 5.5 %collective-permute-start.6 = (bf16[32,3584]{1,0:T(8,128)(2,1)S(1)}, bf16[32,3584]{1,0:T(8,128)(2,1)S(1)}, u32[]{:S(2)}, u32[]{:S(2)}) collective-permute-start(bf16[32,3584]{1,0:T(8,128)(2,1)S(1)} %pad_maximum_fusion.3), channel_id=1, source_target_pairs={{0,5},{1,7},{2,4},{3,6},{4,2},{5,0},{6,3},{7,1},{8,14},{9,12},{10,... | collective-permute-start | bytes 688136 | tf_op jit(solution)/shard_map/ppermute | solution.py:40
  18.9 7.5 %collective-permute-start.8 = (bf16[32,3584]{1,0:T(8,128)(2,1)S(1)}, bf16[32,3584]{1,0:T(8,128)(2,1)S(1)}, u32[]{:S(2)}, u32[]{:S(2)}) collective-permute-start(bf16[32,3584]{1,0:T(8,128)(2,1)S(1)} %pad_maximum_fusion.4), channel_id=1, source_target_pairs={{0,5},{1,7},{2,4},{3,6},{4,2},{5,0},{6,3},{7,1},{8,14},{9,12},{10,... | collective-permute-start | bytes 688136 | tf_op jit(solution)/shard_map/ppermute | solution.py:40
  24.6 6.3 %collective-permute-start.12 = (bf16[32,3584]{1,0:T(8,128)(2,1)S(1)}, bf16[32,3584]{1,0:T(8,128)(2,1)S(1)}, u32[]{:S(2)}, u32[]{:S(2)}) collective-permute-start(bf16[32,3584]{1,0:T(8,128)(2,1)S(1)} %fusion.2), channel_id=1, source_target_pairs={{0,5},{1,7},{2,4},{3,6},{4,2},{5,0},{6,3},{7,1},{8,14},{9,12},{10,... | collective-permute-start | bytes 688136 | tf_op jit(solution)/shard_map/ppermute | solution.py:40
  28.1 5.5 %collective-permute-start.18 = (bf16[32,3584]{1,0:T(8,128)(2,1)S(1)}, bf16[32,3584]{1,0:T(8,128)(2,1)S(1)}, u32[]{:S(2)}, u32[]{:S(2)}) collective-permute-start(bf16[32,3584]{1,0:T(8,128)(2,1)S(1)} %fusion.3), channel_id=1, source_target_pairs={{0,5},{1,7},{2,4},{3,6},{4,2},{5,0},{6,3},{7,1},{8,14},{9,12},{10,... | collective-permute-start | bytes 688136 | tf_op jit(solution)/shard_map/ppermute | solution.py:40
  31.3 4.3 %collective-permute-start.13 = (bf16[16,3584]{1,0:T(8,128)(2,1)S(1)}, bf16[16,3584]{1,0:T(8,128)(2,1)S(1)}, u32[]{:S(2)}, u32[]{:S(2)}) collective-permute-start(bf16[16,3584]{1,0:T(8,128)(2,1)S(1)} %slice.143), channel_id=1, source_target_pairs={{0,6},{1,4},{2,7},{3,5},{4,1},{5,3},{6,0},{7,2},{8,13},{9,15},{10,... | collective-permute-start | bytes 344072 | tf_op jit(solution)/shard_map/ppermute | solution.py:40
  33.7 4.3 %collective-permute-start.19 = (bf16[16,3584]{1,0:T(8,128)(2,1)S(1)}, bf16[16,3584]{1,0:T(8,128)(2,1)S(1)}, u32[]{:S(2)}, u32[]{:S(2)}) collective-permute-start(bf16[16,3584]{1,0:T(8,128)(2,1)S(1)} %slice.142), channel_id=1, source_target_pairs={{0,6},{1,4},{2,7},{3,5},{4,1},{5,3},{6,0},{7,2},{8,13},{9,15},{10,... | collective-permute-start | bytes 344072 | tf_op jit(solution)/shard_map/ppermute | solution.py:40
  35.6 6.5 %collective-permute-start.14 = (bf16[16,3584]{1,0:T(8,128)(2,1)S(1)}, bf16[16,3584]{1,0:T(8,128)(2,1)S(1)}, u32[]{:S(2)}, u32[]{:S(2)}) collective-permute-start(bf16[16,3584]{1,0:T(8,128)(2,1)S(1)} %get-tuple-element.122), channel_id=1, source_target_pairs={{0,20},{1,13},{2,14},{3,23},{4,8},{5,17},{6,18},{7,11},{8,4},{9,29... | collective-permute-start | bytes 344072 | tf_op jit(solution)/shard_map/ppermute | solution.py:40
  38.0 6.5 %collective-permute-start.20 = (bf16[16,3584]{1,0:T(8,128)(2,1)S(1)}, bf16[16,3584]{1,0:T(8,128)(2,1)S(1)}, u32[]{:S(2)}, u32[]{:S(2)}) collective-permute-start(bf16[16,3584]{1,0:T(8,128)(2,1)S(1)} %get-tuple-element.120), channel_id=1, source_target_pairs={{0,20},{1,13},{2,14},{3,23},{4,8},{5,17},{6,18},{7,11},{8,4},{9,29... | collective-permute-start | bytes 344072 | tf_op jit(solution)/shard_map/ppermute | solution.py:40
  42.2 5.5 %collective-permute-start.15 = (bf16[16,3584]{1,0:T(8,128)(2,1)S(1)}, bf16[16,3584]{1,0:T(8,128)(2,1)S(1)}, u32[]{:S(2)}, u32[]{:S(2)}) collective-permute-start(bf16[16,3584]{1,0:T(8,128)(2,1)S(1)} %fusion.31), channel_id=1, source_target_pairs={{0,12},{1,21},{2,22},{3,15},{4,16},{5,9},{6,10},{7,19},{8,28},{9,5... | collective-permute-start | bytes 344072 | tf_op jit(solution)/shard_map/ppermute | solution.py:40
  44.5 5.0 %collective-permute-start.21 = (bf16[16,3584]{1,0:T(8,128)(2,1)S(1)}, bf16[16,3584]{1,0:T(8,128)(2,1)S(1)}, u32[]{:S(2)}, u32[]{:S(2)}) collective-permute-start(bf16[16,3584]{1,0:T(8,128)(2,1)S(1)} %fusion.32), channel_id=1, source_target_pairs={{0,12},{1,21},{2,22},{3,15},{4,16},{5,9},{6,10},{7,19},{8,28},{9,5... | collective-permute-start | bytes 344072 | tf_op jit(solution)/shard_map/ppermute | solution.py:40
  47.7 4.3 %collective-permute-start.16 = (bf16[16,3584]{1,0:T(8,128)(2,1)S(1)}, bf16[16,3584]{1,0:T(8,128)(2,1)S(1)}, u32[]{:S(2)}, u32[]{:S(2)}) collective-permute-start(bf16[16,3584]{1,0:T(8,128)(2,1)S(1)} %get-tuple-element.129), channel_id=1, source_target_pairs={{0,6},{1,4},{2,7},{3,5},{4,1},{5,3},{6,0},{7,2},{8,13},{9,15},{10,... | collective-permute-start | bytes 344072 | tf_op jit(solution)/shard_map/ppermute | solution.py:40
  52.0 5.7 %collective-permute-start.17 = (bf16[32,3584]{1,0:T(8,128)(2,1)S(1)}, bf16[32,3584]{1,0:T(8,128)(2,1)S(1)}, u32[]{:S(2)}, u32[]{:S(2)}) collective-permute-start(bf16[32,3584]{1,0:T(8,128)(2,1)S(1)} %pad_maximum_fusion.5), channel_id=1, source_target_pairs={{0,5},{1,7},{2,4},{3,6},{4,2},{5,0},{6,3},{7,1},{8,14},{9,12},{10,... | collective-permute-start | bytes 688136 | tf_op jit(solution)/shard_map/ppermute | solution.py:40
  53.9 6.1 %collective-permute-start.23 = (bf16[32,3584]{1,0:T(8,128)(2,1)S(1)}, bf16[32,3584]{1,0:T(8,128)(2,1)S(1)}, u32[]{:S(2)}, u32[]{:S(2)}) collective-permute-start(bf16[32,3584]{1,0:T(8,128)(2,1)S(1)} %pad_maximum_fusion.6), channel_id=1, source_target_pairs={{0,5},{1,7},{2,4},{3,6},{4,2},{5,0},{6,3},{7,1},{8,14},{9,12},{10,... | collective-permute-start | bytes 688136 | tf_op jit(solution)/shard_map/ppermute | solution.py:40
  61.9 5.1 %collective-permute-start.26 = (bf16[128,168]{1,0:T(8,128)(2,1)S(1)}, bf16[128,168]{1,0:T(8,128)(2,1)S(1)}, u32[]{:S(2)}, u32[]{:S(2)}) collective-permute-start(bf16[128,168]{1,0:T(8,128)(2,1)S(1)} %pad_maximum_fusion.7), channel_id=1, source_target_pairs={{0,4},{1,5},{2,6},{3,7},{4,0},{5,1},{6,2},{7,3},{8,12},{9,13},{10,... | collective-permute-start | bytes 129032 | tf_op jit(solution)/shard_map/ppermute | solution.py:36
  62.6 4.6 %collective-permute-start.27 = (bf16[128,3584]{1,0:T(8,128)(2,1)S(1)}, bf16[128,3584]{1,0:T(8,128)(2,1)S(1)}, u32[]{:S(2)}, u32[]{:S(2)}) collective-permute-start(bf16[128,3584]{1,0:T(8,128)(2,1)S(1)} %pad_maximum_fusion), channel_id=1, source_target_pairs={{0,4},{1,5},{2,6},{3,7},{4,0},{5,1},{6,2},{7,3},{8,12},{9,13},{10,... | collective-permute-start | bytes 2752520 | tf_op jit(solution)/shard_map/ppermute | solution.py:36
  65.7 4.6 %collective-permute-start.30 = (bf16[128,3584]{1,0:T(8,128)(2,1)S(1)}, bf16[128,3584]{1,0:T(8,128)(2,1)S(1)}, u32[]{:S(2)}, u32[]{:S(2)}) collective-permute-start(bf16[128,3584]{1,0:T(8,128)(2,1)S(1)} %pad_maximum_fusion.1), channel_id=1, source_target_pairs={{0,4},{1,5},{2,6},{3,7},{4,0},{5,1},{6,2},{7,3},{8,12},{9,13},{10,... | collective-permute-start | bytes 2752520 | tf_op jit(solution)/shard_map/ppermute | solution.py:36
  (12 other events, 48.4 us)
